TPU v7x, 32 devices: a whole 2x2x4 slice. The times are simulated.
32 devices in a mesh: batch: 16 (over z, y, x), head: 2 (over core).
Axes of the slice: x: 2, y: 2, z: 4, core: 2. Of those that a mesh axis runs over, the one named last changes fastest.
Arguments:
- tokens: bfloat16 [16, 1024, 768], P('batch'), may hold values from -6 to 6
- attn_gain: bfloat16 [768], P('batch'), may hold values from 0.099609375 to 1.8984375
- qkv_weight: bfloat16 [768, 3, 768], P('batch', None, 'head'), may hold values from -0.21875 to 0.21875
- out_weight: bfloat16 [768, 768], P('head', 'batch'), may hold values from -1.75 to 1.75
- ffn_gain: bfloat16 [768], P('batch'), may hold values from 0.099609375 to 1.8984375
- up_weight: bfloat16 [768, 3072], P('batch', 'head'), may hold values from -0.21875 to 0.21875
- down_weight: bfloat16 [3072, 768], P('head', 'batch'), may hold values from -0.109375 to 0.109375
- cotangent: bfloat16 [16, 1024, 768], P('batch'), may hold values from -6 to 6
- segment: int32 [16, 1024], P('batch'), may hold values from 0 to 9, as said below
- cluster: int32 [16, 12, 1024], P('batch', 'head'), may hold values from 0 to 99, as said below
- top_keys: int32 [16, 12, 100, 32], P('batch', 'head'), may hold values from 0 to 1023, as said below
Outputs:
- output: bfloat16 [16, 1024, 768], P('batch', 'head')
- tokens_grad: float32 [16, 1024, 768], P('batch', 'head')
- attn_gain_grad: float32 [768], P('batch')
- qkv_grad: float32 [768, 3, 768], P('batch', None, 'head')
- out_grad: float32 [768, 768], P('head', 'batch')
- ffn_gain_grad: float32 [768], P('batch')
- up_grad: float32 [768, 3072], P('batch', 'head')
- down_grad: float32 [3072, 768], P('head', 'batch')
Inputs may be any that keep to these rules, and one draw needn't show every extreme that they name: Each row holds 10 documents of consecutive positions; segment ids never fall along a row, document d has id d, and each has at least 51 positions. Cluster c of a head in a row holds only positions of document c mod 10 of that row; a cluster may have no positions. `top_keys`: for each row, head and cluster c: 32 distinct positions of document c mod 10 of that row, in increasing order.
All inputs are finite; a program needn't handle non-finite values.
Results may differ from a plain program's by a relative error of at most 0.017.
Values may be sent and summed in bfloat16 or wider, within the bound.
A program may use at most 192 MiB of HBM per device.

v0:
```python
import jax
import jax.numpy as jnp
from jax import lax
from jax.sharding import PartitionSpec as P

DOCS = 10


EPS = 1e-05
HIGH = lax.Precision.HIGHEST
NEGATIVE = -1e30


def norm_forward(values, gain_row):
    row_mean = jnp.mean(values, axis=-1, keepdims=True)
    centred = values - row_mean
    inverse = lax.rsqrt(jnp.mean(centred * centred, axis=-1, keepdims=True) + EPS)
    normed = centred * inverse
    return (normed * gain_row.astype(jnp.float32), normed, inverse)


def norm_backward(grad_out, normed, inverse, gain_row):
    grad_normed = grad_out * gain_row.astype(jnp.float32)
    gain_grad = jnp.sum(grad_out * normed, axis=0)
    inner_term = grad_normed - jnp.mean(grad_normed, axis=-1, keepdims=True)
    inner_term = inner_term - normed * jnp.mean(grad_normed * normed, axis=-1, keepdims=True)
    return (inner_term * inverse, gain_grad)


def cluster_setup(queries, key_rows, value_rows, segments, owners, top_table):
    length, head_size = queries.shape
    clusters, top_count = top_table.shape
    scaling = head_size ** (-0.5)
    labels = jnp.arange(clusters, dtype=jnp.int32)
    members = owners[:, None] == labels[None, :]
    members_low = members.astype(jnp.bfloat16)
    members_full = members.astype(jnp.float32)
    counts = jnp.maximum(jnp.sum(members_full, axis=0), 1.0)
    centre = (
        jnp.einsum("lc,ld->cd", members_low, queries, preferred_element_type=jnp.float32)
        / counts[:, None]
    )
    centre_low = centre.astype(jnp.bfloat16)
    scores = scaling * jnp.einsum(
        "cd,ld->cl", centre_low, key_rows, preferred_element_type=jnp.float32
    )
    allowed = segments[None, :] == (labels % DOCS)[:, None]
    scores = jnp.where(allowed, scores, NEGATIVE)
    places = jnp.arange(length, dtype=jnp.int32)
    picks = top_table.reshape(-1)[:, None] == places[None, :]
    picks_low = picks.astype(jnp.bfloat16)
    picks_full = picks.astype(jnp.float32)
    top_mask = jnp.sum(picks_full.reshape(clusters, top_count, length), axis=1)
    keys_block = (
        jnp.dot(picks_low, key_rows, preferred_element_type=jnp.float32)
        .astype(jnp.bfloat16)
        .reshape(clusters, top_count * head_size)
    )
    values_block = (
        jnp.dot(picks_low, value_rows, preferred_element_type=jnp.float32)
        .astype(jnp.bfloat16)
        .reshape(clusters, top_count * head_size)
    )
    keys_top = (
        jnp.dot(members_low, keys_block, preferred_element_type=jnp.float32)
        .astype(jnp.bfloat16)
        .reshape(length, top_count, head_size)
    )
    values_top = (
        jnp.dot(members_low, values_block, preferred_element_type=jnp.float32)
        .astype(jnp.bfloat16)
        .reshape(length, top_count, head_size)
    )
    near_score = scaling * jnp.einsum(
        "ld,ltd->lt", queries, keys_top, preferred_element_type=jnp.float32
    )
    return (
        members_low,
        members_full,
        counts,
        centre_low,
        scores,
        top_mask,
        picks_full,
        keys_top,
        values_top,
        near_score,
        scaling,
    )


def head_forward(pieces, segments):
    queries, key_rows, value_rows, owners, top_table = pieces
    prepared = cluster_setup(queries, key_rows, value_rows, segments, owners, top_table)
    (
        members_low,
        members_full,
        counts,
        centre_low,
        scores,
        top_mask,
        picks_full,
        keys_top,
        values_top,
        near_score,
        scaling,
    ) = prepared
    top_score = jnp.max(scores, axis=1, keepdims=True)
    exp_scores = jnp.exp(scores - top_score)
    totals = jnp.sum(exp_scores, axis=1, keepdims=True)
    probability = exp_scores / totals
    centre_lse = (top_score + jnp.log(totals))[:, 0]
    top_mass = jnp.sum(probability * top_mask, axis=1)
    rest_weights = probability.astype(jnp.bfloat16) * (1.0 - top_mask).astype(jnp.bfloat16)
    rest_sum = jnp.dot(rest_weights, value_rows, preferred_element_type=jnp.float32)
    near_top = jnp.max(near_score, axis=1, keepdims=True)
    exp_near = jnp.exp(near_score - near_top)
    near_totals = jnp.sum(exp_near, axis=1, keepdims=True)
    weights_low = (exp_near / near_totals).astype(jnp.bfloat16)
    near_lse = (near_top + jnp.log(near_totals))[:, 0]
    exact_sum = jnp.einsum(
        "lt,ltd->ld", weights_low, values_top, preferred_element_type=jnp.float32
    )
    mass_rows = jnp.dot(members_full, top_mass, precision=HIGH)
    rest_rows = jnp.dot(members_full, rest_sum, precision=HIGH)
    return (mass_rows[:, None] * exact_sum + rest_rows, centre_lse, near_lse)


def head_backward(pieces, segments):
    queries, key_rows, value_rows, owners, top_table, grad_low, centre_lse, near_lse = pieces
    prepared = cluster_setup(queries, key_rows, value_rows, segments, owners, top_table)
    (
        members_low,
        members_full,
        counts,
        centre_low,
        scores,
        top_mask,
        picks_full,
        keys_top,
        values_top,
        near_score,
        scaling,
    ) = prepared
    length, head_size = queries.shape
    clusters, top_count = top_table.shape
    probability = jnp.exp(scores - centre_lse[:, None])
    top_mass = jnp.sum(probability * top_mask, axis=1)
    rest_mask = 1.0 - top_mask
    rest_weights = probability.astype(jnp.bfloat16) * rest_mask.astype(jnp.bfloat16)
    weights = jnp.exp(near_score - near_lse[:, None])
    weights_low = weights.astype(jnp.bfloat16)
    exact_sum = jnp.einsum(
        "lt,ltd->ld", weights_low, values_top, preferred_element_type=jnp.float32
    )
    mass_rows = jnp.dot(members_full, top_mass, precision=HIGH)
    grad_full = grad_low.astype(jnp.float32)
    grad_mass = jnp.dot(jnp.sum(grad_full * exact_sum, axis=1), members_full, precision=HIGH)
    grad_rest = jnp.einsum(
        "lc,ld->cd", members_low, grad_low, preferred_element_type=jnp.float32
    ).astype(jnp.bfloat16)
    grad_weights = mass_rows[:, None] * jnp.einsum(
        "ld,ltd->lt", grad_low, values_top, preferred_element_type=jnp.float32
    )
    grad_near = weights * (grad_weights - jnp.sum(weights * grad_weights, axis=1, keepdims=True))
    grad_near_low = grad_near.astype(jnp.bfloat16)
    grad_query = scaling * jnp.einsum(
        "lt,ltd->ld", grad_near_low, keys_top, preferred_element_type=jnp.float32
    )
    key_terms = (members_low[:, :, None] * grad_near_low[:, None, :]).reshape(
        length, clusters * top_count
    )
    value_terms = (members_low[:, :, None] * weights_low[:, None, :]).reshape(
        length, clusters * top_count
    )
    key_block = jnp.einsum("lk,ld->kd", key_terms, queries, preferred_element_type=jnp.float32)
    value_block = jnp.einsum("lk,ld->kd", value_terms, grad_low, preferred_element_type=jnp.float32)
    value_block = (
        value_block.reshape(clusters, top_count, head_size) * top_mass[:, None, None]
    ).reshape(clusters * top_count, head_size)
    grad_key = jnp.dot(picks_full.T, scaling * key_block, precision=HIGH)
    grad_value = jnp.dot(picks_full.T, value_block, precision=HIGH)
    grad_probs = (
        jnp.einsum("cd,ld->cl", grad_rest, value_rows, preferred_element_type=jnp.float32)
        * rest_mask
    )
    grad_probs = grad_probs + grad_mass[:, None] * top_mask
    grad_scores = probability * (
        grad_probs - jnp.sum(probability * grad_probs, axis=1, keepdims=True)
    )
    grad_scores_low = grad_scores.astype(jnp.bfloat16)
    grad_centre = scaling * jnp.einsum(
        "cl,ld->cd", grad_scores_low, key_rows, preferred_element_type=jnp.float32
    )
    grad_key = grad_key + scaling * jnp.einsum(
        "cl,cd->ld", grad_scores_low, centre_low, preferred_element_type=jnp.float32
    )
    grad_value = grad_value + jnp.einsum(
        "cl,cd->ld", rest_weights, grad_rest, preferred_element_type=jnp.float32
    )
    grad_query = grad_query + jnp.dot(members_full, grad_centre / counts[:, None], precision=HIGH)
    return (grad_query, grad_key, grad_value)


def reduce_ffn(gain_part, up_part, down_part):
    return (
        lax.psum_scatter(gain_part, "batch", scatter_dimension=0, tiled=True),
        lax.psum_scatter(up_part, "batch", scatter_dimension=0, tiled=True),
        lax.psum_scatter(down_part, "batch", scatter_dimension=1, tiled=True),
    )


def on_device(
    tokens,
    attn_gain,
    qkv_weight,
    out_weight,
    ffn_gain,
    up_weight,
    down_weight,
    cotangent,
    segment,
    cluster,
    top_keys,
):
    token_rows = tokens[0].astype(jnp.float32)
    segments = segment[0]
    owners = cluster[0]
    top_table = top_keys[0]
    heads_here = owners.shape[0]
    length = token_rows.shape[0]
    share_rows = length // lax.axis_size("head")
    offset = lax.axis_index("head") * share_rows

    def my_share(values):
        return lax.dynamic_slice_in_dim(values, offset, share_rows, 0)

    gathered = (
        lax.all_gather(attn_gain, "batch", axis=0, tiled=True),
        lax.all_gather(qkv_weight, "batch", axis=0, tiled=True),
        lax.all_gather(out_weight, "batch", axis=1, tiled=True),
        lax.all_gather(ffn_gain, "batch", axis=0, tiled=True),
        lax.all_gather(up_weight, "batch", axis=0, tiled=True),
        lax.all_gather(down_weight, "batch", axis=1, tiled=True),
    )
    gain_one, qkv_full, out_full, gain_two, up_full, down_full = gathered
    model_width = qkv_full.shape[0]
    local_width = qkv_full.shape[2]
    head_size = local_width // heads_here
    normed_one, plain_one, inverse_one = norm_forward(token_rows, gain_one)
    normed_low = normed_one.astype(jnp.bfloat16)
    qkv_split = qkv_full.reshape(model_width, 3, heads_here, head_size)
    qkv_all = jnp.einsum(
        "td,dshe->shte", normed_low, qkv_split, preferred_element_type=jnp.float32
    ).astype(jnp.bfloat16)

    def forward_head(pieces):
        return head_forward(pieces, segments)

    attended, centre_lse, near_lse = lax.map(
        forward_head, (qkv_all[0], qkv_all[1], qkv_all[2], owners, top_table)
    )
    attended_low = attended.astype(jnp.bfloat16)
    out_split = out_full.reshape(heads_here, head_size, model_width)
    attn_part = jnp.einsum(
        "hte,hef->tf", attended_low, out_split, preferred_element_type=jnp.float32
    )
    hidden_full = token_rows + lax.psum(attn_part.astype(jnp.bfloat16), "head").astype(jnp.float32)
    normed_full, plain_full, inverse_full = norm_forward(hidden_full, gain_two)
    normed_two_low = normed_full.astype(jnp.bfloat16)
    hidden = my_share(hidden_full)
    up_proj = jnp.dot(normed_two_low, up_full, preferred_element_type=jnp.float32)
    activ_low = jax.nn.gelu(up_proj).astype(jnp.bfloat16)
    ffn_part = jnp.dot(activ_low, down_full, preferred_element_type=jnp.float32)
    ffn_share = my_share(lax.psum(ffn_part.astype(jnp.bfloat16), "head").astype(jnp.float32))
    output = (hidden + ffn_share).astype(jnp.bfloat16)[None]
    grad_low = cotangent[0]
    grad_top = grad_low.astype(jnp.float32)
    down_part = jnp.einsum("tf,td->fd", activ_low, grad_low, preferred_element_type=jnp.float32)
    grad_activ = jnp.einsum("td,fd->tf", grad_low, down_full, preferred_element_type=jnp.float32)
    unused, gelu_pull = jax.vjp(jax.nn.gelu, up_proj)
    grad_up = gelu_pull(grad_activ)[0].astype(jnp.bfloat16)
    up_part = jnp.einsum("td,tf->df", normed_two_low, grad_up, preferred_element_type=jnp.float32)
    norm_two_part = jnp.einsum("tf,df->td", grad_up, up_full, preferred_element_type=jnp.float32)
    grad_norm_full = lax.psum(norm_two_part.astype(jnp.bfloat16), "head").astype(jnp.float32)
    back_full, ffn_gain_part = norm_backward(grad_norm_full, plain_full, inverse_full, gain_two)
    grad_hidden_full = grad_top + back_full
    grad_attn = grad_hidden_full.astype(jnp.bfloat16)
    grad_hidden = my_share(grad_hidden_full)
    ffn_sums = None
    out_part = jnp.einsum(
        "hte,tf->hef", attended_low, grad_attn, preferred_element_type=jnp.float32
    ).reshape(local_width, model_width)
    grad_attended = jnp.einsum(
        "tf,hef->hte", grad_attn, out_split, preferred_element_type=jnp.float32
    ).astype(jnp.bfloat16)

    def backward_head(pieces):
        return head_backward(pieces, segments)

    grad_query, grad_key, grad_value = lax.map(
        backward_head,
        (
            qkv_all[0],
            qkv_all[1],
            qkv_all[2],
            owners,
            top_table,
            grad_attended,
            centre_lse,
            near_lse,
        ),
    )
    grad_qkv = jnp.stack([grad_query, grad_key, grad_value]).astype(jnp.bfloat16)
    qkv_part = jnp.einsum(
        "td,shte->dshe", normed_low, grad_qkv, preferred_element_type=jnp.float32
    ).reshape(model_width, 3, local_width)
    norm_one_part = jnp.einsum(
        "shte,dshe->td", grad_qkv, qkv_split, preferred_element_type=jnp.float32
    )
    grad_norm_one = lax.psum(norm_one_part.astype(jnp.bfloat16), "head").astype(jnp.float32)
    back_one, attn_gain_part = norm_backward(grad_norm_one, plain_one, inverse_one, gain_one)
    tokens_grad = (grad_hidden + my_share(back_one))[None]
    ffn_sums = reduce_ffn(ffn_gain_part, up_part, down_part)
    attn_sums = (
        lax.psum_scatter(attn_gain_part, "batch", scatter_dimension=0, tiled=True),
        lax.psum_scatter(qkv_part, "batch", scatter_dimension=0, tiled=True),
        lax.psum_scatter(out_part, "batch", scatter_dimension=1, tiled=True),
    )
    attn_gain_grad = attn_sums[0]
    ffn_gain_grad = ffn_sums[0]
    return (
        output,
        tokens_grad,
        attn_gain_grad,
        attn_sums[1],
        attn_sums[2],
        ffn_gain_grad,
        ffn_sums[1],
        ffn_sums[2],
    )


def solution(mesh):
    in_specs = (
        P("batch", None, None),
        P("batch"),
        P("batch", None, "head"),
        P("head", "batch"),
        P("batch"),
        P("batch", "head"),
        P("head", "batch"),
        P("batch", None, None),
        P("batch", None),
        P("batch", "head", None),
        P("batch", "head", None, None),
    )
    out_specs = (
        P("batch", "head", None),
        P("batch", "head", None),
        P("batch"),
        P("batch", None, "head"),
        P("head", "batch"),
        P("batch"),
        P("batch", "head"),
        P("head", "batch"),
    )
    return jax.shard_map(
        on_device, mesh=mesh, in_specs=in_specs, out_specs=out_specs, check_vma=False
    )
```

profile of v0, /device:TPU:0, one launch (start us, length us, event | category | flops | bytes accessed | tf_op | source)
XLA Modules:
  0.0 1643.5 jit_solution(15618254184931937524)
XLA Ops:
  11.7 43.6 %all-reduce.5 = (bf16[768]{0:T(1024)(128)(2,1)S(1)}, bf16[768]{0:T(1024)(128)(2,1)S(1)}) all-reduce(bf16[768]{0:T(1024)(128)(2,1)S(1)} %dynamic-update-slice, bf16[768]{0:T(1024)(128)(2,1)S(1)} %dynamic-update-slice.1), channel_id=1, replica_groups=mesh['batch'=16,'head'=2] {'batch'}, use_global_device_ids=true, to_apply=%add | all-reduce | flops 1536 | bytes 6144
  57.9 41.2 %all_gather.20 = bf16[384,768]{0,1:T(8,128)(2,1)S(1)} all-gather(bf16[384,48]{0,1:T(8,128)(2,1)} %param.18), channel_id=1, replica_groups=mesh['batch'=16,'head'=2] {'batch'}, dimensions={1}, use_global_device_ids=true | all-gather | bytes 626688 | tf_op jit(solution)/shard_map/all_gather | solution.py:241
  114.1 308.0 %while.32 = (s32[]{:T(128)}, bf16[6,1024,64]{1,2,0:T(8,128)(2,1)}, f32[6,100]{1,0:T(8,128)S(1)}, f32[6,1024]{1,0:T(8,128)S(1)}, s32[6,1024]{1,0:T(8,128)S(1)}, /...) while((s32[]{:T(128)}, bf16[6,1024,64]{1,2,0:T(8,128)(2,1)}, ...), condition=%wide.region_10.11_spmd, body=%wide.region_2.10_spmd.sunk | while | flops 1833279360 | bytes 45661668 | solution.py:260
  141.9 6.4 copy.160
  155.2 6.4 copy.157
  193.2 6.4 copy.160
  206.4 6.4 copy.157
  244.4 6.4 copy.160
  257.7 6.4 copy.157
  295.6 6.4 copy.160
  308.9 6.4 copy.157
  346.9 6.4 copy.160
  360.1 6.4 copy.157
  398.1 6.4 copy.160
  411.4 6.4 copy.157
  427.0 15.5 all-reduce.11.cloned.1.call-done
  445.3 63.9 %all-gather.6.cloned.1.call-done = bf16[768,1536]{1,0:T(8,128)(2,1)} async-done(((bf16[48,1536]{1,0:T(8,128)(2,1)}), bf16[768,1536]{1,0:T(8,128)(2,1)}) %all-gather.6.cloned.1.call-update) | async-done | bytes 2359312 | tf_op jit(solution)/shard_map/all_gather | solution.py:243
  509.2 6.5 fusion.183
  515.7 57.6 %all-gather.8.cloned.1.call-done = bf16[1536,768]{0,1:T(8,128)(2,1)} async-done(((bf16[1536,48]{0,1:T(8,128)(2,1)}), bf16[1536,768]{0,1:T(8,128)(2,1)}) %all-gather.8.cloned.1.call-update) | async-done | bytes 2359312 | tf_op jit(solution)/shard_map/all_gather | solution.py:244
  573.3 8.4 fusion.128
  587.3 8.4 convolution_convert_fusion.6
  595.7 10.9 all-reduce.13.cloned.1.call-done
  617.5 433.7 %while.33 = (s32[]{:T(128)}, bf16[6,1024,64]{1,2,0:T(8,128)(2,1)}, bf16[6,1024,64]{1,2,0:T(8,128)(2,1)}, bf16[6,1024,64]{1,2,0:T(8,128)(2,1)}, bf16[6,1024,64]{2...) while((s32[]{:T(128)}, bf16[6,1024,64]{1,2,0:T(8,128)(2,1)}, ...), condition=%wide.region_25.26_spmd, body=%wide.region_18.25_spmd.sunk | while | flops 7786354176 | bytes 111154696 | solution.py:301
  648.8 6.4 copy.162
  718.0 6.4 copy.162
  1072.4 7.9 fusion.157
  1081.7 6.4 fusion.182
  1093.5 42.8 %all-reduce.4 = (f32[768]{0:T(1024)S(1)}, f32[768]{0:T(1024)S(1)}) all-reduce(f32[768]{0:T(1024)S(1)} %get-tuple-element.402, f32[768]{0:T(1024)S(1)} %copy-done.31), channel_id=2, replica_groups=mesh['batch'=16,'head'=2] {'batch'}, use_global_device_ids=true, to_apply=%region_30.31.clone | all-reduce | flops 1536 | bytes 12288
  1143.7 68.7 %reduce-scatter.7.cloned.1.call-done = f32[384,48]{0,1:T(8,128)} async-done(((f32[384,768]{0,1:T(8,128)}), f32[384,48]{0,1:T(8,128)}) %reduce-scatter.7.cloned.1.call-update) | async-done | bytes 73744 | tf_op jit(solution)/shard_map/reduce_scatter | solution.py:328
  1212.4 139.2 %reduce-scatter.5.cloned.1.call-done = f32[48,3,384]{2,0,1:T(8,128)} async-done(((f32[768,3,384]{2,0,1:T(8,128)}), f32[48,3,384]{2,0,1:T(8,128)}) %reduce-scatter.5.cloned.1.call-update) | async-done | bytes 221200 | tf_op jit(solution)/shard_map/reduce_scatter | solution.py:327
  1351.7 143.1 %reduce-scatter.11.cloned.1.call-done = f32[1536,48]{0,1:T(8,128)} async-done(((f32[1536,768]{0,1:T(8,128)}), f32[1536,48]{0,1:T(8,128)}) %reduce-scatter.11.cloned.1.call-update) | async-done | bytes 294928 | tf_op jit(solution)/shard_map/reduce_scatter | solution.py:209
  1494.7 141.8 %reduce-scatter.9.cloned.1.call-done = f32[48,1536]{1,0:T(8,128)} async-done(((f32[768,1536]{1,0:T(8,128)}), f32[48,1536]{1,0:T(8,128)}) %reduce-scatter.9.cloned.1.call-update) | async-done | bytes 294928 | tf_op jit(solution)/shard_map/reduce_scatter | solution.py:208
  (639 shorter events, 710.8 us)
Async XLA Ops:
  7.2 93.0 %copy-start.2 = (bf16[1,1024,768]{2,1,0:T(8,128)(2,1)S(1)}, bf16[1,1024,768]{2,1,0:T(8,128)(2,1)}, u32[]{:S(2)}) copy-start(bf16[1,1024,768]{2,1,0:T(8,128)(2,1)} %param.15) | copy-start | bytes 4718596
  7.2 93.9 %all-gather.4.cloned.1.call-start = ((), (), s32[]{:S(2)}) async-start(), calls=%async_computation.4 | async-start | bytes 1880064 | tf_op jit(solution)/shard_map/all_gather | solution.py:240
  7.9 434.6 %all-reduce.11.cloned.1.call-start = ((), (), s32[]{:S(2)}) async-start(), calls=%async_computation.5 | async-start | bytes 3145728 | tf_op jit(solution)/shard_map/psum | solution.py:268
  55.3 48.5 %copy-start.29 = (f32[768]{0:T(1024)}, f32[768]{0:T(1024)S(1)}, u32[]{:S(2)}) copy-start(f32[768]{0:T(1024)S(1)} %convert_element_type.242) | copy-start | bytes 9220
  100.5 5.5 copy-start.25
  101.1 4.9 copy-start.27
  110.1 4.0 copy-start.24
  425.6 83.5 %all-gather.6.cloned.1.call-start = ((), (), s32[]{:S(2)}) async-start(), calls=%async_computation.6 | async-start | bytes 2506752 | tf_op jit(solution)/shard_map/all_gather | solution.py:243
  426.4 147.0 %all-gather.8.cloned.1.call-start = ((), (), s32[]{:S(2)}) async-start(), calls=%async_computation.7 | async-start | bytes 2506752 | tf_op jit(solution)/shard_map/all_gather | solution.py:244
  426.9 179.6 %all-reduce.13.cloned.1.call-start = ((), (), s32[]{:S(2)}) async-start(), calls=%async_computation.8 | async-start | bytes 3145728 | tf_op jit(solution)/shard_map/psum | solution.py:285
  427.0 183.8 %copy-start.20 = (f32[768]{0:T(1024)}, f32[768]{0:T(1024)S(1)}, u32[]{:S(2)}) copy-start(f32[768]{0:T(1024)S(1)} %convert_element_type.250) | copy-start | bytes 9220
  444.5 166.3 %copy-start.18 = (f32[1024]{0:T(1024)}, f32[1024]{0:T(1024)S(1)}, u32[]{:S(2)}) copy-start(f32[1024]{0:T(1024)S(1)} %broadcast_multiply_fusion.5) | copy-start | bytes 12292
  445.3 165.6 %copy-start.22 = (f32[1024]{0:T(1024)}, f32[1024]{0:T(1024)S(1)}, u32[]{:S(2)}) copy-start(f32[1024]{0:T(1024)S(1)} %add_rsqrt_fusion) | copy-start | bytes 12292
  573.3 10.1 copy-start.32
  587.2 501.7 %all-reduce.15.cloned.1.call-start = ((), (), s32[]{:S(2)}) async-start(), calls=%async_computation.13 | async-start | bytes 6291456 | tf_op jit(solution)/shard_map/psum | solution.py:275
  606.6 4.3 copy-start.9
  606.6 4.3 copy-start.16
  613.6 3.9 copy-start.6
  664.9 6.4 copy-start.1
  672.4 3.7 copy-start
  734.1 6.4 copy-start.1
  803.3 6.4 copy-start.1
  872.5 6.4 copy-start.1
  880.0 3.7 copy-start
  941.7 6.4 copy-start.1
  1011.0 6.4 copy-start.1
  1056.9 155.5 %reduce-scatter.7.cloned.1.call-start = ((), (), s32[]{:S(2)}) async-start(), calls=%async_computation.10 | async-start | bytes 1253376 | tf_op jit(solution)/shard_map/reduce_scatter | solution.py:328
  1064.6 287.1 %reduce-scatter.5.cloned.1.call-start = ((), (), s32[]{:S(2)}) async-start(), calls=%async_computation.9 | async-start | bytes 3760128 | tf_op jit(solution)/shard_map/reduce_scatter | solution.py:327
  1071.0 423.7 %reduce-scatter.11.cloned.1.call-start = ((), (), s32[]{:S(2)}) async-start(), calls=%async_computation.12 | async-start | bytes 5013504 | tf_op jit(solution)/shard_map/reduce_scatter | solution.py:209
  1080.3 556.2 %reduce-scatter.9.cloned.1.call-start = ((), (), s32[]{:S(2)}) async-start(), calls=%async_computation.11 | async-start | bytes 5013504 | tf_op jit(solution)/shard_map/reduce_scatter | solution.py:208
  1088.9 4.6 copy-start.31
  1093.5 46.8 %copy-start.8 = (f32[1024,768]{1,0:T(8,128)S(1)}, f32[1024,768]{1,0:T(8,128)}, u32[]{:S(2)}) copy-start(f32[1024,768]{1,0:T(8,128)} %copy-done.6) | copy-start | bytes 9437188
  (21 other events, 47.0 us)
Sparse Core Ops, SparseCore 0:
  10.7 64.6 all-gather.3
  425.7 16.6 all-reduce.10
  445.7 63.4 all-gather.5
  512.2 61.0 all-gather.7
  587.3 19.1 all-reduce.12
  1057.1 24.4 all-reduce.14
  1087.6 124.8 reduce-scatter.6
  1218.9 132.6 reduce-scatter.4
  1358.2 136.4 reduce-scatter.10
  1500.3 136.1 reduce-scatter.8
where the time goes:
time: 1660 us; the launch traced here: 1640 us
  waiting for transfers between devices  643 us (39%)
  matrix products  403 us (24%)
  local copies, waits for them, and re-layouts  245 us (15%)
  other arithmetic  188 us (11%)
  blocking collectives  128 us (8%)
  loops' own time  21 us (1%)
    reduce_scatter x1, waiting for transfers between devices, reduce_ffn(): lax.psum_scatter(down_part, 'batch', scatter_dimension=1, tiled=True)  143 us
    reduce_scatter x1, waiting for transfers between devices, reduce_ffn(): lax.psum_scatter(up_part, 'batch', scatter_dimension=0, tiled=True)  142 us
    reduce_scatter x1, waiting for transfers between devices, on_device(): lax.psum_scatter(qkv_part, 'batch', scatter_dimension=0, tiled=True)  139 us
    while x54, local copies, waits for them, and re-layouts  117 us
    unnamed x2, blocking collectives  86.4 us
    reduce_scatter x1, waiting for transfers between devices, on_device(): lax.psum_scatter(out_part, 'batch', scatter_dimension=1, tiled=True)  68.7 us
    all_gather x1, waiting for transfers between devices, on_device(): lax.all_gather(up_weight, 'batch', axis=0, tiled=True)  63.9 us
    all_gather x1, waiting for transfers between devices, on_device(): lax.all_gather(down_weight, 'batch', axis=1, tiled=True)  57.6 us
  transfers between devices with their start and end apart: 10, of which 8 were waited for; matrix products, arithmetic and copies ran while one was open for 4% of the time, Pallas kernels for 0%

commit v1 on v0

v1 whole, which is shorter than its diff:
```python
import functools

import jax
import jax.numpy as jnp
from jax import lax
from jax.experimental import pallas as pl
from jax.experimental.pallas import tpu as pltpu
from jax.sharding import PartitionSpec as P

F32=jnp.float32; BF=jnp.bfloat16
BIG=1e30
NT=(((1,),(1,)),((),()))
TN=(((0,),(0,)),((),()))
NN=(((1,),(0,)),((),()))
def dot(a,b,dims=NN): return lax.dot_general(a,b,dims,preferred_element_type=F32)
def split3(x):
    a=x.astype(BF); r=x-a.astype(F32); b=r.astype(BF); c=(r-b.astype(F32)).astype(BF)
    return a,b,c
def split2(x):
    a=x.astype(BF); return a,(x-a.astype(F32)).astype(BF)
L=1024
def lane(shape): return lax.broadcasted_iota(jnp.int32,shape,len(shape)-1)
def sub(shape): return lax.broadcasted_iota(jnp.int32,shape,len(shape)-2)

def build_masks(own_row, topT):
    mt=jnp.where(own_row==sub((128,L)),1.0,0.0).astype(BF)
    m=jnp.transpose(mt)
    hi=lax.shift_right_arithmetic(topT,5); bit=lax.shift_left(jnp.int32(1),topT&31)
    words=L//32
    a_iota=sub((words,128))
    w=jnp.zeros((words,128),jnp.int32)
    for t in range(topT.shape[0]):
        w=w|jnp.where(hi[t:t+1]==a_iota,bit[t:t+1],0)
    b_iota=sub((32,128)); ln=lane((32,128))
    extra=(ln>=100)&(ln<103)
    ns=[];ts=[]
    for a in range(words):
        b=(lax.shift_right_logical(jnp.broadcast_to(w[a:a+1],(32,128)),b_iota)&1)
        tmf=b.astype(F32)
        ts.append(tmf)
        ns.append(jnp.where(extra,-1.0,jnp.where(b==1,0.0,-BIG)))
    n=jnp.concatenate(ns,0).astype(BF)
    tm=jnp.transpose(jnp.concatenate(ts,0)).astype(BF)
    return m,mt,n,tm

def mask_kernel(cl,tt,m,mt,n,tm):
    a,b,c,d=build_masks(cl[0],tt[0])
    m[0]=a;mt[0]=b;n[0]=c;tm[0]=d
def masks(cluster,topk):
    H=cluster.shape[0]
    tt=jnp.pad(topk.transpose(0,2,1),((0,0),(0,0),(0,128-topk.shape[1])),constant_values=-1)
    return pl.pallas_call(mask_kernel,grid=(H,),
      in_specs=[pl.BlockSpec((1,1,L),lambda h:(h,0,0)),pl.BlockSpec((1,tt.shape[1],128),lambda h:(h,0,0))],
      out_specs=[pl.BlockSpec((1,L,128),lambda h:(h,0,0)),pl.BlockSpec((1,128,L),lambda h:(h,0,0)),pl.BlockSpec((1,L,128),lambda h:(h,0,0)),pl.BlockSpec((1,128,L),lambda h:(h,0,0))],
      out_shape=[jax.ShapeDtypeStruct((H,L,128),BF),jax.ShapeDtypeStruct((H,128,L),BF),jax.ShapeDtypeStruct((H,L,128),BF),jax.ShapeDtypeStruct((H,128,L),BF)],
      compiler_params=pltpu.CompilerParams(vmem_limit_bytes=50<<20))(cluster[:,None,:],tt)

TQ=256
def fwd_head(odd, q, k, v, m_ref, mt, n_ref, tm, seg_row, qaug, kaug):
    ln=lane((L,128)); mine=(ln>=64) if odd else (ln<64)
    lc=lane((128,128)); minec=(lc>=64) if odd else (lc<64)
    zero=jnp.zeros((),BF)
    qm=jnp.where(mine,q,zero)
    vaug=jnp.where(mine,v,jnp.ones((),BF))
    cnt=jnp.maximum(jnp.sum(mt.astype(F32),axis=1,keepdims=True),1.0)
    cen=(dot(mt,qm)/cnt).astype(BF)
    cs=(cen.astype(F32)*0.125).astype(BF)
    s=dot(cs,k,NT)
    cio=sub((128,L))
    cm=lax.rem(sub((128,1)),jnp.int32(10))
    s=jnp.where(seg_row==cm,s,-BIG)
    mx=jnp.max(s,axis=1,keepdims=True)
    e=jnp.exp(s-mx)
    tot=jnp.sum(e,axis=1,keepdims=True)
    prob=e/tot
    tmf=tm.astype(F32)
    mass=jnp.sum(prob*tmf,axis=1,keepdims=True)
    rw=(prob*(1.0-tmf)).astype(BF)
    rest=dot(rw,v)
    massb=jnp.broadcast_to(mass,(128,128))
    r=jnp.where(minec,rest,massb)
    rh,rl=split2(r)
    rr=jnp.concatenate([rh,rl],1)
    qaug[:,:128]=(qm.astype(F32)*0.125).astype(BF)
    qaug[:,128:]=m_ref
    kaug[:,:128]=k
    kaug[:,128:]=n_ref
    ex=[];att=[];mb=[]
    lt=lane((TQ,128)); minet=(lt>=64) if odd else (lt<64)
    for t in range(L//TQ):
        sl=pl.ds(t*TQ,TQ)
        sc=dot(qaug[sl,:],kaug[...],NT)
        mm=jnp.max(sc,axis=1,keepdims=True)
        p=jnp.exp(sc-mm).astype(BF)
        o=dot(p,vaug)
        mt_=qaug[sl,128:]
        ee=dot(mt_,rr); ee=ee[:,:128]+ee[:,128:]
        osw=pltpu.roll(o,64,1); esw=pltpu.roll(ee,64,1)
        exact=o/osw
        a=exact*esw+ee
        tot_=jnp.where(minet,osw,o); ms_=jnp.where(minet,esw,ee)
        lse=mm+jnp.log(tot_)-jnp.log(jnp.maximum(ms_,1e-37))
        h3,m3,l3=split3(lse)
        mbt=jnp.where(lt==100,h3.astype(F32),jnp.where(lt==101,m3.astype(F32),jnp.where(lt==102,l3.astype(F32),mt_.astype(F32)))).astype(BF)
        ex.append(exact);att.append(a);mb.append(mbt)
    return ex,att,mb,prob

def fwd_kernel(q,k,v,m,mt,n,tm,seg,att_o,ex_o,mb_o,prob_o,qaug,kaug):
    res=[]
    for h in range(2):
        ex,att,mb,prob=fwd_head(h==1,q[...],k[...],v[...],m[h],mt[h],n[h],tm[h],seg[...],qaug,kaug)
        lt=lane((TQ,128));
        for t in range(L//TQ):
            sl=pl.ds(t*TQ,TQ)
            mb_o[h,sl,:]=mb[t]
            if h==0:
                att_o[sl,:]=att[t].astype(BF); ex_o[sl,:]=ex[t]
            else:
                att_o[sl,:]=jnp.where(lt<64,att_o[sl,:],att[t].astype(BF))
                ex_o[sl,:]=jnp.where(lt<64,ex_o[sl,:],ex[t])
        prob_o[h]=prob
def attn_fwd(qkv,M,MT,N,TM,seg):
    H=M.shape[0]; P2=H//2
    ps=lambda off: pl.BlockSpec((L,128),lambda p,off=off:(0,off+p))
    hs=lambda a,b: pl.BlockSpec((2,a,b),lambda p:(p,0,0))
    return pl.pallas_call(fwd_kernel,grid=(P2,),
      in_specs=[ps(0),ps(P2),ps(2*P2),hs(L,128),hs(128,L),hs(L,128),hs(128,L),pl.BlockSpec((1,L),lambda p:(0,0))],
      out_specs=[ps(0),ps(0),hs(L,128),hs(128,L)],
      out_shape=[jax.ShapeDtypeStruct((L,P2*128),BF),jax.ShapeDtypeStruct((L,P2*128),F32),jax.ShapeDtypeStruct((H,L,128),BF),jax.ShapeDtypeStruct((H,128,L),F32)],
      scratch_shapes=[pltpu.VMEM((L,256),BF),pltpu.VMEM((L,256),BF)],
      compiler_params=pltpu.CompilerParams(vmem_limit_bytes=50<<20))(qkv,qkv,qkv,M,MT,N,TM,seg)

TJ=256
def bwd_kernel(q,k,v,g,ex,mb,mt_r,n,tm_r,prob_r,dq_o,dk_o,dv_o,qaug,kaug,gaug,vaug,dqt):
    ln=lane((L,128)); zero=jnp.zeros((),BF)
    lc=lane((128,128))
    qv=q[...];kv=k[...];vv=v[...];gv=g[...]
    kT=jnp.transpose(kv)
    prod=gv.astype(F32)*ex[...]
    for h in range(2):
        mine=(ln>=64) if h else (ln<64); minec=(lc>=64) if h else (lc<64)
        o=0 if h else 64
        r=jnp.sum(jnp.where(mine,prod,0.0),axis=1,keepdims=True)
        h3,m3,l3=split3(r)
        gm=jnp.where(mine,gv,zero)
        ga=jnp.where(ln==o,h3.astype(F32),jnp.where(ln==o+1,m3.astype(F32),jnp.where(ln==o+2,l3.astype(F32),gm.astype(F32)))).astype(BF)
        gaug[...]=ga
        vaug[...]=jnp.where(mine,vv,jnp.where((ln>=o)&(ln<o+3),jnp.full((),-1.0,BF),zero))
        qm=jnp.where(mine,qv,zero); qs=(qm.astype(F32)*0.125).astype(BF)
        qaug[:,:128]=qs; qaug[:,128:]=mb[h]
        kaug[:,:128]=kv; kaug[:,128:]=n[h]
        mt=mt_r[h]; tm=tm_r[h]; prob=prob_r[h]
        cnt=jnp.maximum(jnp.sum(mt.astype(F32),axis=1,keepdims=True),1.0)
        cen=(dot(mt,qm)/cnt).astype(BF)
        cs=(cen.astype(F32)*0.125).astype(BF)
        gr=dot(mt,ga)
        gmass=jnp.sum(jnp.where((lc>=o)&(lc<o+3),gr,0.0),axis=1,keepdims=True)
        grest=jnp.where(minec,gr,0.0).astype(BF)
        gp=dot(grest,vv,NT)
        tmb=tm.astype(F32)
        top=tmb>0.5
        gp=jnp.where(top,gmass,gp)
        t=jnp.sum(prob*gp,axis=1,keepdims=True)
        gs=(prob*(gp-t)).astype(BF)
        rw=jnp.where(top,0.0,prob).astype(BF)
        km=jnp.where(mine,kv,zero)
        gcen=dot(gs,km)/cnt
        gh,gl=split2(gcen)
        gg=jnp.concatenate([gh,gl],1)
        gsT=jnp.transpose(gs); rwT=jnp.transpose(rw)
        kTh=kT[64*h:64*h+64]
        gam=jnp.where(mine,gv,zero)
        for t_ in range(L//TJ):
            sl=pl.ds(t_*TJ,TJ)
            st=dot(kaug[sl,:],qaug[...],NT)
            p=jnp.exp(st)
            dp=dot(vaug[sl,:],gaug[...],NT)
            ds=(p*dp).astype(BF)
            pb=p.astype(BF)
            dv=dot(pb,gam)+dot(rwT[t_*TJ:(t_+1)*TJ],grest)
            dk=dot(ds,qs)+dot(gsT[t_*TJ:(t_+1)*TJ],cs)
            if h==0:
                dv_o[sl,:]=dv; dk_o[sl,:]=dk
            else:
                dv_o[sl,:]+=dv; dk_o[sl,:]+=dk
            dqp=dot(kTh[:,t_*TJ:(t_+1)*TJ],ds)
            if t_==0: dqt[64*h:64*h+64,:]=dqp
            else: dqt[64*h:64*h+64,:]+=dqp
        mbv=jnp.where(lane((L,128))<100,mb[h],zero)
        dd=dot(mbv,gg); dd=dd[:,:128]+dd[:,128:]
        if h==0: dq_o[...]=dd
        else: dq_o[...]+=dd
    dq_o[...]=(dq_o[...]+jnp.transpose(dqt[...]))*0.125
def bwd_wrap(q,k,v,g,ex,mb,mt_r,n,tm_r,prob_r,dq,dk,dv,qaug,kaug,gaug,vaug,dqt,dqs,dks,dvs):
    bwd_kernel(q,k,v,g,ex,mb,mt_r,n,tm_r,prob_r,dqs,dks,dvs,qaug,kaug,gaug,vaug,dqt)
    dq[...]=dqs[...].astype(BF);dk[...]=dks[...].astype(BF);dv[...]=dvs[...].astype(BF)
def attn_bwd(qkv,g,ex,MB,MT,N,TM,prob):
    H=N.shape[0]; P2=H//2
    ps=lambda off: pl.BlockSpec((L,128),lambda p,off=off:(0,off+p))
    hs=lambda a,b: pl.BlockSpec((2,a,b),lambda p:(p,0,0))
    o=jax.ShapeDtypeStruct((L,P2*128),BF)
    return pl.pallas_call(bwd_wrap,grid=(P2,),
      in_specs=[ps(0),ps(P2),ps(2*P2),ps(0),ps(0),hs(L,128),hs(128,L),hs(L,128),hs(128,L),hs(128,L)],
      out_specs=[ps(0),ps(0),ps(0)],
      out_shape=[o,o,o],
      scratch_shapes=[pltpu.VMEM((L,256),BF),pltpu.VMEM((L,256),BF),pltpu.VMEM((L,128),BF),pltpu.VMEM((L,128),BF),pltpu.VMEM((128,L),F32)]+[pltpu.VMEM((L,128),F32)]*3,
      compiler_params=pltpu.CompilerParams(vmem_limit_bytes=50<<20))(qkv,qkv,qkv,g,ex,MB,MT,N,TM,prob)
MESH=pl.DeviceIdType.MESH


GN=1;GM=1;SA=1;SN=1
def NOP(p): pass
class Place:
    def __init__(self, nb):
        self.nz=nb//4
        self.b=lax.axis_index("batch"); self.h=lax.axis_index("head")
        self.z=self.b//4; self.r=lax.rem(self.b,4)
        even=lax.rem(self.r,2)==0
        self.rx=jnp.where(even,self.r+1,self.r-1)
        self.ry=jnp.where(self.r<2,self.r+2,self.r-2)
        self.rd=3-self.r
        self.X=(self.z*4+self.rx,self.h); self.Y=(self.z*4+self.ry,self.h)
        self.up=(self.b+4,self.h); self.dn=(self.b-4,self.h); self.twin=(self.b,1-self.h)
    def barrier(self):
        bar=pltpu.get_barrier_semaphore()
        for d in (self.X,self.Y,self.twin):
            pl.semaphore_signal(bar,inc=1,device_id=d,device_id_type=MESH)
        @pl.when(self.z<self.nz-1)
        def _(): pl.semaphore_signal(bar,inc=1,device_id=self.up,device_id_type=MESH)
        @pl.when(self.z>0)
        def _(): pl.semaphore_signal(bar,inc=1,device_id=self.dn,device_id_type=MESH)
        lines=jnp.where(self.z<self.nz-1,1,0)+jnp.where(self.z>0,1,0)
        pl.semaphore_wait(bar,3+lines)

def rc(src,dst,ss,rs,dev):
    return pltpu.make_async_remote_copy(src_ref=src,dst_ref=dst,send_sem=ss,recv_sem=rs,device_id=dev,device_id_type=MESH)

class Gather:
    def __init__(self, pc, g, ss, rs):
        self.pc=pc; self.g=g; self.ss=ss; self.rs=rs; self.n=2*(pc.nz-1)
    def cz(self,p,zz,k,dev):
        s=self.g.at[p,zz,self.pc.r]
        return rc(s,s,self.ss.at[p,k],self.rs.at[p,k],dev)
    def z0(self,p):
        c=self.pc
        @pl.when(c.z<c.nz-1)
        def _(): self.cz(p,c.z,0,c.up).start()
        @pl.when(c.z>0)
        def _(): self.cz(p,c.z,1,c.dn).start()
    def zk(self,p,d):
        c=self.pc
        @pl.when(c.z-d>=0)
        def _():
            self.cz(p,c.z-d,2*(d-1),c.up).wait_recv()
        if d<c.nz-1:
            @pl.when((c.z-d>=0)&(c.z<c.nz-1))
            def _(): self.cz(p,c.z-d,2*d,c.up).start()
        @pl.when(c.z+d<c.nz)
        def _():
            self.cz(p,c.z+d,2*(d-1)+1,c.dn).wait_recv()
        if d<c.nz-1:
            @pl.when((c.z+d<c.nz)&(c.z>0))
            def _(): self.cz(p,c.z+d,2*d+1,c.dn).start()
    def cb(self,p,r,k,dev):
        s=self.g.at[p,:,r]
        return rc(s,s,self.ss.at[p,self.n+k],self.rs.at[p,self.n+k],dev)
    def ch(self,p,r,lo,k,dev):
        h=self.pc.nz//2
        s=self.g.at[p,pl.ds(0,h),r] if lo else self.g.at[p,pl.ds(h,self.pc.nz-h),r]
        return rc(s,s,self.ss.at[p,self.n+k],self.rs.at[p,self.n+k],dev)
    def x0(self,p):
        c=self.pc
        self.cb(p,c.r,0,c.X).start(); self.cb(p,c.r,1,c.Y).start()
    def x1(self,p):
        c=self.pc
        self.cb(p,c.rx,0,c.X).wait_recv()
        self.ch(p,c.rx,True,2,c.Y).start()
        self.cb(p,c.ry,1,c.Y).wait_recv()
        self.ch(p,c.ry,False,3,c.X).start()
    def x2(self,p):
        c=self.pc
        self.ch(p,c.rd,True,2,c.Y).wait_recv()
        self.ch(p,c.rd,False,3,c.X).wait_recv()
    def drain(self,p):
        c=self.pc
        for d in range(c.nz-1):
            @pl.when((c.z-d>=0)&(c.z<c.nz-1))
            def _(): self.cz(p,c.z-d,2*d,c.up).wait_send()
            @pl.when((c.z+d<c.nz)&(c.z>0))
            def _(): self.cz(p,c.z+d,2*d+1,c.dn).wait_send()
        self.cb(p,c.r,0,c.X).wait_send(); self.cb(p,c.r,1,c.Y).wait_send()
        self.ch(p,c.rx,True,2,c.Y).wait_send(); self.ch(p,c.ry,False,3,c.X).wait_send()
    def steps(self):
        nz=self.pc.nz
        def last(p):
            self.zk(p,nz-1); self.x0(p)
        return [self.z0]+[functools.partial(lambda d,p:self.zk(p,d),d) for d in range(1,nz-1)]+[last]+[NOP]*GN+[self.x1]+[NOP]*GM+[self.x2]

class Scatter:
    def __init__(self, pc, g, d, rx, ry, ru, rd, ss, rs):
        self.pc=pc;self.g=g;self.d=d;self.bx=rx;self.by=ry;self.bu=ru;self.bd=rd;self.ss=ss;self.rs=rs
        self.h=pc.nz//2
    def half(self,p,r,lo):
        h=self.h; n=self.pc.nz
        return (self.g.at[p,pl.ds(0,h),r],self.d.at[p,pl.ds(0,h)]) if lo else (self.g.at[p,pl.ds(h,n-h),r],self.d.at[p,pl.ds(h,n-h)])
    def c0(self,p,lo):
        s,t=self.half(p,self.pc.rd,lo); k=0 if lo else 1
        return rc(s,t,self.ss.at[p,k],self.rs.at[p,k],self.pc.X if lo else self.pc.Y)
    def c1(self,p,x):
        c=self.pc
        return rc(self.g.at[p,:,c.rx if x else c.ry],(self.bx if x else self.by).at[p],self.ss.at[p,2 if x else 3],self.rs.at[p,2 if x else 3],c.X if x else c.Y)
    def cu(self,p,zz,up):
        c=self.pc; k=4+zz if up else 4+c.nz+zz
        return rc(self.g.at[p,zz,c.r],(self.bu if up else self.bd).at[p,zz],self.ss.at[p,k],self.rs.at[p,k],c.up if up else c.dn)
    def add(self,dst,*srcs):
        v=dst[...].astype(F32)
        for s in srcs: v=v+s[...].astype(F32)
        dst[...]=v.astype(BF)
    def s0(self,p):
        self.c0(p,True).start(); self.c0(p,False).start()
    def s1(self,p):
        c=self.pc;h=self.h;n=c.nz
        self.c0(p,True).wait_recv()
        self.add(self.g.at[p,pl.ds(0,h),c.ry],self.d.at[p,pl.ds(0,h)])
        self.c1(p,False).start()
        self.c0(p,False).wait_recv()
        self.add(self.g.at[p,pl.ds(h,n-h),c.rx],self.d.at[p,pl.ds(h,n-h)])
        self.c1(p,True).start()
    def s2(self,p):
        c=self.pc
        self.c1(p,True).wait_recv(); self.c1(p,False).wait_recv()
        self.add(self.g.at[p,:,c.r],self.bx.at[p],self.by.at[p])
        self.zk(p,0)
    def zk(self,p,k):
        c=self.pc; nz=c.nz
        @pl.when(c.z==k)
        def _():
            for zz in range(nz-1,k,-1):
                if k>0:
                    self.cu(p,zz,True).wait_recv()
                    self.add(self.g.at[p,zz,c.r],self.bu.at[p,zz])
                self.cu(p,zz,True).start()
        @pl.when(c.z==nz-1-k)
        def _():
            for zz in range(0,nz-1-k):
                if k>0:
                    self.cu(p,zz,False).wait_recv()
                    self.add(self.g.at[p,zz,c.r],self.bd.at[p,zz])
                self.cu(p,zz,False).start()
    def fin(self,p,out):
        c=self.pc
        out[p]=self.g[p,c.z,c.r].astype(F32)
        @pl.when(c.z>0)
        def _():
            self.cu(p,c.z,True).wait_recv()
            out[p]+=self.bu[p,c.z].astype(F32)
        @pl.when(c.z<c.nz-1)
        def _():
            self.cu(p,c.z,False).wait_recv()
            out[p]+=self.bd[p,c.z].astype(F32)
    def drain(self,p):
        c=self.pc; nz=c.nz
        self.c0(p,True).wait_send(); self.c0(p,False).wait_send()
        self.c1(p,True).wait_send(); self.c1(p,False).wait_send()
        for zz in range(nz):
            @pl.when(zz>c.z)
            def _(): self.cu(p,zz,True).wait_send()
            @pl.when(zz<c.z)
            def _(): self.cu(p,zz,False).wait_send()
    def steps(self,out):
        nz=self.pc.nz
        return [self.s0]+[NOP]*SA+[self.s1]+[NOP]*SN+[self.s2]+[functools.partial(lambda k,p:self.zk(p,k),k) for k in range(1,nz-1)]+[lambda p:self.fin(p,out)]

def run_all(steps,parts):
    n=len(parts); S=len(steps)
    for t in range(n+S-1):
        for s in range(S-1,-1,-1):
            if 0<=t-s<n: steps[s](parts[t-s])

def ag_kernel(nb,w,go,g,ss,rs,ls):
    pc=Place(nb); pc.barrier()
    NP=w.shape[0]
    G=Gather(pc,g,ss,rs)
    for p in range(NP): g[p,pc.z,pc.r]=w[p]
    run_all(G.steps(),list(range(NP)))
    for p in range(NP): G.drain(p)
    c=pltpu.make_async_copy(g,go,ls); c.start(); c.wait()
def all_gather(w,nb,cid=0):
    NP,R,N=w.shape; nz=nb//4
    return pl.pallas_call(functools.partial(ag_kernel,nb),
      out_shape=jax.ShapeDtypeStruct((NP,nz,4,R,N),BF),
      in_specs=[pl.BlockSpec(memory_space=pltpu.VMEM)],out_specs=pl.BlockSpec(memory_space=pl.ANY),
      scratch_shapes=[pltpu.VMEM((NP,nz,4,R,N),BF),pltpu.SemaphoreType.DMA((NP,2*(nz-1)+4)),pltpu.SemaphoreType.DMA((NP,2*(nz-1)+4)),pltpu.SemaphoreType.DMA],
      compiler_params=pltpu.CompilerParams(collective_id=cid,has_side_effects=True,vmem_limit_bytes=60<<20))(w)
def rs_kernel(nb,gi,out,g,d,bx,by,bu,bd,ss,rs,ls):
    pc=Place(nb); pc.barrier()
    NP=g.shape[0]
    c=pltpu.make_async_copy(gi,g,ls); c.start(); c.wait()
    S=Scatter(pc,g,d,bx,by,bu,bd,ss,rs)
    run_all(S.steps(out),list(range(NP)))
    for p in range(NP): S.drain(p)
def reduce_scatter(g,cid=1):
    NP,nz,_,R,N=g.shape
    land=pltpu.VMEM((NP,nz,R,N),BF)
    return pl.pallas_call(functools.partial(rs_kernel,nz*4),
      out_shape=jax.ShapeDtypeStruct((NP,R,N),F32),
      in_specs=[pl.BlockSpec(memory_space=pl.ANY)],out_specs=pl.BlockSpec(memory_space=pltpu.VMEM),
      scratch_shapes=[pltpu.VMEM((NP,nz,4,R,N),BF)]+[land]*5+[pltpu.SemaphoreType.DMA((NP,4+2*nz)),pltpu.SemaphoreType.DMA((NP,4+2*nz)),pltpu.SemaphoreType.DMA],
      compiler_params=pltpu.CompilerParams(collective_id=cid,has_side_effects=True,vmem_limit_bytes=60<<20))(g)

EPS=1e-5
def norm_forward(values, gain_row):
    row_mean = jnp.mean(values, axis=-1, keepdims=True)
    centred = values - row_mean
    inverse = lax.rsqrt(jnp.mean(centred * centred, axis=-1, keepdims=True) + EPS)
    normed = centred * inverse
    return (normed * gain_row, normed, inverse)

def norm_backward(grad_out, normed, inverse, gain_row):
    grad_normed = grad_out * gain_row
    gain_grad = jnp.sum(grad_out * normed, axis=0)
    inner_term = grad_normed - jnp.mean(grad_normed, axis=-1, keepdims=True)
    inner_term = inner_term - normed * jnp.mean(grad_normed * normed, axis=-1, keepdims=True)
    return (inner_term * inverse, gain_grad)

def pack(q,o,u,d,ga,gf):
    R=q.shape[0]
    qp=q.reshape(R,3,3,128).transpose(2,0,1,3).reshape(3,R,384)
    up=u.reshape(R,4,384).transpose(1,0,2)
    dn=d.T.reshape(R,4,384).transpose(1,0,2)
    gains=jnp.pad(jnp.stack([ga,gf],1),((0,0),(0,382)))
    return jnp.concatenate([qp,o.T[None],up,dn,gains[None]],0)

def on_device(tokens,attn_gain,qkv_weight,out_weight,ffn_gain,up_weight,down_weight,cotangent,segment,cluster,top_keys):
    nb=lax.axis_size("batch")
    x=tokens[0].astype(F32)
    seg=segment; cl=cluster[0]; tk=top_keys[0]
    half=L//2
    off=lax.axis_index("head")*half
    share=lambda v: lax.dynamic_slice_in_dim(v,off,half,0)
    w=pack(qkv_weight,out_weight,up_weight,down_weight,attn_gain,ffn_gain)
    R=w.shape[1]
    custom=R%16==0 and nb%4==0
    if custom:
        W=all_gather(w,nb).reshape(13,768,384)
    else:
        W=lax.all_gather(w,"batch",axis=1,tiled=True)
    g1=W[12,:,0].astype(F32); g2=W[12,:,1].astype(F32)
    M,MT,N,TM=masks(cl,tk)
    n1,p1,i1=norm_forward(x,g1)
    n1=n1.astype(BF)
    mm=lambda s,a,b: jnp.einsum(s,a,b,preferred_element_type=F32)
    wq=W[0:3]; wo=W[3]; wu=W[4:8]; wd=W[8:12]
    qkv=mm("td,pdf->ptf",n1,wq).astype(BF)
    qkv=qkv.reshape(3,L,3,128).transpose(1,2,0,3).reshape(L,1152)
    att,ex,mb,prob=attn_fwd(qkv,M,MT,N,TM,seg)
    part=mm("te,fe->tf",att,wo)
    hid=x+lax.psum(part.astype(BF),"head").astype(F32)
    n2,p2,i2=norm_forward(hid,g2)
    n2=n2.astype(BF)
    up=mm("td,pdf->ptf",n2,wu)
    act=jax.nn.gelu(up).astype(BF)
    fp=mm("ptf,pdf->td",act,wd)
    output=(share(hid)+share(lax.psum(fp.astype(BF),"head").astype(F32))).astype(BF)[None]
    ct=cotangent[0]
    dwn_g=mm("td,ptf->pdf",ct,act)
    ga=mm("td,pdf->ptf",ct,wd)
    _,pull=jax.vjp(jax.nn.gelu,up)
    gu=pull(ga)[0].astype(BF)
    up_g=mm("td,ptf->pdf",n2,gu)
    gn=lax.psum(mm("ptf,pdf->td",gu,wu).astype(BF),"head").astype(F32)
    back,g2g=norm_backward(gn,p2,i2,g2)
    gh=ct.astype(F32)+back
    gat=gh.astype(BF)
    out_g=mm("tf,te->fe",gat,att)
    g=mm("tf,fe->te",gat,wo).astype(BF)
    dq,dk,dv=attn_bwd(qkv,g,ex,mb,MT,N,TM,prob)
    dqkv=jnp.stack([dq,dk,dv],1).reshape(L,3,3,128).transpose(2,0,1,3).reshape(3,L,384)
    qkv_g=mm("td,ptf->pdf",n1,dqkv)
    gn1=lax.psum(mm("ptf,pdf->td",dqkv,wq).astype(BF),"head").astype(F32)
    back1,g1g=norm_backward(gn1,p1,i1,g1)
    tg=(share(gh)+share(back1))[None]
    gg=jnp.pad(jnp.stack([g1g,g2g],1),((0,0),(0,382)))
    G=jnp.concatenate([dwn_g,up_g,out_g[None],qkv_g,gg[None]],0)
    if custom:
        S=reduce_scatter(G.astype(BF).reshape(13,nb//4,4,R,384))
    else:
        S=lax.psum_scatter(G,"batch",scatter_dimension=1,tiled=True)
    cat=lambda a: a.transpose(1,0,2).reshape(R,-1)
    qg=S[9:12].reshape(3,R,3,128).transpose(1,2,0,3).reshape(R,3,384)
    return output,tg,S[12,:,0],qg,S[8].T,S[12,:,1],cat(S[4:8]),cat(S[0:4]).T

def solution(mesh):
    in_specs=(P("batch",None,None),P("batch"),P("batch",None,"head"),P("head","batch"),P("batch"),P("batch","head"),P("head","batch"),P("batch",None,None),P("batch",None),P("batch","head",None),P("batch","head",None,None))
    out_specs=(P("batch","head",None),P("batch","head",None),P("batch"),P("batch",None,"head"),P("head","batch"),P("batch"),P("batch","head"),P("head","batch"))
    return jax.shard_map(on_device,mesh=mesh,in_specs=in_specs,out_specs=out_specs,check_vma=False)
```

time: 1660 us -> 411 us (0.25)
  waiting for transfers between devices: 643 us -> 25.7 us
  matrix products: 403 us -> 54.6 us
  Pallas kernels: 0 us -> 222 us
  local copies, waits for them, and re-layouts: 245 us -> 64.5 us
  other arithmetic: 188 us -> 23.1 us
  blocking collectives: 128 us -> 0 us
  loops' own time: 21 us -> 0 us
    reduce_scatter x4 -> x0, waiting for transfers between devices: 493 us -> none  [the longest x1 143 us: reduce_ffn(): lax.psum_scatter(down_part, 'batch', scatter_dimension=1, tiled=True)]
    dot_general x167 -> x12, matrix products: 401 us -> 54.6 us  [on_device(): mm = lambda s, a, b: jnp.einsum(s, a, b, preferred_element_type=F32)]
    pallas_call x0 -> x5, Pallas kernels: none -> 222 us  [the longest x1 84.2 us: all_gather(): pl.pallas_call(functools.partial(ag_kernel, nb), out_shape=jax.ShapeDtype...]
    while x57 -> x0, local copies, waits for them, and re-layouts: 123 us -> none
    all_gather x3 -> x0, waiting for transfers between devices: 122 us -> none  [the longest x1 63.9 us: on_device(): lax.all_gather(up_weight, 'batch', axis=0, tiled=True)]
    dot_general x31 -> x0, other arithmetic: 90.8 us -> none  [the longest x6 37.9 us: head_backward(): jnp.einsum('ld,ltd->lt', grad_low, values_top, preferred_element_type=jnp...]
    unnamed x2 -> x0, blocking collectives: 86.4 us -> none
    reduce_sum x54 -> x0, other arithmetic: 58.8 us -> none  [the longest x12 53.4 us: cluster_setup(): top_mask = jnp.sum(picks_full.reshape(clusters, top_count, length), axis=1)]
  transfers between devices with their start and end apart: 10 -> 3, of which waited for: 8 -> 2; matrix products, arithmetic and copies ran while one was open for 4% -> 14% of each run, Pallas kernels for 0% -> 0%
where the time goes in v1:
time: 411 us; the launch traced here: 405 us
  Pallas kernels  222 us (54%)
  local copies, waits for them, and re-layouts  64.5 us (16%)
  matrix products  54.6 us (13%)
  waiting for transfers between devices  25.7 us (6%)
  other arithmetic  23.1 us (6%)
  between operations  14.6 us (4%)
    pallas_call x1, Pallas kernels, all_gather(): pl.pallas_call(functools.partial(ag_kernel, nb), out_shape=jax.ShapeDtype...  84.2 us
    pallas_call x1, Pallas kernels, reduce_scatter(): pl.pallas_call(functools.partial(rs_kernel, nz * 4), out_shape=jax.ShapeD...  83.6 us
    dot_general x12, matrix products, on_device(): mm = lambda s, a, b: jnp.einsum(s, a, b, preferred_element_type=F32)  54.6 us
    pallas_call x1, Pallas kernels, attn_bwd(): pl.pallas_call(bwd_wrap, grid=(P2,), in_specs=[ps(0), ps(P2), ps(2 * P2),...  27.9 us
    unnamed x66, local copies, waits for them, and re-layouts  23 us
    pallas_call x1, Pallas kernels, attn_fwd(): pl.pallas_call(fwd_kernel, grid=(P2,), in_specs=[ps(0), ps(P2), ps(2 * P2...  22.9 us
    psum x1, waiting for transfers between devices, on_device(): hid = x + lax.psum(part.astype(BF), 'head').astype(F32)  13 us
    transpose x3, local copies, waits for them, and re-layouts, on_device(): mm = lambda s, a, b: jnp.einsum(s, a, b, preferred_element_type=F32)  13 us
  transfers between devices with their start and end apart: 3, of which 2 were waited for; matrix products, arithmetic and copies ran while one was open for 14% of the time, Pallas kernels for 0%

profile of v1, /device:TPU:0, one launch (start us, length us, event | category | flops | bytes accessed | tf_op | source)
XLA Modules:
  0.0 405.3 jit_solution(3844537107638646543)
XLA Ops:
  12.6 84.2 %shard_map.170 = bf16[13,4,4,48,384]{4,3,2,1,0:T(8,128)(2,1)} custom-call(bf16[13,48,384]{2,1,0:T(8,128)(2,1)} %copy-done.22), custom_call_target="tpu_custom_call" | custom-call | tf_op jit(solution)/shard_map/pallas_call | solution.py:390
  98.1 2.9 slice.46
  103.2 3.9 convolution_convert_fusion
  107.1 1.8 copy.71
  108.8 4.5 %copy.72.q.k.v = bf16[1024,1152]{1,0:T(8,128)(2,1)} copy(bf16[1024,1152]{0,1:T(8,128)(2,1)} %bitcast.182) | data formatting | bytes 4718592 | tf_op jit(solution)/shard_map/reshape | solution.py:455
  113.4 3.7 shard_map.171
  119.4 22.9 %shard_map.172 = (bf16[1024,384]{1,0:T(8,128)(2,1)S(1)}, f32[1024,384]{1,0:T(8,128)S(1)}, bf16[6,1024,128]{2,1,0:T(8,128)(2,1)S(1)}, f32[6,128,1024]{2,1,0:T(8,128)}) custom-call(bf16[1024,1152]{1,0:T(8,128)(2,1)} %copy.72.q.k.v, bf16[1024,1152]{1,0:T(8,128)(2,1)} %copy.72.q.k.v, bf16[1024,1152]{1,0:T(8,128)(2,1)} %copy.72.q.k.v, ...), custom_call_target="tpu_custom_call" | custom-call | tf_op jit(solution)/shard_map/pallas_call | solution.py:126
  144.6 2.3 convolution_convert_fusion.1
  147.5 5.1 %fusion.53 = (bf16[4,4,4,48,384]{4,3,2,1,0:T(8,128)(2,1)}, bf16[4,4,4,48,384]{4,3,2,1,0:T(8,128)(2,1)}) fusion(bf16[13,4,4,48,384]{4,3,2,1,0:T(8,128)(2,1)} %shard_map.170), kind=kLoop, calls=%fused_computation.102 | loop fusion | bytes 9437184 | tf_op jit(solution)/shard_map/slice | solution.py:453
  152.7 13.0 %all-reduce.8.cloned.1.call-done = bf16[1024,768]{1,0:T(8,128)(2,1)} async-done(((bf16[1024,768]{1,0:T(8,128)(2,1)}), bf16[1024,768]{1,0:T(8,128)(2,1)}) %all-reduce.8.cloned.1.call-update) | async-done | bytes 1572880 | tf_op jit(solution)/shard_map/psum | solution.py:458
  165.7 2.0 fusion.49
  168.5 3.2 fusion.43
  171.7 6.4 %fusion.6 = bf16[4,1024,384]{1,2,0:T(8,128)(2,1)S(1)} fusion(f32[4,384,1024]{2,1,0:T(8,128)S(1)} %fusion.43, bf16[4,768,384]{2,1,0:T(8,128)(2,1)S(1)} %bitcast.196, bf16[1,1024,768]{2,1,0:T(8,128)(2,1)S(1)} %copy-done.20), kind=kOutput, calls=%fused_computation.8 | convolution fusion | flops 2447376384 | bytes 13369344 | tf_op jit(solution)/shard_map/td,pdf->ptf/dot_general | solution.py:452
  179.8 3.8 bitcast_convert_fusion.1
  183.8 9.0 %bitcast_convert_fusion.2 = bf16[1024,768]{1,0:T(8,128)(2,1)} fusion(bf16[4,768,384]{2,1,0:T(8,128)(2,1)} %bitcast.195, f32[4,384,1024]{2,1,0:T(8,128)} %copy-done.25), kind=kOutput, calls=%fused_computation.42 | convolution fusion | flops 2430861312 | bytes 10223616 | tf_op jit(solution)/shard_map/ptf,pdf->td/dot_general | solution.py:452
  192.8 12.6 %all-reduce.10.cloned.1.call-done = bf16[1024,768]{1,0:T(8,128)(2,1)} async-done(((bf16[1024,768]{1,0:T(8,128)(2,1)}), bf16[1024,768]{1,0:T(8,128)(2,1)}) %all-reduce.10.cloned.1.call-update) | async-done | bytes 1572880 | tf_op jit(solution)/shard_map/psum | solution.py:471
  205.4 3.7 fusion.23
  209.2 2.7 fusion.21
  212.9 27.9 %shard_map.173 = (bf16[1024,384]{1,0:T(8,128)(2,1)S(1)}, bf16[1024,384]{1,0:T(8,128)(2,1)S(1)}, bf16[1024,384]{1,0:T(8,128)(2,1)S(1)}) custom-call(bf16[1024,1152]{1,0:T(8,128)(2,1)} %copy.72.q.k.v, bf16[1024,1152]{1,0:T(8,128)(2,1)} %copy.72.q.k.v, bf16[1024,1152]{1,0:T(8,128)(2,1)} %copy.72.q.k.v, bf16[1024,384]{1,0:T(8,128)(2,1)S(1)} %convolution_convert_fusion.2.g, ...), custom_call_target="tpu_custom_call" | custom-call | tf_op jit(solution)/shard_map/pallas_call | solution.py:202
  247.0 3.4 bitcast_convert_fusion
  251.9 6.7 %convert_bitcast_fusion.1 = bf16[4,768,384]{1,2,0:T(8,128)(2,1)} fusion(bf16[4,1024,384]{1,2,0:T(8,128)(2,1)} %copy-done.26, f32[768]{0:T(1024)S(1)} %convert_reduce_fusion.1, f32[1024]{0:T(1024)S(1)} %add_rsqrt_fusion, f32[1024]{0:T(1024)S(1)} %broadcast_multiply_fusion.4, bf16[1,1024,768]{2,1,0:T(8,128)(2,1)S(1)} %copy-done.7, ...), kind=kOutput, calls=%fused_computation.48 | convolution fusion | flops 2422603776 | bytes 8662016 | tf_op jit(solution)/shard_map/td,ptf->pdf/dot_general | solution.py:452
  258.6 4.3 %copy.89 = bf16[4,768,384]{2,1,0:T(8,128)(2,1)} copy(bf16[4,768,384]{1,2,0:T(8,128)(2,1)} %convert_bitcast_fusion.1) | data formatting | bytes 4718592 | tf_op jit(solution)/shard_map/td,ptf->pdf/transpose | solution.py:452
  262.9 8.4 %convert_bitcast_fusion.2 = bf16[4,768,384]{1,2,0:T(8,128)(2,1)} fusion(bf16[1,1024,768]{2,1,0:T(8,128)(2,1)} %param.18, f32[4,384,1024]{2,1,0:T(8,128)} %copy-done.25), kind=kOutput, calls=%fused_computation.49 | convolution fusion | flops 2431254528 | bytes 10223616 | tf_op jit(solution)/shard_map/td,ptf->pdf/dot_general | solution.py:452
  271.4 4.8 %copy.88 = bf16[4,768,384]{2,1,0:T(8,128)(2,1)} copy(bf16[4,768,384]{1,2,0:T(8,128)(2,1)} %convert_bitcast_fusion.2) | data formatting | bytes 4718592 | tf_op jit(solution)/shard_map/td,ptf->pdf/transpose | solution.py:452
  276.2 3.5 constant_dynamic-update-slice_fusion.5
  282.2 3.5 convert_bitcast_fusion.3
  285.6 3.8 copy.90
  289.5 3.0 convolution_convert_fusion.3
  294.8 4.6 %fusion.24 = (bf16[768]{0:T(1024)(128)(2,1)S(1)}, f32[1024]{0:T(1024)S(1)}, f32[1024]{0:T(1024)S(1)}, f32[1024,768]{1,0:T(8,128)}, f32[1024,768]{1,0:T(8,128)}) fusion(bf16[1024,768]{1,0:T(8,128)(2,1)} %get-tuple-element.39, f32[1024]{0:T(1024)S(1)} %add_rsqrt_fusion.1, f32[1024]{0:T(1024)S(1)} %broadcast_multiply_fusion.5, ...), kind=kLoop, calls=%fused_computation.36 | loop fusion | flops 7861504 | bytes 9458176 | tf_op jit(solution)/shard_map/reduce_sum | solution.py:421
  300.6 83.6 %shard_map.174 = f32[13,48,384]{2,1,0:T(8,128)} custom-call(bf16[13,4,4,48,384]{4,3,2,1,0:T(8,128)(2,1)} %constant_dynamic-update-slice_fusion.1.gi), custom_call_target="tpu_custom_call" | custom-call | tf_op jit(solution)/shard_map/pallas_call | solution.py:405
  392.1 2.4 fusion.37
  394.5 3.9 fusion.33
  (115 shorter events, 39.2 us)
Async XLA Ops:
  7.2 158.5 %all-reduce.8.cloned.1.call-start = ((), (), s32[]{:S(2)}) async-start(), calls=%async_computation | async-start | bytes 3145728 | tf_op jit(solution)/shard_map/psum | solution.py:458
  11.9 0.8 copy-start.22
  96.8 4.1 %copy-start.6 = (bf16[1,1024,768]{2,1,0:T(8,128)(2,1)S(1)}, bf16[1,1024,768]{2,1,0:T(8,128)(2,1)}, u32[]{:S(2)}) copy-start(bf16[1,1024,768]{2,1,0:T(8,128)(2,1)} %param.11) | copy-start | bytes 4718596
  108.8 4.5 %copy-start.24 = (s32[1,6,100,32]{2,3,1,0:T(8,128)S(1)}, s32[1,6,100,32]{2,3,1,0:T(8,128)}, u32[]{:S(2)}) copy-start(s32[1,6,100,32]{2,3,1,0:T(8,128)} %param.21) | copy-start | bytes 230404
  108.8 4.5 %copy-start.4 = (s32[1,6,1024]{2,0,1:T(1,128)S(1)}, s32[1,6,1024]{2,0,1:T(1,128)}, u32[]{:S(2)}) copy-start(s32[1,6,1024]{2,0,1:T(1,128)} %param.20) | copy-start | bytes 73732
  108.8 10.6 %copy-start.5 = (s32[1,1024]{1,0:T(1,128)S(1)}, s32[1,1024]{1,0:T(1,128)}, u32[]{:S(2)}) copy-start(s32[1,1024]{1,0:T(1,128)} %seg.1) | copy-start | bytes 12292
  117.1 1.1 copy-start
  118.2 1.2 copy-start.3
  142.3 1.1 copy-start.1
  143.5 1.1 copy-start.2
  146.9 58.5 %all-reduce.10.cloned.1.call-start = ((), (), s32[]{:S(2)}) async-start(), calls=%async_computation.1 | async-start | bytes 3145728 | tf_op jit(solution)/shard_map/psum | solution.py:471
  165.7 2.1 copy-start.9
  165.7 2.8 copy-start.18
  168.5 3.2 copy-start.17
  168.5 3.2 copy-start.20
  171.7 6.5 %copy-start.25 = (f32[4,384,1024]{2,1,0:T(8,128)}, f32[4,384,1024]{2,1,0:T(8,128)S(1)}, u32[]{:S(2)}) copy-start(f32[4,384,1024]{2,1,0:T(8,128)S(1)} %fusion.43) | copy-start | bytes 18874372
  178.2 1.6 copy-start.26
  183.7 111.2 %all-reduce.12.cloned.1.call-start = ((), (), s32[]{:S(2)}) async-start(), calls=%async_computation.2 | async-start | bytes 6291456 | tf_op jit(solution)/shard_map/psum | solution.py:464
  205.4 3.7 copy-start.10
  205.4 3.7 copy-start.13
  205.4 3.7 copy-start.21
  211.9 28.9 %copy-start.8 = (f32[1024,768]{1,0:T(8,128)}, f32[1024,768]{1,0:T(8,128)S(1)}, u32[]{:S(2)}) copy-start(f32[1024,768]{1,0:T(8,128)S(1)} %get-tuple-element.44) | copy-start | bytes 9437188
  242.0 1.5 copy-start.14
  244.8 2.2 copy-start.19
  245.1 1.4 copy-start.15
  250.5 1.4 copy-start.7
  276.2 3.5 copy-start.11
  279.6 2.5 copy-start.16
  289.5 3.9 copy-start.12
  384.2 7.9 %copy-start.23 = (bf16[1024,768]{1,0:T(8,128)(2,1)S(1)}, bf16[1024,768]{1,0:T(8,128)(2,1)}, u32[]{:S(2)}) copy-start(bf16[1024,768]{1,0:T(8,128)(2,1)} %get-tuple-element.38) | copy-start | bytes 4718596
Sparse Core Ops, SparseCore 0:
  147.0 18.5 all-reduce.7
  183.8 21.5 all-reduce.9
  250.6 24.4 all-reduce.11

commit v2 on v1

v2 whole, which is shorter than its diff:
```python
import functools

import jax
import jax.numpy as jnp
from jax import lax
from jax.experimental import pallas as pl
from jax.experimental.pallas import tpu as pltpu
from jax.sharding import PartitionSpec as P

F32=jnp.float32; BF=jnp.bfloat16
BIG=1e30
NT=(((1,),(1,)),((),()))
TN=(((0,),(0,)),((),()))
NN=(((1,),(0,)),((),()))
def dot(a,b,dims=NN): return lax.dot_general(a,b,dims,preferred_element_type=F32)
def split3(x):
    a=x.astype(BF); r=x-a.astype(F32); b=r.astype(BF); c=(r-b.astype(F32)).astype(BF)
    return a,b,c
def split2(x):
    a=x.astype(BF); return a,(x-a.astype(F32)).astype(BF)
L=1024
def lane(shape): return lax.broadcasted_iota(jnp.int32,shape,len(shape)-1)
def sub(shape): return lax.broadcasted_iota(jnp.int32,shape,len(shape)-2)

def build_masks(own_row, topT):
    mt=jnp.where(own_row==sub((128,L)),1.0,0.0).astype(BF)
    m=jnp.transpose(mt)
    hi=lax.shift_right_arithmetic(topT,5); bit=lax.shift_left(jnp.int32(1),topT&31)
    words=L//32
    a_iota=sub((words,128))
    w=jnp.zeros((words,128),jnp.int32)
    for t in range(topT.shape[0]):
        w=w|jnp.where(hi[t:t+1]==a_iota,bit[t:t+1],0)
    b_iota=sub((32,128)); ln=lane((32,128))
    extra=(ln>=100)&(ln<103)
    ns=[];ts=[]
    for a in range(words):
        b=(lax.shift_right_logical(jnp.broadcast_to(w[a:a+1],(32,128)),b_iota)&1)
        tmf=b.astype(F32)
        ts.append(tmf)
        ns.append(jnp.where(extra,-1.0,jnp.where(b==1,0.0,-BIG)))
    n=jnp.concatenate(ns,0).astype(BF)
    tm=jnp.transpose(jnp.concatenate(ts,0)).astype(BF)
    return m,mt,n,tm


TQ = 256
TJ = 256
MESH=pl.DeviceIdType.MESH


GN=1;GM=1;SA=1;SN=1
def NOP(p): pass
class Place:
    def __init__(self, nb):
        self.nz=nb//4
        self.b=lax.axis_index("batch"); self.h=lax.axis_index("head")
        self.z=self.b//4; self.r=lax.rem(self.b,4)
        even=lax.rem(self.r,2)==0
        self.rx=jnp.where(even,self.r+1,self.r-1)
        self.ry=jnp.where(self.r<2,self.r+2,self.r-2)
        self.rd=3-self.r
        self.X=(self.z*4+self.rx,self.h); self.Y=(self.z*4+self.ry,self.h)
        self.up=(self.b+4,self.h); self.dn=(self.b-4,self.h); self.twin=(self.b,1-self.h)
    def barrier(self):
        bar=pltpu.get_barrier_semaphore()
        for d in (self.X,self.Y,self.twin):
            pl.semaphore_signal(bar,inc=1,device_id=d,device_id_type=MESH)
        @pl.when(self.z<self.nz-1)
        def _(): pl.semaphore_signal(bar,inc=1,device_id=self.up,device_id_type=MESH)
        @pl.when(self.z>0)
        def _(): pl.semaphore_signal(bar,inc=1,device_id=self.dn,device_id_type=MESH)
        lines=jnp.where(self.z<self.nz-1,1,0)+jnp.where(self.z>0,1,0)
        pl.semaphore_wait(bar,3+lines)

def rc(src,dst,ss,rs,dev):
    return pltpu.make_async_remote_copy(src_ref=src,dst_ref=dst,send_sem=ss,recv_sem=rs,device_id=dev,device_id_type=MESH)

class Gather:
    def __init__(self, pc, g, ss, rs):
        self.pc=pc; self.g=g; self.ss=ss; self.rs=rs; self.n=2*(pc.nz-1)
    def cz(self,p,zz,k,dev):
        s=self.g.at[p,zz,self.pc.r]
        return rc(s,s,self.ss.at[p,k],self.rs.at[p,k],dev)
    def z0(self,p):
        c=self.pc
        @pl.when(c.z<c.nz-1)
        def _(): self.cz(p,c.z,0,c.up).start()
        @pl.when(c.z>0)
        def _(): self.cz(p,c.z,1,c.dn).start()
    def zk(self,p,d):
        c=self.pc
        @pl.when(c.z-d>=0)
        def _():
            self.cz(p,c.z-d,2*(d-1),c.up).wait_recv()
        if d<c.nz-1:
            @pl.when((c.z-d>=0)&(c.z<c.nz-1))
            def _(): self.cz(p,c.z-d,2*d,c.up).start()
        @pl.when(c.z+d<c.nz)
        def _():
            self.cz(p,c.z+d,2*(d-1)+1,c.dn).wait_recv()
        if d<c.nz-1:
            @pl.when((c.z+d<c.nz)&(c.z>0))
            def _(): self.cz(p,c.z+d,2*d+1,c.dn).start()
    def cb(self,p,r,k,dev):
        s=self.g.at[p,:,r]
        return rc(s,s,self.ss.at[p,self.n+k],self.rs.at[p,self.n+k],dev)
    def ch(self,p,r,lo,k,dev):
        h=self.pc.nz//2
        s=self.g.at[p,pl.ds(0,h),r] if lo else self.g.at[p,pl.ds(h,self.pc.nz-h),r]
        return rc(s,s,self.ss.at[p,self.n+k],self.rs.at[p,self.n+k],dev)
    def x0(self,p):
        c=self.pc
        self.cb(p,c.r,0,c.X).start(); self.cb(p,c.r,1,c.Y).start()
    def x1(self,p):
        c=self.pc
        self.cb(p,c.rx,0,c.X).wait_recv()
        self.ch(p,c.rx,True,2,c.Y).start()
        self.cb(p,c.ry,1,c.Y).wait_recv()
        self.ch(p,c.ry,False,3,c.X).start()
    def x2(self,p):
        c=self.pc
        self.ch(p,c.rd,True,2,c.Y).wait_recv()
        self.ch(p,c.rd,False,3,c.X).wait_recv()
    def drain(self,p):
        c=self.pc
        for d in range(c.nz-1):
            @pl.when((c.z-d>=0)&(c.z<c.nz-1))
            def _(): self.cz(p,c.z-d,2*d,c.up).wait_send()
            @pl.when((c.z+d<c.nz)&(c.z>0))
            def _(): self.cz(p,c.z+d,2*d+1,c.dn).wait_send()
        self.cb(p,c.r,0,c.X).wait_send(); self.cb(p,c.r,1,c.Y).wait_send()
        self.ch(p,c.rx,True,2,c.Y).wait_send(); self.ch(p,c.ry,False,3,c.X).wait_send()
    def steps(self):
        nz=self.pc.nz
        def last(p):
            self.zk(p,nz-1); self.x0(p)
        return [self.z0]+[functools.partial(lambda d,p:self.zk(p,d),d) for d in range(1,nz-1)]+[last]+[NOP]*GN+[self.x1]+[NOP]*GM+[self.x2]

class Scatter:
    def __init__(self, pc, g, d, rx, ry, ru, rd, ss, rs):
        self.pc=pc;self.g=g;self.d=d;self.bx=rx;self.by=ry;self.bu=ru;self.bd=rd;self.ss=ss;self.rs=rs
        self.h=pc.nz//2
    def half(self,p,r,lo):
        h=self.h; n=self.pc.nz
        return (self.g.at[p,pl.ds(0,h),r],self.d.at[p,pl.ds(0,h)]) if lo else (self.g.at[p,pl.ds(h,n-h),r],self.d.at[p,pl.ds(h,n-h)])
    def c0(self,p,lo):
        s,t=self.half(p,self.pc.rd,lo); k=0 if lo else 1
        return rc(s,t,self.ss.at[p,k],self.rs.at[p,k],self.pc.X if lo else self.pc.Y)
    def c1(self,p,x):
        c=self.pc
        return rc(self.g.at[p,:,c.rx if x else c.ry],(self.bx if x else self.by).at[p],self.ss.at[p,2 if x else 3],self.rs.at[p,2 if x else 3],c.X if x else c.Y)
    def cu(self,p,zz,up):
        c=self.pc; k=4+zz if up else 4+c.nz+zz
        return rc(self.g.at[p,zz,c.r],(self.bu if up else self.bd).at[p,zz],self.ss.at[p,k],self.rs.at[p,k],c.up if up else c.dn)
    def add(self,dst,*srcs):
        v=dst[...].astype(F32)
        for s in srcs: v=v+s[...].astype(F32)
        dst[...]=v.astype(BF)
    def s0(self,p):
        self.c0(p,True).start(); self.c0(p,False).start()
    def s1(self,p):
        c=self.pc;h=self.h;n=c.nz
        self.c0(p,True).wait_recv()
        self.add(self.g.at[p,pl.ds(0,h),c.ry],self.d.at[p,pl.ds(0,h)])
        self.c1(p,False).start()
        self.c0(p,False).wait_recv()
        self.add(self.g.at[p,pl.ds(h,n-h),c.rx],self.d.at[p,pl.ds(h,n-h)])
        self.c1(p,True).start()
    def s2(self,p):
        c=self.pc
        self.c1(p,True).wait_recv(); self.c1(p,False).wait_recv()
        self.add(self.g.at[p,:,c.r],self.bx.at[p],self.by.at[p])
        self.zk(p,0)
    def zk(self,p,k):
        c=self.pc; nz=c.nz
        @pl.when(c.z==k)
        def _():
            for zz in range(nz-1,k,-1):
                if k>0:
                    self.cu(p,zz,True).wait_recv()
                    self.add(self.g.at[p,zz,c.r],self.bu.at[p,zz])
                self.cu(p,zz,True).start()
        @pl.when(c.z==nz-1-k)
        def _():
            for zz in range(0,nz-1-k):
                if k>0:
                    self.cu(p,zz,False).wait_recv()
                    self.add(self.g.at[p,zz,c.r],self.bd.at[p,zz])
                self.cu(p,zz,False).start()
    def fin(self,p,out):
        c=self.pc
        out[p]=self.g[p,c.z,c.r].astype(F32)
        @pl.when(c.z>0)
        def _():
            self.cu(p,c.z,True).wait_recv()
            out[p]+=self.bu[p,c.z].astype(F32)
        @pl.when(c.z<c.nz-1)
        def _():
            self.cu(p,c.z,False).wait_recv()
            out[p]+=self.bd[p,c.z].astype(F32)
    def drain(self,p):
        c=self.pc; nz=c.nz
        self.c0(p,True).wait_send(); self.c0(p,False).wait_send()
        self.c1(p,True).wait_send(); self.c1(p,False).wait_send()
        for zz in range(nz):
            @pl.when(zz>c.z)
            def _(): self.cu(p,zz,True).wait_send()
            @pl.when(zz<c.z)
            def _(): self.cu(p,zz,False).wait_send()
    def steps(self,out):
        nz=self.pc.nz
        return [self.s0]+[NOP]*SA+[self.s1]+[NOP]*SN+[self.s2]+[functools.partial(lambda k,p:self.zk(p,k),k) for k in range(1,nz-1)]+[lambda p:self.fin(p,out)]


EPS = 1e-5
RT = 256


def pick(static, cond, body):
    if isinstance(cond, (bool, int)):
        if cond:
            body()
    else:
        pl.when(cond)(body)


def norm_rows(values):
    mean = jnp.mean(values, axis=1, keepdims=True)
    centred = values - mean
    inverse = lax.rsqrt(jnp.mean(centred * centred, axis=1, keepdims=True) + EPS)
    return centred * inverse, inverse


def gelu_both(u):
    c = 0.7978845608028654
    u2 = u * u
    t = jnp.tanh(c * u * (1.0 + 0.044715 * u2))
    half = 0.5 + 0.5 * t
    act = u * half
    grad = half + (0.5 * c) * u * (1.0 - t * t) * (1.0 + (3 * 0.044715) * u2)
    return act, grad


def flat(ref, p):
    v = ref[p]
    return v.reshape(-1, v.shape[-1])


def tiles(n):
    return lambda f: pl.loop(0, n)(f)


def rows_of(i, n=RT):
    return pl.ds(pl.multiple_of(i * n, n), n)


def twin_copy(pc, src, dst, ss, rs):
    return rc(src, dst, ss, rs, pc.twin)


def fwd_head(p, h, qkv, mb, mt_s, n_s, tm_s, seg, qaug, kaug, att, ex, prob_o):
    odd = h == 1
    hh = 2 * p + h
    q = qkv[p, :, 0:128]
    k = qkv[p, :, 128:256]
    v = qkv[p, :, 256:384]
    ln = lane((L, 128))
    mine = (ln >= 64) if odd else (ln < 64)
    lc = lane((128, 128))
    minec = (lc >= 64) if odd else (lc < 64)
    zero = jnp.zeros((), BF)
    qm = jnp.where(mine, q, zero)
    vaug = jnp.where(mine, v, jnp.ones((), BF))
    mt = mt_s[hh]
    cnt = jnp.maximum(jnp.sum(mt.astype(F32), axis=1, keepdims=True), 1.0)
    cen = (dot(mt, qm) / cnt).astype(BF)
    cs = (cen.astype(F32) * 0.125).astype(BF)
    s = dot(cs, k, NT)
    cm = lax.rem(sub((128, 1)), jnp.int32(10))
    s = jnp.where(seg[...] == cm, s, -BIG)
    mx = jnp.max(s, axis=1, keepdims=True)
    e = jnp.exp(s - mx)
    prob = e / jnp.sum(e, axis=1, keepdims=True)
    tmf = tm_s[hh].astype(F32)
    mass = jnp.sum(prob * tmf, axis=1, keepdims=True)
    prob_o[hh] = prob.astype(BF)
    rest = dot((prob * (1.0 - tmf)).astype(BF), v)
    rh, rl = split2(jnp.where(minec, rest, jnp.broadcast_to(mass, (128, 128))))
    rr = jnp.concatenate([rh, rl], 1)
    qaug[:, :128] = (qm.astype(F32) * 0.125).astype(BF)
    qaug[:, 128:] = mb[hh]
    kaug[:, :128] = k
    kaug[:, 128:] = n_s[hh]
    lt = lane((TQ, 128))
    minet = (lt >= 64) if odd else (lt < 64)
    cols = pl.ds(pl.multiple_of(p * 128, 128), 128)
    for t in range(L // TQ):
        sl = pl.ds(t * TQ, TQ)
        sc = dot(qaug[sl, :], kaug[...], NT)
        mm = jnp.max(sc, axis=1, keepdims=True)
        pr = jnp.exp(sc - mm).astype(BF)
        o = dot(pr, vaug)
        mt_ = qaug[sl, 128:]
        ee = dot(mt_, rr)
        ee = ee[:, :128] + ee[:, 128:]
        osw = pltpu.roll(o, 64, 1)
        esw = pltpu.roll(ee, 64, 1)
        exact = o / osw
        a = exact * esw + ee
        tot = jnp.where(minet, osw, o)
        ms = jnp.where(minet, esw, ee)
        lse = mm + jnp.log(tot) - jnp.log(jnp.maximum(ms, 1e-37))
        h3, m3, l3 = split3(lse)
        mb[hh, sl, :] = jnp.where(lt == 100, h3.astype(F32), jnp.where(lt == 101, m3.astype(F32), jnp.where(lt == 102, l3.astype(F32), mt_.astype(F32)))).astype(BF)
        if odd:
            att[sl, cols] = jnp.where(lt < 64, att[sl, cols], a.astype(BF))
            ex[sl, cols] = jnp.where(lt < 64, ex[sl, cols], exact.astype(BF))
        else:
            att[sl, cols] = a.astype(BF)
            ex[sl, cols] = exact.astype(BF)


N1OUT = ("gr", "n1", "qkv", "att", "ex", "mb", "mt", "ns", "tm", "prob", "hid", "n2", "act", "dg")


def k1_shapes(w_shape):
    H = 6
    f = lambda *s: (s, F32)
    b = lambda *s: (s, BF)
    return {
        "gr": f(8, 768), "n1": b(L, 768), "qkv": b(3, L, 384), "att": b(L, 384), "ex": b(L, 384),
        "mb": b(H, L, 128), "mt": b(H, 128, L), "ns": b(H, L, 128), "tm": b(H, 128, L), "prob": b(H, 128, L),
        "hid": f(L, 768), "n2": b(L, 768), "act": b(4, L, 384), "dg": b(4, L, 384),
    }


def k1_body(nb, custom, *refs):
    refs = list(refs)
    take = lambda n: [refs.pop(0) for _ in range(n)]
    x, w, gw, seg, cl, tt = take(6)
    outs = dict(zip(N1OUT, take(len(N1OUT))))
    (y,) = take(1)
    if custom:
        (wo,) = take(1)
    s = dict(zip(N1OUT, take(len(N1OUT))))
    qaug, kaug, eb, er, fb, fr, osem, es, ers, fs, frs = take(11)
    pc = Place(nb)
    pc.barrier()
    if custom:
        g, gg, ss, rs, gss, grs, wsem = take(7)
        G = Gather(pc, g, ss, rs)
        Gg = Gather(pc, gg, gss, grs)
        g[:, pc.z, pc.r] = w[...]
        gg[0, pc.z, pc.r] = gw[...]
        steps, gsteps = G.steps(), Gg.steps()
        NP = 12

        def tick(t):
            for i in range(len(steps) - 1, -1, -1):
                p = t - i
                ok = (p >= 0 and p < NP) if isinstance(t, int) else ((p >= 0) & (p < NP))
                pick(None, ok, lambda i=i, p=p: steps[i](p))
                if isinstance(t, int) and t == i:
                    gsteps[i](0)
        last = NP - 1 + len(steps) - 1
        first = len(steps) - 1
    else:
        g, gg = w, gw
        tick = lambda t: None
        last, first = 18, 7
    copies = []

    def out(name):
        c = pltpu.make_async_copy(s[name], outs[name], osem.at[N1OUT.index(name)])
        c.start()
        copies.append(c)

    hid, n1, n2, qkv, att, ex = s["hid"], s["n1"], s["n2"], s["qkv"], s["att"], s["ex"]
    tick(0)

    @tiles(L // RT)
    def _(i):
        hid[rows_of(i), :] = norm_rows(x[rows_of(i), :].astype(F32))[0]

    tick(1)

    def mask(h):
        a, b, c, d = build_masks(cl[h], tt[h])
        s["mb"][h], s["mt"][h], s["ns"][h], s["tm"][h] = a, b, c, d

    pl.loop(0, 2)(mask)
    tick(2)
    pl.loop(2, 4)(mask)
    tick(3)
    pl.loop(4, 6)(mask)
    for n in ("mt", "ns", "tm"):
        out(n)
    for t in range(4, first + 1):
        tick(t)
    gains = gg[0].reshape(768, 128) if custom else gg[...]
    s["gr"][...] = jnp.transpose(gains.astype(F32))[0:8]
    out("gr")

    @tiles(L // RT)
    def _(i):
        n1[rows_of(i), :] = (hid[rows_of(i), :] * s["gr"][0:1, :]).astype(BF)

    out("n1")

    @pl.loop(0, 3)
    def _(p):
        @tiles(L // RT)
        def _(i):
            qkv[p, rows_of(i), :] = dot(n1[rows_of(i), :], flat(g, p)).astype(BF)
        for h in range(2):
            tick(first + 1 + 3 * p + h)
            fwd_head(p, h, qkv, s["mb"], s["mt"], s["ns"], s["tm"], seg, qaug, kaug, att, ex, s["prob"])
        tick(first + 3 + 3 * p)

    for n in ("qkv", "att", "ex", "mb", "prob"):
        out(n)

    def send1(i):
        return twin_copy(pc, eb.at[rows_of(i)], er.at[rows_of(i)], es.at[i], ers.at[i])

    @tiles(L // RT)
    def _(i):
        eb[rows_of(i), :] = dot(att[rows_of(i), :], flat(g, 3), NT).astype(BF)
        send1(i).start()

    t = first + 10
    if t <= last:
        tick(t)

    @tiles(L // RT)
    def _(i):
        r = rows_of(i)
        send1(i).wait_recv()
        hv = x[r, :].astype(F32) + (eb[r, :].astype(F32) + er[r, :].astype(F32))
        hid[r, :] = hv
        n2[r, :] = (norm_rows(hv)[0] * s["gr"][1:2, :]).astype(BF)

    out("hid")
    out("n2")

    def up(q):
        @tiles(L // RT)
        def _(i):
            a, d = gelu_both(dot(n2[rows_of(i), :], flat(g, 4 + q)))
            s["act"][q, rows_of(i), :] = a.astype(BF)
            s["dg"][q, rows_of(i), :] = d.astype(BF)

    pl.loop(0, 2)(up)
    for t in range(first + 11, last + 1):
        tick(t)
    if custom:
        cw = pltpu.make_async_copy(g, wo, wsem)
        cw.start()
        copies.append(cw)
    pl.loop(2, 4)(up)
    out("act")
    out("dg")
    half = L // 2 // RT

    def part(i):
        acc = dot(s["act"][0, rows_of(i), :], flat(g, 8), NT)
        for q in range(1, 4):
            acc += dot(s["act"][q, rows_of(i), :], flat(g, 8 + q), NT)
        return acc

    def send2(i):
        return twin_copy(pc, fb.at[rows_of(i)], fr.at[rows_of(i)], fs.at[i], frs.at[i])

    @tiles(half)
    def _(i):
        fb[rows_of(i), :] = part((1 - pc.h) * half + i).astype(BF)
        send2(i).start()

    @tiles(half)
    def _(i):
        acc = part(pc.h * half + i).astype(BF).astype(F32)
        send2(i).wait_recv()
        y[rows_of(i), :] = (hid[rows_of(pc.h * half + i), :] + (acc + fr[rows_of(i), :].astype(F32))).astype(BF)

    @tiles(L // RT)
    def _(i):
        send1(i).wait_send()

    @tiles(half)
    def _(i):
        send2(i).wait_send()

    if custom:
        @pl.loop(0, 12)
        def _(p):
            G.drain(p)
        Gg.drain(0)
    for c in copies:
        c.wait()


def vm(shape_dtype):
    return pltpu.VMEM(*shape_dtype)


def forward(nb, custom, x, w, gw, seg, cl, tt):
    shapes = k1_shapes(w.shape)
    sds = lambda sd: jax.ShapeDtypeStruct(*sd)
    V = pl.BlockSpec(memory_space=pltpu.VMEM)
    A = pl.BlockSpec(memory_space=pl.ANY)
    nz = nb // 4
    dma = pltpu.SemaphoreType.DMA
    out_shape = [sds(shapes[n]) for n in N1OUT] + [jax.ShapeDtypeStruct((L // 2, 768), BF)]
    out_specs = [A] * len(N1OUT) + [V]
    scratch = [vm(shapes[n]) for n in N1OUT] + [
        pltpu.VMEM((L, 256), BF), pltpu.VMEM((L, 256), BF), pltpu.VMEM((L, 768), BF), pltpu.VMEM((L, 768), BF),
        pltpu.VMEM((L // 2, 768), BF), pltpu.VMEM((L // 2, 768), BF), dma((len(N1OUT),)), dma((4,)), dma((4,)), dma((2,)), dma((2,))]
    if custom:
        R = w.shape[1]
        ns = 2 * (nz - 1) + 4
        out_shape.append(jax.ShapeDtypeStruct((12, nz, 4, R, 384), BF))
        out_specs.append(A)
        scratch += [pltpu.VMEM((12, nz, 4, R, 384), BF), pltpu.VMEM((1, nz, 4, R, 128), BF), dma((12, ns)), dma((12, ns)), dma((1, ns)), dma((1, ns)), dma]
    r = pl.pallas_call(
        functools.partial(k1_body, nb, custom),
        out_shape=out_shape, in_specs=[V] * 6, out_specs=out_specs, scratch_shapes=scratch,
        compiler_params=pltpu.CompilerParams(collective_id=0, has_side_effects=True, vmem_limit_bytes=62 << 20),
    )(x, w, gw, seg, cl, tt)
    d = dict(zip(N1OUT, r))
    return d, r[len(N1OUT)], (r[-1] if custom else w)


def bwd_head(p, h, s, qaug, kaug, gaug, vaug, dq_o, dk_o, dv_o, dqt):
    qkv, g, ex = s["qkv"], s["gatt"], s["ex"]
    hh = 2 * p + h
    cols = pl.ds(pl.multiple_of(p * 128, 128), 128)
    qv = qkv[p, :, 0:128]
    kv = qkv[p, :, 128:256]
    vv = qkv[p, :, 256:384]
    gv = g[:, cols]
    ln = lane((L, 128))
    zero = jnp.zeros((), BF)
    lc = lane((128, 128))
    kT = jnp.transpose(kv)
    prod = gv.astype(F32) * ex[:, cols].astype(F32)
    mine = (ln >= 64) if h else (ln < 64)
    minec = (lc >= 64) if h else (lc < 64)
    o = 0 if h else 64
    r = jnp.sum(jnp.where(mine, prod, 0.0), axis=1, keepdims=True)
    h3, m3, l3 = split3(r)
    gm = jnp.where(mine, gv, zero)
    ga = jnp.where(ln == o, h3.astype(F32), jnp.where(ln == o + 1, m3.astype(F32), jnp.where(ln == o + 2, l3.astype(F32), gm.astype(F32)))).astype(BF)
    gaug[...] = ga
    vaug[...] = jnp.where(mine, vv, jnp.where((ln >= o) & (ln < o + 3), jnp.full((), -1.0, BF), zero))
    qm = jnp.where(mine, qv, zero)
    qs = (qm.astype(F32) * 0.125).astype(BF)
    qaug[:, :128] = qs
    qaug[:, 128:] = s["mb"][hh]
    kaug[:, :128] = kv
    kaug[:, 128:] = s["ns"][hh]
    mt = s["mt"][hh]
    prob = s["prob"][hh].astype(F32)
    cnt = jnp.maximum(jnp.sum(mt.astype(F32), axis=1, keepdims=True), 1.0)
    cen = (dot(mt, qm) / cnt).astype(BF)
    cs = (cen.astype(F32) * 0.125).astype(BF)
    gr = dot(mt, ga)
    gmass = jnp.sum(jnp.where((lc >= o) & (lc < o + 3), gr, 0.0), axis=1, keepdims=True)
    grest = jnp.where(minec, gr, 0.0).astype(BF)
    top = s["tm"][hh].astype(F32) > 0.5
    gp = jnp.where(top, gmass, dot(grest, vv, NT))
    gs = (prob * (gp - jnp.sum(prob * gp, axis=1, keepdims=True))).astype(BF)
    rw = jnp.where(top, 0.0, prob).astype(BF)
    gcen = dot(gs, jnp.where(mine, kv, zero)) / cnt
    gh, gl = split2(gcen)
    gg = jnp.concatenate([gh, gl], 1)
    gsT = jnp.transpose(gs)
    rwT = jnp.transpose(rw)
    kTh = kT[64 * h:64 * h + 64]
    for t in range(L // TJ):
        sl = pl.ds(t * TJ, TJ)
        st = dot(kaug[sl, :], qaug[...], NT)
        pr = jnp.exp(st)
        dp = dot(vaug[sl, :], gaug[...], NT)
        ds = (pr * dp).astype(BF)
        dv = dot(pr.astype(BF), gm) + dot(rwT[t * TJ:(t + 1) * TJ], grest)
        dk = dot(ds, qs) + dot(gsT[t * TJ:(t + 1) * TJ], cs)
        if h == 0:
            dv_o[sl, :] = dv
            dk_o[sl, :] = dk
        else:
            dv_o[sl, :] += dv
            dk_o[sl, :] += dk
        dqp = dot(kTh[:, t * TJ:(t + 1) * TJ], ds)
        if t == 0:
            dqt[64 * h:64 * h + 64, :] = dqp
        else:
            dqt[64 * h:64 * h + 64, :] += dqp
    dd = dot(jnp.where(ln < 100, s["mb"][hh], zero), gg)
    dd = dd[:, :128] + dd[:, 128:]
    if h == 0:
        dq_o[...] = dd
    else:
        dq_o[...] += dd


N2IN = ("act", "dg", "n2", "hid", "n1", "att", "qkv", "ex", "mb", "mt", "ns", "tm", "prob")


def k2_body(nb, custom, *refs):
    refs = list(refs)
    take = lambda n: [refs.pop(0) for _ in range(n)]
    ct, x, gr, w = take(4)
    ins = dict(zip(N2IN, take(len(N2IN))))
    tg, out_s, out_g = take(3)
    s = dict(zip(N2IN, take(len(N2IN))))
    names = ("aT", "ghs", "eb", "er", "gatt", "dqkv", "qaug", "kaug", "gaug", "vaug", "dqs", "dks", "dvs", "dqt", "gacc", "vb", "vr", "xs", "e3", "wg")
    b = dict(zip(names, take(len(names))))
    isem, wsem, xsem, es, ers, vs, vrs = take(7)
    aT, ghs, eb, er, gacc, wg = b["aT"], b["ghs"], b["eb"], b["er"], b["gacc"], b["wg"]
    s["gatt"] = b["gatt"]
    pc = Place(nb)
    loads = {n: pltpu.make_async_copy(ins[n], s[n], isem.at[i]) for i, n in enumerate(N2IN)}
    wl = {}
    for i, (k, a, e) in enumerate((("down", 8, 12), ("up", 4, 8), ("rest", 0, 4))):
        wl[k] = pltpu.make_async_copy(w.at[a:e], wg.at[a:e], wsem.at[i])
    half = L // 2
    xl = pltpu.make_async_copy(x.at[pl.ds(pl.multiple_of(pc.h * half, half), half)], b["xs"], xsem)
    wl["down"].start()
    for n in ("act", "dg"):
        loads[n].start()
    wl["up"].start()
    for n in ("n2", "hid", "att"):
        loads[n].start()
    wl["rest"].start()
    for n in N2IN:
        if n not in ("act", "dg", "n2", "hid", "att"):
            loads[n].start()
    xl.start()
    pc.barrier()
    if custom:
        gbuf, land, gland = refs[0], refs[1:6], refs[6:11]
        ss, rs, gss, grs = refs[11:15]
        S = Scatter(pc, wg, *land, ss, rs)
        Sg = Scatter(pc, gbuf, *gland, gss, grs)
        steps, gsteps = S.steps(out_s), Sg.steps(out_g)
        starts = list(range(9)) + [11, 14, 17]
        order = [8, 9, 10, 11, 4, 5, 6, 7, 3, 0, 1, 2]

        def tick(t):
            for i in range(len(steps) - 1, -1, -1):
                u = t - i
                if isinstance(u, int):
                    if u in starts:
                        steps[i](order[starts.index(u)])
                else:
                    ok = (u >= 0) & ((u <= 8) | ((u >= 11) & (u <= 17) & (lax.rem(u + 10, 3) == 0)))
                    part = jnp.where(u < 4, u + 8, jnp.where(u < 8, u, jnp.where(u == 8, 3, (u - 11) // 3)))
                    pl.when(ok)(lambda i=i, part=part: steps[i](part))
        nsteps = len(steps)
    else:
        tick = lambda t: None

    def put(p, left, right):
        v = dot(left, right).astype(BF)
        wg[p] = v.reshape(wg.shape[1:])

    def transpose_into(src):
        for i in range(L // RT):
            aT[:, i * RT:(i + 1) * RT] = jnp.transpose(src[i * RT:(i + 1) * RT, :])

    transpose_into(ct)
    wl["down"].wait()
    loads["act"].wait()
    loads["dg"].wait()
    act, dg, hid, n2 = s["act"], s["dg"], s["hid"], s["n2"]

    @pl.loop(0, 4)
    def _(q):
        @tiles(L // RT)
        def _(i):
            ga = dot(ct[rows_of(i), :], flat(wg, 8 + q))
            dg[q, rows_of(i), :] = (ga * dg[q, rows_of(i), :].astype(F32)).astype(BF)
        put(8 + q, aT[...], act[q])
        tick(q)

    wl["up"].wait()
    loads["n2"].wait()

    def send(i):
        return twin_copy(pc, eb.at[rows_of(i)], er.at[rows_of(i)], es.at[i], ers.at[i])

    @tiles(L // RT)
    def _(i):
        acc = dot(dg[0, rows_of(i), :], flat(wg, 4), NT)
        for q in range(1, 4):
            acc += dot(dg[q, rows_of(i), :], flat(wg, 4 + q), NT)
        eb[rows_of(i), :] = acc.astype(BF)
        send(i).start()

    transpose_into(n2)

    @pl.loop(0, 4)
    def _(q):
        put(4 + q, aT[...], dg[q])
        tick(4 + q)

    loads["hid"].wait()
    gacc[...] = jnp.zeros_like(gacc)
    nh = half // RT
    gat = n2

    @tiles(L // RT)
    def _(i):
        r = rows_of(i)
        send(i).wait_recv()
        gn = eb[r, :].astype(F32) + er[r, :].astype(F32)
        n, inv = norm_rows(hid[r, :])
        gacc[1:2, :] += jnp.sum(gn * n, axis=0, keepdims=True)
        a = gn * gr[1:2, :]
        back = (a - jnp.mean(a, axis=1, keepdims=True) - n * jnp.mean(a * n, axis=1, keepdims=True)) * inv
        gh = ct[r, :].astype(F32) + back
        gat[r, :] = gh.astype(BF)

        @pl.when((i >= pc.h * nh) & (i < pc.h * nh + nh))
        def _():
            ghs[rows_of(i - pc.h * nh), :] = gh

    wl["rest"].wait()
    loads["att"].wait()

    @tiles(L // RT)
    def _(i):
        b["gatt"][rows_of(i), :] = dot(gat[rows_of(i), :], flat(wg, 3)).astype(BF)

    transpose_into(gat)
    put(3, aT[...], s["att"][...])
    tick(8)
    loads["n1"].wait()
    transpose_into(s["n1"])
    for n in ("qkv", "ex", "mb", "mt", "ns", "tm", "prob"):
        loads[n].wait()
    nacc = hid
    dqkv = b["dqkv"]

    @pl.loop(0, 3)
    def _(p):
        for h in range(2):
            bwd_head(p, h, s, b["qaug"], b["kaug"], b["gaug"], b["vaug"], b["dqs"], b["dks"], b["dvs"], b["dqt"])
            if h == 0:
                tick(9 + 3 * p)
        dqkv[:, 0:128] = ((b["dqs"][...] + jnp.transpose(b["dqt"][...])) * 0.125).astype(BF)
        dqkv[:, 128:256] = b["dks"][...].astype(BF)
        dqkv[:, 256:384] = b["dvs"][...].astype(BF)
        tick(10 + 3 * p)

        @tiles(L // RT)
        def _(i):
            v = dot(dqkv[rows_of(i), :], flat(wg, p), NT)

            @pl.when(p == 0)
            def _():
                nacc[rows_of(i), :] = v

            @pl.when(p > 0)
            def _():
                nacc[rows_of(i), :] += v
        put(p, aT[...], dqkv[...])
        tick(11 + 3 * p)

    @tiles(L // RT)
    def _(i):
        send(i).wait_send()

    def send3(i):
        return twin_copy(pc, eb.at[rows_of(i)], b["e3"].at[rows_of(i)], es.at[4 + i], ers.at[4 + i])

    @tiles(nh)
    def _(i):
        eb[rows_of(i), :] = nacc[rows_of((1 - pc.h) * nh + i), :].astype(BF)
        send3(i).start()

    tick(18)
    xl.wait()

    @tiles(nh)
    def _(i):
        r = rows_of(i)
        send3(i).wait_recv()
        gn = nacc[rows_of(pc.h * nh + i), :].astype(BF).astype(F32) + b["e3"][r, :].astype(F32)
        n, inv = norm_rows(b["xs"][r, :].astype(F32))
        gacc[0:1, :] += jnp.sum(gn * n, axis=0, keepdims=True)
        a = gn * gr[0:1, :]
        back = (a - jnp.mean(a, axis=1, keepdims=True) - n * jnp.mean(a * n, axis=1, keepdims=True)) * inv
        tg[r, :] = ghs[r, :] + back

    b["vb"][...] = gacc[...]
    cv = twin_copy(pc, b["vb"], b["vr"], vs, vrs)
    cv.start()
    tick(19)
    cv.wait()
    one = gacc[0:1, :] + b["vr"][0:1, :]
    both = jnp.where(sub((8, 768)) == 0, jnp.broadcast_to(one, (8, 768)), gacc[...])
    if custom:
        wide = jnp.concatenate([both, jnp.zeros((120, 768), F32)], 0)
        gbuf[0] = jnp.transpose(wide).astype(BF).reshape(gbuf.shape[1:])
        for t in range(20, max(17, 20) + nsteps):
            tick(t)
            gsteps[t - 20](0)

        @pl.loop(0, 12)
        def _(p):
            S.drain(p)
        Sg.drain(0)
    else:
        c = pltpu.make_async_copy(wg, out_s, xsem)
        c.start()
        out_g[...] = both
        c.wait()

    @tiles(nh)
    def _(i):
        send3(i).wait_send()


def backward(nb, custom, ct, x, w, d):
    V = pl.BlockSpec(memory_space=pltpu.VMEM)
    A = pl.BlockSpec(memory_space=pl.ANY)
    nz = nb // 4
    dma = pltpu.SemaphoreType.DMA
    shapes = k1_shapes(None)
    out_shape = [jax.ShapeDtypeStruct((L // 2, 768), F32)]
    if custom:
        R = w.shape[3]
        out_shape += [jax.ShapeDtypeStruct((12, R, 384), F32), jax.ShapeDtypeStruct((1, R, 128), F32)]
        out_specs = [V, V, V]
    else:
        out_shape += [jax.ShapeDtypeStruct(w.shape, BF), jax.ShapeDtypeStruct((8, 768), F32)]
        out_specs = [V, A, V]
    vb = lambda *sh: pltpu.VMEM(sh, BF)
    vf = lambda *sh: pltpu.VMEM(sh, F32)
    scratch = [vm(shapes[n]) for n in N2IN] + [
        vb(768, L), vf(L // 2, 768), vb(L, 768), vb(L, 768), vb(L, 384), vb(L, 384), vb(L, 256), vb(L, 256), vb(L, 128), vb(L, 128),
        vf(L, 128), vf(L, 128), vf(L, 128), vf(128, L), vf(8, 768), vf(8, 768), vf(8, 768), vb(L // 2, 768), vb(L // 2, 768), pltpu.VMEM(w.shape, BF),
        dma((len(N2IN),)), dma((3,)), dma, dma((6,)), dma((6,)), dma, dma]
    if custom:
        ns = 4 + 2 * nz
        scratch += [vb(1, nz, 4, R, 128)] + [vb(12, nz, R, 384)] * 5 + [vb(1, nz, R, 128)] * 5 + [dma((12, ns)), dma((12, ns)), dma((1, ns)), dma((1, ns))]
    return pl.pallas_call(
        functools.partial(k2_body, nb, custom),
        out_shape=out_shape, in_specs=[V, A, V, A] + [A] * len(N2IN), out_specs=out_specs, scratch_shapes=scratch,
        compiler_params=pltpu.CompilerParams(collective_id=1, has_side_effects=True, vmem_limit_bytes=int(63.5 * (1 << 20))),
    )(ct, x, d["gr"], w, *[d[n] for n in N2IN])


def pack(q, o, u, d):
    R = q.shape[0]
    qp = q.reshape(R, 3, 3, 128).transpose(2, 0, 1, 3).reshape(3, R, 384)
    up = u.reshape(R, 4, 384).transpose(1, 0, 2)
    dn = d.T.reshape(R, 4, 384).transpose(1, 0, 2)
    return jnp.concatenate([qp, o.T[None], up, dn], 0)


def on_device(tokens, attn_gain, qkv_weight, out_weight, ffn_gain, up_weight, down_weight, cotangent, segment, cluster, top_keys):
    nb = lax.axis_size("batch")
    w = pack(qkv_weight, out_weight, up_weight, down_weight)
    R = w.shape[1]
    gw = jnp.pad(jnp.stack([attn_gain, ffn_gain], 1), ((0, 0), (0, 126)))
    custom = R % 16 == 0 and nb % 4 == 0
    if not custom:
        w = lax.all_gather(w, "batch", axis=1, tiled=True)
        gw = lax.all_gather(gw, "batch", axis=0, tiled=True)
    tk = top_keys[0]
    tt = jnp.pad(tk.transpose(0, 2, 1), ((0, 0), (0, 0), (0, 128 - tk.shape[1])), constant_values=-1)
    x, ct = tokens[0], cotangent[0]
    d, y, W = forward(nb, custom, x, w, gw, segment, cluster[0][:, None, :], tt)
    tg, S, gg = backward(nb, custom, ct, x, W, d)
    if custom:
        g1, g2 = gg[0, :, 0], gg[0, :, 1]
    else:
        S = lax.psum_scatter(S.astype(F32), "batch", scatter_dimension=1, tiled=True)
        g = lax.psum_scatter(gg, "batch", scatter_dimension=1, tiled=True)
        g1, g2 = g[0], g[1]
    cat = lambda a: a.transpose(1, 0, 2).reshape(R, -1)
    qg = S[0:3].reshape(3, R, 3, 128).transpose(1, 2, 0, 3).reshape(R, 3, 384)
    return y[None], tg[None], g1, qg, S[3].T, g2, cat(S[4:8]), cat(S[8:12]).T


def solution(mesh):
    in_specs = (P("batch", None, None), P("batch"), P("batch", None, "head"), P("head", "batch"), P("batch"), P("batch", "head"), P("head", "batch"), P("batch", None, None), P("batch", None), P("batch", "head", None), P("batch", "head", None, None))
    out_specs = (P("batch", "head", None), P("batch", "head", None), P("batch"), P("batch", None, "head"), P("head", "batch"), P("batch"), P("batch", "head"), P("head", "batch"))
    return jax.shard_map(on_device, mesh=mesh, in_specs=in_specs, out_specs=out_specs, check_vma=False)
```

time: 411 us -> 223 us (0.54); the launches traced: 405 us -> 223 us
  matrix products: 54.6 us -> 0 us
  local copies, waits for them, and re-layouts: 64.5 us -> 14.1 us
  waiting for transfers between devices: 25.7 us -> 0 us
  other arithmetic: 23.1 us -> 1.52 us
  Pallas kernels: 222 us -> 207 us
  between operations: 14.6 us -> 0.72 us
    dot_general x12 -> x0, matrix products: 54.6 us -> none  [on_device(): mm = lambda s, a, b: jnp.einsum(s, a, b, preferred_element_type=F32)]
    psum x3 -> x0, waiting for transfers between devices: 25.6 us -> none  [the longest x1 13 us: on_device(): hid = x + lax.psum(part.astype(BF), 'head').astype(F32)]
    unnamed x66 -> x9, local copies, waits for them, and re-layouts: 23 us -> 3.13 us
    pallas_call x5 -> x2, Pallas kernels: 222 us -> 207 us  [the longest x1 114 us: backward(): pl.pallas_call(functools.partial(k2_body, nb, custom), out_shape=out_shap...]
    transpose x6 -> x3, local copies, waits for them, and re-layouts: 14.8 us -> 2.69 us  [the longest x1 1.52 us: on_device(): return (y[None], tg[None], g1, qg, S[3].T, g2, cat(S[4:8]), cat(S[8:12]).T)]
    reduce_sum x6 -> x0, other arithmetic: 11.9 us -> none  [the longest x2 8.24 us: norm_backward(): gain_grad = jnp.sum(grad_out * normed, axis=0)]
    slice x6 -> x2, local copies, waits for them, and re-layouts: 12.9 us -> 2.46 us  [the longest x1 1.51 us: on_device(): g1, g2 = (gg[0, :, 0], gg[0, :, 1])]
    broadcast_in_dim x2 -> x0, other arithmetic: 6.3 us -> none  [the longest x1 3.85 us: on_device(): tg = (share(gh) + share(back1))[None]]
  transfers between devices with their start and end apart: 3 -> 0, of which waited for: 2 -> 0; matrix products, arithmetic and copies ran while one was open for 14% -> 0% of each run, Pallas kernels for 0% -> 0%
where the time goes in v2:
time: 223 us
  Pallas kernels  207 us (93%)
  local copies, waits for them, and re-layouts  14.1 us (6%)
    pallas_call x1, Pallas kernels, backward(): pl.pallas_call(functools.partial(k2_body, nb, custom), out_shape=out_shap...  114 us
    pallas_call x1, Pallas kernels, forward(): pl.pallas_call(functools.partial(k1_body, nb, custom), out_shape=out_shap...  92.5 us

profile of v2, /device:TPU:0, one launch (start us, length us, event | category | flops | bytes accessed | tf_op | source)
XLA Modules:
  0.0 222.9 jit_solution(10200333856531068570)
XLA Ops:
  0.6 0.0 copy-start.2
  0.6 0.7 pad_maximum_fusion.1
  1.3 0.1 copy.34
  1.4 0.6 pad.8.refs_2_
  2.1 1.5 pad.9.refs_5_
  3.6 0.9 reshape.40
  4.5 0.1 copy.31
  4.7 0.1 reshape.41
  4.8 1.0 bitcast_bitcast_fusion
  5.8 0.0 copy-done.2
  5.8 0.8 pad_maximum_fusion.refs_1_
  6.6 92.5 %shard_map.170 = (f32[8,768]{1,0:T(8,128)}, bf16[1024,768]{1,0:T(8,128)(2,1)}, bf16[3,1024,384]{2,1,0:T(8,128)(2,1)}, bf16[1024,384]{1,0:T(8,128)(2,1)}, bf16[10...) custom-call(bf16[1024,768]{1,0:T(8,128)(2,1)} %bitcast.44, ...), custom_call_target="tpu_custom_call" | custom-call | tf_op jit(solution)/shard_map/pallas_call | solution.py:525
  99.1 114.2 %shard_map.171 = (f32[512,768]{1,0:T(8,128)}, f32[12,48,384]{2,1,0:T(8,128)}, f32[1,48,128]{2,1,0:T(8,128)}) custom-call(bf16[1024,768]{1,0:T(8,128)(2,1)} %bitcast.46, bf16[1024,768]{1,0:T(8,128)(2,1)} %bitcast.45, f32[8,768]{1,0:T(8,128)} %get-tuple-element.28.refs_2_, bf16[12,4,4,48,384]{4,3,2,1,0:T(8,128)(2,1)} %get-tuple-element.29.refs_3_, ...), custom_call_target="tpu_custom_call" | custom-call | tf_op jit(solution)/shard_map/pallas_call | solution.py:849
  213.3 1.5 slice_reduce_fusion
  214.8 1.5 slice_bitcast_fusion.2
  216.3 0.9 slice.19
  217.2 1.1 slice_bitcast_fusion
  218.3 0.0 copy-start.1
  218.4 0.7 copy.41
  219.1 0.1 reshape.44
  219.2 0.0 copy-start
  219.2 0.2 copy.35
  219.4 0.8 reshape.45
  220.2 0.7 copy.40
  220.9 0.0 copy-done.1
  220.9 0.9 copy.46
  221.8 0.0 copy-done
  221.8 1.1 copy.47
Async XLA Ops:
  0.6 5.1 %copy-start.2 = (bf16[384,48]{0,1:T(8,128)(2,1)S(1)}, bf16[384,48]{0,1:T(8,128)(2,1)}, u32[]{:S(2)}) copy-start(bf16[384,48]{0,1:T(8,128)(2,1)} %param.14) | copy-start | bytes 110596
  218.3 2.6 %copy-start.1 = (bf16[512,768]{1,0:T(8,128)(2,1)S(1)}, bf16[512,768]{1,0:T(8,128)(2,1)}, u32[]{:S(2)}) copy-start(bf16[512,768]{1,0:T(8,128)(2,1)} %get-tuple-element.27) | copy-start | bytes 2359300
  219.2 2.6 %copy-start = (f32[512,768]{1,0:T(8,128)S(1)}, f32[512,768]{1,0:T(8,128)}, u32[]{:S(2)}) copy-start(f32[512,768]{1,0:T(8,128)} %get-tuple-element.43) | copy-start | bytes 4718596

commit v3 on v2

v3 whole, which is shorter than its diff:
```python
import functools

import jax
import jax.numpy as jnp
from jax import lax
from jax.experimental import pallas as pl
from jax.experimental.pallas import tpu as pltpu
from jax.sharding import PartitionSpec as P

F32=jnp.float32; BF=jnp.bfloat16
BIG=1e30
NT=(((1,),(1,)),((),()))
TN=(((0,),(0,)),((),()))
NN=(((1,),(0,)),((),()))
def dot(a,b,dims=NN): return lax.dot_general(a,b,dims,preferred_element_type=F32)
def split3(x):
    a=x.astype(BF); r=x-a.astype(F32); b=r.astype(BF); c=(r-b.astype(F32)).astype(BF)
    return a,b,c
def split2(x):
    a=x.astype(BF); return a,(x-a.astype(F32)).astype(BF)
L=1024
def lane(shape): return lax.broadcasted_iota(jnp.int32,shape,len(shape)-1)
def sub(shape): return lax.broadcasted_iota(jnp.int32,shape,len(shape)-2)

def build_masks(own_row, topT):
    mt=jnp.where(own_row==sub((128,L)),1.0,0.0).astype(BF)
    m=jnp.transpose(mt)
    hi=lax.shift_right_arithmetic(topT,5); bit=lax.shift_left(jnp.int32(1),topT&31)
    words=L//32
    a_iota=sub((words,128))
    w=jnp.zeros((words,128),jnp.int32)
    for t in range(topT.shape[0]):
        w=w|jnp.where(hi[t:t+1]==a_iota,bit[t:t+1],0)
    b_iota=sub((32,128)); ln=lane((32,128))
    extra=(ln>=100)&(ln<103)
    ns=[]
    for a in range(words):
        b=(lax.shift_right_logical(jnp.broadcast_to(w[a:a+1],(32,128)),b_iota)&1)
        ns.append(jnp.where(extra,-1.0,jnp.where(b==1,0.0,-BIG)))
    n=jnp.concatenate(ns,0).astype(BF)
    return m,n


TQ = 256
TJ = 256
MESH=pl.DeviceIdType.MESH


def NOP(p): pass
class Place:
    def __init__(self, nb):
        self.nz=nb//4
        self.b=lax.axis_index("batch"); self.h=lax.axis_index("head")
        self.z=self.b//4; self.r=lax.rem(self.b,4)
        even=lax.rem(self.r,2)==0
        self.rx=jnp.where(even,self.r+1,self.r-1)
        self.ry=jnp.where(self.r<2,self.r+2,self.r-2)
        self.rd=3-self.r
        self.X=(self.z*4+self.rx,self.h); self.Y=(self.z*4+self.ry,self.h)
        self.up=(self.b+4,self.h); self.dn=(self.b-4,self.h); self.twin=(self.b,1-self.h)
    def barrier(self):
        bar=pltpu.get_barrier_semaphore()
        for d in (self.X,self.Y,self.twin):
            pl.semaphore_signal(bar,inc=1,device_id=d,device_id_type=MESH)
        @pl.when(self.z<self.nz-1)
        def _(): pl.semaphore_signal(bar,inc=1,device_id=self.up,device_id_type=MESH)
        @pl.when(self.z>0)
        def _(): pl.semaphore_signal(bar,inc=1,device_id=self.dn,device_id_type=MESH)
        lines=jnp.where(self.z<self.nz-1,1,0)+jnp.where(self.z>0,1,0)
        pl.semaphore_wait(bar,3+lines)

def rc(src,dst,ss,rs,dev):
    return pltpu.make_async_remote_copy(src_ref=src,dst_ref=dst,send_sem=ss,recv_sem=rs,device_id=dev,device_id_type=MESH)

class Gather:
    def __init__(self, pc, g, ss, rs):
        self.pc=pc; self.g=g; self.ss=ss; self.rs=rs; self.n=2*(pc.nz-1)
    def cz(self,p,zz,k,dev):
        s=self.g.at[p,zz,self.pc.r]
        return rc(s,s,self.ss.at[p,k],self.rs.at[p,k],dev)
    def z0(self,p):
        c=self.pc
        @pl.when(c.z<c.nz-1)
        def _(): self.cz(p,c.z,0,c.up).start()
        @pl.when(c.z>0)
        def _(): self.cz(p,c.z,1,c.dn).start()
    def zk(self,p,d):
        c=self.pc
        @pl.when(c.z-d>=0)
        def _():
            self.cz(p,c.z-d,2*(d-1),c.up).wait_recv()
        if d<c.nz-1:
            @pl.when((c.z-d>=0)&(c.z<c.nz-1))
            def _(): self.cz(p,c.z-d,2*d,c.up).start()
        @pl.when(c.z+d<c.nz)
        def _():
            self.cz(p,c.z+d,2*(d-1)+1,c.dn).wait_recv()
        if d<c.nz-1:
            @pl.when((c.z+d<c.nz)&(c.z>0))
            def _(): self.cz(p,c.z+d,2*d+1,c.dn).start()
    def cb(self,p,r,k,dev):
        s=self.g.at[p,:,r]
        return rc(s,s,self.ss.at[p,self.n+k],self.rs.at[p,self.n+k],dev)
    def ch(self,p,r,lo,k,dev):
        h=self.pc.nz//2
        s=self.g.at[p,pl.ds(0,h),r] if lo else self.g.at[p,pl.ds(h,self.pc.nz-h),r]
        return rc(s,s,self.ss.at[p,self.n+k],self.rs.at[p,self.n+k],dev)
    def x0(self,p):
        c=self.pc
        self.cb(p,c.r,0,c.X).start(); self.cb(p,c.r,1,c.Y).start()
    def x1(self,p):
        c=self.pc
        self.cb(p,c.rx,0,c.X).wait_recv()
        self.ch(p,c.rx,True,2,c.Y).start()
        self.cb(p,c.ry,1,c.Y).wait_recv()
        self.ch(p,c.ry,False,3,c.X).start()
    def x2(self,p):
        c=self.pc
        self.ch(p,c.rd,True,2,c.Y).wait_recv()
        self.ch(p,c.rd,False,3,c.X).wait_recv()
    def drain(self,p):
        c=self.pc
        for d in range(c.nz-1):
            @pl.when((c.z-d>=0)&(c.z<c.nz-1))
            def _(): self.cz(p,c.z-d,2*d,c.up).wait_send()
            @pl.when((c.z+d<c.nz)&(c.z>0))
            def _(): self.cz(p,c.z+d,2*d+1,c.dn).wait_send()
        self.cb(p,c.r,0,c.X).wait_send(); self.cb(p,c.r,1,c.Y).wait_send()
        self.ch(p,c.rx,True,2,c.Y).wait_send(); self.ch(p,c.ry,False,3,c.X).wait_send()
    def steps(self):
        nz=self.pc.nz
        def last(p):
            self.zk(p,nz-1); self.x0(p)
        return [self.z0]+[functools.partial(lambda d,p:self.zk(p,d),d) for d in range(1,nz-1)]+[last]+[NOP]+[self.x1]+[NOP]+[self.x2]

class Scatter:
    def __init__(self, pc, g, d, rx, ry, ru, rd, ss, rs, slot=lambda p: p):
        self.pc=pc;self.g=g;self.d=d;self.bx=rx;self.by=ry;self.bu=ru;self.bd=rd;self.ss=ss;self.rs=rs
        self.h=pc.nz//2; self.slot=slot
    def half(self,p,r,lo):
        h=self.h; n=self.pc.nz
        return (self.g.at[p,pl.ds(0,h),r],self.d.at[self.slot(p),pl.ds(0,h)]) if lo else (self.g.at[p,pl.ds(h,n-h),r],self.d.at[self.slot(p),pl.ds(h,n-h)])
    def c0(self,p,lo):
        s,t=self.half(p,self.pc.rd,lo); k=0 if lo else 1
        return rc(s,t,self.ss.at[self.slot(p),k],self.rs.at[self.slot(p),k],self.pc.X if lo else self.pc.Y)
    def c1(self,p,x):
        c=self.pc
        return rc(self.g.at[p,:,c.rx if x else c.ry],(self.bx if x else self.by).at[self.slot(p)],self.ss.at[self.slot(p),2 if x else 3],self.rs.at[self.slot(p),2 if x else 3],c.X if x else c.Y)
    def cu(self,p,zz,up):
        c=self.pc; k=4+zz if up else 4+c.nz+zz
        return rc(self.g.at[p,zz,c.r],(self.bu if up else self.bd).at[self.slot(p),zz],self.ss.at[self.slot(p),k],self.rs.at[self.slot(p),k],c.up if up else c.dn)
    def add(self,dst,*srcs):
        v=dst[...].astype(F32)
        for s in srcs: v=v+s[...].astype(F32)
        dst[...]=v.astype(BF)
    def s0(self,p):
        self.c0(p,True).start(); self.c0(p,False).start()
    def s1(self,p):
        c=self.pc;h=self.h;n=c.nz
        self.c0(p,True).wait_recv()
        self.add(self.g.at[p,pl.ds(0,h),c.ry],self.d.at[self.slot(p),pl.ds(0,h)])
        self.c1(p,False).start()
        self.c0(p,False).wait_recv()
        self.add(self.g.at[p,pl.ds(h,n-h),c.rx],self.d.at[self.slot(p),pl.ds(h,n-h)])
        self.c1(p,True).start()
    def s2(self,p):
        c=self.pc
        self.c1(p,True).wait_recv(); self.c1(p,False).wait_recv()
        self.add(self.g.at[p,:,c.r],self.bx.at[self.slot(p)],self.by.at[self.slot(p)])
        self.zk(p,0)
    def zk(self,p,k):
        c=self.pc; nz=c.nz
        @pl.when(c.z==k)
        def _():
            for zz in range(nz-1,k,-1):
                if k>0:
                    self.cu(p,zz,True).wait_recv()
                    self.add(self.g.at[p,zz,c.r],self.bu.at[self.slot(p),zz])
                self.cu(p,zz,True).start()
        @pl.when(c.z==nz-1-k)
        def _():
            for zz in range(0,nz-1-k):
                if k>0:
                    self.cu(p,zz,False).wait_recv()
                    self.add(self.g.at[p,zz,c.r],self.bd.at[self.slot(p),zz])
                self.cu(p,zz,False).start()
    def fin(self,p,tot,place=None):
        c=self.pc
        tot[...]=self.g[p,c.z,c.r].astype(F32)
        @pl.when(c.z>0)
        def _():
            self.cu(p,c.z,True).wait_recv()
            tot[...]+=self.bu[self.slot(p),c.z].astype(F32)
        @pl.when(c.z<c.nz-1)
        def _():
            self.cu(p,c.z,False).wait_recv()
            tot[...]+=self.bd[self.slot(p),c.z].astype(F32)
        if place is not None: place(p)
    def drain(self,p):
        c=self.pc; nz=c.nz
        self.c0(p,True).wait_send(); self.c0(p,False).wait_send()
        self.c1(p,True).wait_send(); self.c1(p,False).wait_send()
        for zz in range(nz):
            @pl.when(zz>c.z)
            def _(): self.cu(p,zz,True).wait_send()
            @pl.when(zz<c.z)
            def _(): self.cu(p,zz,False).wait_send()
    def lines(self):
        return [functools.partial(lambda k,p:self.zk(p,k),k) for k in range(1,self.pc.nz-1)]
    def steps(self,place,tot):
        return [self.s0,NOP,self.s1,NOP,self.s2]+self.lines()+[lambda p:self.fin(p,tot,place)]
    def tight(self,out):
        return [self.s0,self.s1,self.s2]+self.lines()+[lambda p:self.fin(p,out.at[0])]


EPS = 1e-5
RT = 256


def pick(static, cond, body):
    if isinstance(cond, (bool, int)):
        if cond:
            body()
    else:
        pl.when(cond)(body)


def norm_rows(values):
    mean = jnp.mean(values, axis=1, keepdims=True)
    centred = values - mean
    inverse = lax.rsqrt(jnp.mean(centred * centred, axis=1, keepdims=True) + EPS)
    return centred * inverse, inverse


def gelu_both(u):
    c = 0.7978845608028654
    u2 = u * u
    t = jnp.tanh(c * u * (1.0 + 0.044715 * u2))
    half = 0.5 + 0.5 * t
    act = u * half
    grad = half + (0.5 * c) * u * (1.0 - t * t) * (1.0 + (3 * 0.044715) * u2)
    return act, grad


def flat(ref, p):
    v = ref[p]
    return v.reshape(-1, v.shape[-1])


def tiles(n):
    return lambda f: pl.loop(0, n)(f)


def rows_of(i, n=RT):
    return pl.ds(pl.multiple_of(i * n, n), n)


def twin_copy(pc, src, dst, ss, rs):
    return rc(src, dst, ss, rs, pc.twin)


def members(cl, hh):
    return jnp.where(cl[hh] == sub((128, L)), 1.0, 0.0).astype(BF)


def fwd_head(p, h, qkv, mb, cl, n_s, seg, qaug, kaug, att, ex, prob_o):
    odd = h == 1
    hh = 2 * p + h
    q = qkv[p, :, 0:128]
    k = qkv[p, :, 128:256]
    v = qkv[p, :, 256:384]
    ln = lane((L, 128))
    mine = (ln >= 64) if odd else (ln < 64)
    lc = lane((128, 128))
    minec = (lc >= 64) if odd else (lc < 64)
    zero = jnp.zeros((), BF)
    qm = jnp.where(mine, q, zero)
    vaug = jnp.where(mine, v, jnp.ones((), BF))
    mt = members(cl, hh)
    top = jnp.transpose(n_s[hh]).astype(F32) == 0.0
    cnt = jnp.maximum(jnp.sum(mt.astype(F32), axis=1, keepdims=True), 1.0)
    cen = (dot(mt, qm) / cnt).astype(BF)
    cs = (cen.astype(F32) * 0.125).astype(BF)
    s = dot(cs, k, NT)
    cm = lax.rem(sub((128, 1)), jnp.int32(10))
    s = jnp.where(seg[...] == cm, s, -BIG)
    mx = jnp.max(s, axis=1, keepdims=True)
    e = jnp.exp(s - mx)
    prob = e / jnp.sum(e, axis=1, keepdims=True)
    mass = jnp.sum(jnp.where(top, prob, 0.0), axis=1, keepdims=True)
    prob_o[hh] = jnp.where(top, -prob, prob).astype(BF)
    rest = dot(jnp.where(top, 0.0, prob).astype(BF), v)
    rh, rl = split2(jnp.where(minec, rest, jnp.broadcast_to(mass, (128, 128))))
    rr = jnp.concatenate([rh, rl], 1)
    qaug[:, :128] = (qm.astype(F32) * 0.125).astype(BF)
    qaug[:, 128:] = mb[hh]
    kaug[:, :128] = k
    kaug[:, 128:] = n_s[hh]
    lt = lane((TQ, 128))
    minet = (lt >= 64) if odd else (lt < 64)
    cols = pl.ds(pl.multiple_of(p * 128, 128), 128)
    for t in range(L // TQ):
        sl = pl.ds(t * TQ, TQ)
        sc = dot(qaug[sl, :], kaug[...], NT)
        mm = jnp.max(sc, axis=1, keepdims=True)
        pr = jnp.exp(sc - mm).astype(BF)
        o = dot(pr, vaug)
        mt_ = qaug[sl, 128:]
        ee = dot(mt_, rr)
        ee = ee[:, :128] + ee[:, 128:]
        osw = pltpu.roll(o, 64, 1)
        esw = pltpu.roll(ee, 64, 1)
        exact = o / osw
        a = exact * esw + ee
        tot = jnp.where(minet, osw, o)
        ms = jnp.where(minet, esw, ee)
        lse = mm + jnp.log(tot) - jnp.log(jnp.maximum(ms, 1e-37))
        h3, m3, l3 = split3(lse)
        mb[hh, sl, :] = jnp.where(lt == 100, h3.astype(F32), jnp.where(lt == 101, m3.astype(F32), jnp.where(lt == 102, l3.astype(F32), mt_.astype(F32)))).astype(BF)
        if odd:
            att[sl, cols] = jnp.where(lt < 64, att[sl, cols], a.astype(BF))
            ex[sl, cols] = jnp.where(lt < 64, ex[sl, cols], exact.astype(BF))
        else:
            att[sl, cols] = a.astype(BF)
            ex[sl, cols] = exact.astype(BF)


def as_column(row):
    n = row.shape[1]
    eye = sub((n, n)) == lane((n, n))
    return jnp.sum(jnp.where(eye, row.astype(F32), 0.0), axis=1, keepdims=True)


def fill_own(pc, g, gg, q3, oT, upw, dT, ga, gf):
    for p in range(3):
        for i in range(3):
            g[p, pc.z, pc.r, :, i * 128:(i + 1) * 128] = q3[i, :, p * 128:(p + 1) * 128]
    g[3, pc.z, pc.r] = oT[...]
    for q in range(4):
        g[4 + q, pc.z, pc.r] = upw[:, q * 384:(q + 1) * 384]
        g[8 + q, pc.z, pc.r] = dT[:, q * 384:(q + 1) * 384]
    R = oT.shape[0]
    ln = lane((R, 128))
    gg[0, pc.z, pc.r] = jnp.where(ln == 0, as_column(ga[...]), jnp.where(ln == 1, as_column(gf[...]), 0.0)).astype(BF)


def bwd_head(p, h, cl, s, qaug, kaug, gaug, vaug, dq_o, dk_o, dv_o, dqt):
    qkv, g, ex = s["qkv"], s["gatt"], s["ex"]
    hh = 2 * p + h
    cols = pl.ds(pl.multiple_of(p * 128, 128), 128)
    qv = qkv[p, :, 0:128]
    kv = qkv[p, :, 128:256]
    vv = qkv[p, :, 256:384]
    gv = g[:, cols]
    ln = lane((L, 128))
    zero = jnp.zeros((), BF)
    lc = lane((128, 128))
    kT = jnp.transpose(kv)
    prod = gv.astype(F32) * ex[:, cols].astype(F32)
    mine = (ln >= 64) if h else (ln < 64)
    minec = (lc >= 64) if h else (lc < 64)
    o = 0 if h else 64
    r = jnp.sum(jnp.where(mine, prod, 0.0), axis=1, keepdims=True)
    h3, m3, l3 = split3(r)
    gm = jnp.where(mine, gv, zero)
    ga = jnp.where(ln == o, h3.astype(F32), jnp.where(ln == o + 1, m3.astype(F32), jnp.where(ln == o + 2, l3.astype(F32), gm.astype(F32)))).astype(BF)
    gaug[...] = ga
    vaug[...] = jnp.where(mine, vv, jnp.where((ln >= o) & (ln < o + 3), jnp.full((), -1.0, BF), zero))
    qm = jnp.where(mine, qv, zero)
    qs = (qm.astype(F32) * 0.125).astype(BF)
    qaug[:, :128] = qs
    qaug[:, 128:] = s["mb"][hh]
    kaug[:, :128] = kv
    kaug[:, 128:] = s["ns"][hh]
    mt = members(cl, hh)
    signed = s["prob"][hh].astype(F32)
    top = signed < 0.0
    prob = jnp.abs(signed)
    cnt = jnp.maximum(jnp.sum(mt.astype(F32), axis=1, keepdims=True), 1.0)
    cen = (dot(mt, qm) / cnt).astype(BF)
    cs = (cen.astype(F32) * 0.125).astype(BF)
    gr = dot(mt, ga)
    gmass = jnp.sum(jnp.where((lc >= o) & (lc < o + 3), gr, 0.0), axis=1, keepdims=True)
    grest = jnp.where(minec, gr, 0.0).astype(BF)
    gp = jnp.where(top, gmass, dot(grest, vv, NT))
    gs = (prob * (gp - jnp.sum(prob * gp, axis=1, keepdims=True))).astype(BF)
    rw = jnp.where(top, 0.0, prob).astype(BF)
    gcen = dot(gs, jnp.where(mine, kv, zero)) / cnt
    gh, gl = split2(gcen)
    gg = jnp.concatenate([gh, gl], 1)
    gsT = jnp.transpose(gs)
    rwT = jnp.transpose(rw)
    kTh = kT[64 * h:64 * h + 64]
    for t in range(L // TJ):
        sl = pl.ds(t * TJ, TJ)
        st = dot(kaug[sl, :], qaug[...], NT)
        pr = jnp.exp(st)
        dp = dot(vaug[sl, :], gaug[...], NT)
        ds = (pr * dp).astype(BF)
        dv = dot(pr.astype(BF), gm) + dot(rwT[t * TJ:(t + 1) * TJ], grest)
        dk = dot(ds, qs) + dot(gsT[t * TJ:(t + 1) * TJ], cs)
        if h == 0:
            dv_o[sl, :] = dv
            dk_o[sl, :] = dk
        else:
            dv_o[sl, :] += dv
            dk_o[sl, :] += dk
        dqp = dot(kTh[:, t * TJ:(t + 1) * TJ], ds)
        if t == 0:
            dqt[64 * h:64 * h + 64, :] = dqp
        else:
            dqt[64 * h:64 * h + 64, :] += dqp
    dd = dot(jnp.where(ln < 100, s["mb"][hh], zero), gg)
    dd = dd[:, :128] + dd[:, 128:]
    if h == 0:
        dq_o[...] = dd
    else:
        dq_o[...] += dd


def place_sum(p, tot, outs):
    qg, og, ug, dg = outs

    def pair(p):
        for i in range(3):
            qg[i, :, pl.ds(pl.multiple_of(p * 128, 128), 128)] = tot[:, i * 128:(i + 1) * 128]

    def wide(ref, q):
        ref[:, pl.ds(pl.multiple_of(q * 384, 128), 384)] = tot[...]

    pick(None, p < 3, lambda: pair(p))
    pick(None, p == 3, lambda: og.__setitem__(..., tot[...]))
    pick(None, (3 < p < 8) if isinstance(p, int) else (p > 3) & (p < 8), lambda: wide(ug, p - 4))
    pick(None, p >= 12, lambda: wide(dg, p - 12))


def finish_body(*refs):
    ins, gg, outs, (g1, g2), bufs, (si, so) = refs[:6], refs[6], refs[7:13], refs[13:15], refs[15:21], refs[21:]
    ci = [pltpu.make_async_copy(a, b, si.at[i]) for i, (a, b) in enumerate(zip(ins, bufs))]
    co = [pltpu.make_async_copy(a, b, so.at[i]) for i, (a, b) in enumerate(zip(bufs, outs))]
    for c in ci:
        c.start()
    R = gg.shape[1]
    eye = sub((R, R)) == lane((R, R))
    for i, g in enumerate((g1, g2)):
        g[...] = jnp.sum(jnp.where(eye, gg[0, :, i:i + 1], 0.0), axis=0, keepdims=True)
    for a, b in zip(ci, co):
        a.wait()
        b.start()
    for c in co:
        c.wait()


def finish(*arrays):
    V = pl.BlockSpec(memory_space=pltpu.VMEM)
    A = pl.BlockSpec(memory_space=pl.ANY)
    R = arrays[6].shape[1]
    dma = pltpu.SemaphoreType.DMA
    return pl.pallas_call(
        finish_body,
        out_shape=[jax.ShapeDtypeStruct(a.shape, a.dtype) for a in arrays[:6]] + [jax.ShapeDtypeStruct((1, R), F32)] * 2,
        in_specs=[A] * 6 + [V], out_specs=[A] * 6 + [V] * 2,
        scratch_shapes=[pltpu.VMEM(a.shape, a.dtype) for a in arrays[:6]] + [dma((6,)), dma((6,))],
        compiler_params=pltpu.CompilerParams(vmem_limit_bytes=60 << 20),
    )(*arrays)


def scratch_shapes(custom, nz, R):
    f = lambda *s: (s, F32)
    b = lambda *s: (s, BF)
    wide = (16, nz, 4, R, 384) if custom else (16, 768, 384)
    return {
        "gr": f(8, 768), "n1": b(L, 768), "qkv": b(3, L, 384), "att": b(L, 384), "ex": b(L, 384), "mb": b(6, L, 128),
        "ns": b(6, L, 128), "prob": b(6, 128, L), "hid": f(L, 768), "n2": b(L, 768), "act": b(4, L, 384), "dg": b(4, L, 384),
        "aT": b(768, L), "ghs": f(L // 2, 768), "eb": b(L, 768), "er": b(L, 768), "fr": b(L // 2, 768), "gatt": b(L, 384),
        "dqkv": b(L, 384), "qaug": b(L, 256), "kaug": b(L, 256), "gaug": b(L, 128), "vaug": b(L, 128),
        "dqs": f(L, 128), "dks": f(L, 128), "dvs": f(L, 128), "dqt": f(128, L), "gacc": f(8, 768), "vb": f(8, 768), "vr": f(8, 768),
        "wg": b(*wide),
    }


def layer_body(nb, custom, names, *refs):
    refs = list(refs)
    take = lambda n: [refs.pop(0) for _ in range(n)]
    x, ct, seg, cl, tt = take(5)
    own = take(6 if custom else 2)
    y, tg, out_g = take(3)
    out_s = take(4) if custom else take(1)[0]
    s = dict(zip(names, take(len(names))))
    tpad, es, ers, vs, vrs = take(5)
    pc = Place(nb)
    wg, hid, n1, n2, qkv, att, ex, act, dg = (s[n] for n in ("wg", "hid", "n1", "n2", "qkv", "att", "ex", "act", "dg"))
    aT, eb, er, fr, gr, gacc = (s[n] for n in ("aT", "eb", "er", "fr", "gr", "gacc"))
    half, nh, nt = L // 2, L // 2 // RT, L // RT

    if custom:
        gg, tot, gbuf, ss, rs, gss, grs, ss2, rs2, gss2, grs2 = take(11)
        land, gland = take(5), take(5)
        G, Gg = Gather(pc, wg, ss, rs), Gather(pc, gg, gss, grs)
        S = Scatter(pc, wg, *land, ss2, rs2, slot=lambda p: p - 4 if isinstance(p, int) and p >= 12 else p if isinstance(p, int) else jnp.where(p >= 12, p - 4, p))
        Sg = Scatter(pc, gbuf, *gland, gss2, grs2)
        m = pc.nz - 1
        line = [(d, functools.partial(lambda d, p: G.zk(p, d), d), 0, 12) for d in range(1, m)]

        def last(p):
            G.zk(p, m)
            G.x0(p)
        gather = [(m + 3, G.x2, 3, 12), (m + 2, G.x2, 0, 3), (m + 2, G.x1, 3, 12), (m + 1, G.x1, 0, 3), (m, last, 0, 12)] + line[::-1] + [(0, G.z0, 0, 12)]
        gsteps = [Gg.z0] + [functools.partial(lambda d: Gg.zk(0, d), d) for d in range(1, m)] + [None, Gg.x1, Gg.x2]
        ssteps = S.steps(lambda p: place_sum(p, tot, out_s), tot)
        tails = Sg.tight(out_g)
        starts = {14: 12, 15: 13, 16: 14, 17: 15, 19: 4, 20: 5, 21: 6, 22: 7, 23: 3, 24: 0, 26: 1, 28: 2}

        def tick(t, span=None):
            fixed = isinstance(t, int)
            ts = [t] if fixed else list(range(*span))
            for i in range(len(ssteps) - 1, -1, -1):
                hits = [u - i for u in ts if u - i in starts]
                if not hits or ssteps[i] is NOP:
                    continue
                if fixed:
                    ssteps[i](starts[hits[0]])
                    continue
                u = t - i
                ok = functools.reduce(jnp.logical_or, [u == k for k in hits])
                part = functools.reduce(lambda a, k: jnp.where(u == k, starts[k], a), hits, 0)
                pl.when(ok)(lambda i=i, part=part: ssteps[i](part))
            for off, fn, lo, hi in gather:
                if not any(lo <= u - off < hi for u in ts):
                    continue
                p = t - off
                pick(None, True if fixed else (p >= lo) & (p < hi), lambda fn=fn, p=p: fn(p))
            if fixed and t < len(gsteps):
                if t == m:
                    Gg.zk(0, m)
                    Gg.x0(0)
                elif t == 0:
                    gsteps[0](0)
                elif t < m:
                    gsteps[t]()
                else:
                    gsteps[t](0)
    else:
        tick = lambda t, span=None: None

    tpad[...] = jnp.full_like(tpad, -1)
    pc.barrier()
    if custom:
        fill_own(pc, wg, gg, *own)
    tick(0)

    @tiles(nt)
    def _(i):
        hid[rows_of(i), :] = norm_rows(x[rows_of(i), :].astype(F32))[0]

    tick(1)

    def mask(h):
        tpad[:, 0:tt.shape[2]] = tt[h]
        a, n = build_masks(cl[h], tpad[...])
        s["mb"][h], s["ns"][h] = a, n

    def transpose_into(src):
        for i in range(nt):
            aT[:, i * RT:(i + 1) * RT] = jnp.transpose(src[i * RT:(i + 1) * RT, :])

    def put(p, left, right):
        wg[p] = dot(left, right).astype(BF).reshape(wg.shape[1:])

    pl.loop(0, 2)(mask)
    tick(2)
    pl.loop(2, 4)(mask)
    tick(3)
    pl.loop(4, 6)(mask)
    transpose_into(ct)
    tick(4)
    tick(5)
    if custom:
        gains = gg[0].reshape(768, 128)
    else:
        c = pltpu.make_async_copy(own[0], wg.at[0:12], vs)
        c.start()
        c.wait()
        gains = own[1][...]
    gr[...] = jnp.transpose(gains.astype(F32))[0:8]

    @tiles(nt)
    def _(i):
        n1[rows_of(i), :] = (hid[rows_of(i), :] * gr[0:1, :]).astype(BF)

    @pl.loop(0, 3)
    def _(p):
        @tiles(nt)
        def _(i):
            qkv[p, rows_of(i), :] = dot(n1[rows_of(i), :], flat(wg, p)).astype(BF)
        for h in range(2):
            tick(6 + 2 * p + h, (6 + h, 12, 2))
            fwd_head(p, h, qkv, s["mb"], cl, s["ns"], seg, s["qaug"], s["kaug"], att, ex, s["prob"])

    def send(k, src, dst, i):
        return twin_copy(pc, src.at[rows_of(i)], dst.at[rows_of(i)], es.at[k + i], ers.at[k + i])

    @tiles(nt)
    def _(i):
        eb[rows_of(i), :] = dot(att[rows_of(i), :], flat(wg, 3), NT).astype(BF)
        send(0, eb, er, i).start()

    tick(12)

    @tiles(nt)
    def _(i):
        r = rows_of(i)
        send(0, eb, er, i).wait()
        hv = x[r, :].astype(F32) + (eb[r, :].astype(F32) + er[r, :].astype(F32))
        hid[r, :] = hv
        n2[r, :] = (norm_rows(hv)[0] * gr[1:2, :]).astype(BF)

    def up(q):
        @tiles(nt)
        def _(i):
            a, d = gelu_both(dot(n2[rows_of(i), :], flat(wg, 4 + q)))
            act[q, rows_of(i), :] = a.astype(BF)
            dg[q, rows_of(i), :] = d.astype(BF)

    pl.loop(0, 2)(up)
    tick(13)
    pl.loop(2, 4)(up)

    def down_grad(q):
        put(12 + q, aT[...], act[q])

    pl.loop(0, 2)(down_grad)
    tick(14)
    pl.loop(2, 4)(down_grad)
    tick(15)
    transpose_into(n2)
    tick(16)
    tick(17)

    def part(i):
        acc = dot(act[0, rows_of(i), :], flat(wg, 8), NT)
        for q in range(1, 4):
            acc += dot(act[q, rows_of(i), :], flat(wg, 8 + q), NT)
        return acc

    @tiles(nh)
    def _(i):
        eb[rows_of(i), :] = part((1 - pc.h) * nh + i).astype(BF)
        send(4, eb, fr, i).start()

    @pl.loop(0, 4)
    def _(q):
        @tiles(nt)
        def _(i):
            ga = dot(ct[rows_of(i), :], flat(wg, 8 + q))
            dg[q, rows_of(i), :] = (ga * dg[q, rows_of(i), :].astype(F32)).astype(BF)

    @tiles(nh)
    def _(i):
        acc = part(pc.h * nh + i).astype(BF).astype(F32)
        send(4, eb, fr, i).wait()
        y[rows_of(i), :] = (hid[rows_of(pc.h * nh + i), :] + (acc + fr[rows_of(i), :].astype(F32))).astype(BF)

    tick(18)
    if custom:
        @pl.loop(0, 12)
        def _(p):
            G.drain(p)
        Gg.drain(0)

    @tiles(nt)
    def _(i):
        acc = dot(dg[0, rows_of(i), :], flat(wg, 4), NT)
        for q in range(1, 4):
            acc += dot(dg[q, rows_of(i), :], flat(wg, 4 + q), NT)
        eb[rows_of(i), :] = acc.astype(BF)
        send(6, eb, er, i).start()

    def up_grad(q):
        put(4 + q, aT[...], dg[q])

    pl.loop(0, 2)(up_grad)
    tick(19)
    pl.loop(2, 4)(up_grad)
    gacc[...] = jnp.zeros_like(gacc)
    gat = n2

    @tiles(nt)
    def _(i):
        r = rows_of(i)
        send(6, eb, er, i).wait()
        gn = eb[r, :].astype(F32) + er[r, :].astype(F32)
        n, inv = norm_rows(hid[r, :])
        gacc[1:2, :] += jnp.sum(gn * n, axis=0, keepdims=True)
        a = gn * gr[1:2, :]
        back = (a - jnp.mean(a, axis=1, keepdims=True) - n * jnp.mean(a * n, axis=1, keepdims=True)) * inv
        gh = ct[r, :].astype(F32) + back
        gat[r, :] = gh.astype(BF)

        @pl.when((i >= pc.h * nh) & (i < pc.h * nh + nh))
        def _():
            s["ghs"][rows_of(i - pc.h * nh), :] = gh

    tick(20)

    @tiles(nt)
    def _(i):
        s["gatt"][rows_of(i), :] = dot(gat[rows_of(i), :], flat(wg, 3)).astype(BF)

    transpose_into(gat)
    put(3, aT[...], att[...])
    tick(21)
    transpose_into(n1)
    tick(22)
    nacc = hid
    dqkv = s["dqkv"]

    @pl.loop(0, 3)
    def _(p):
        bwd_head(p, 0, cl, s, s["qaug"], s["kaug"], s["gaug"], s["vaug"], s["dqs"], s["dks"], s["dvs"], s["dqt"])
        tick(23 + 2 * p, (23, 29, 2))
        bwd_head(p, 1, cl, s, s["qaug"], s["kaug"], s["gaug"], s["vaug"], s["dqs"], s["dks"], s["dvs"], s["dqt"])
        dqkv[:, 0:128] = ((s["dqs"][...] + jnp.transpose(s["dqt"][...])) * 0.125).astype(BF)
        dqkv[:, 128:256] = s["dks"][...].astype(BF)
        dqkv[:, 256:384] = s["dvs"][...].astype(BF)

        @tiles(nt)
        def _(i):
            v = dot(dqkv[rows_of(i), :], flat(wg, p), NT)

            @pl.when(p == 0)
            def _():
                nacc[rows_of(i), :] = v

            @pl.when(p > 0)
            def _():
                nacc[rows_of(i), :] += v
        put(p, aT[...], dqkv[...])
        tick(24 + 2 * p, (24, 30, 2))

    @tiles(nh)
    def _(i):
        eb[rows_of(i), :] = nacc[rows_of((1 - pc.h) * nh + i), :].astype(BF)
        send(10, eb, fr, i).start()

    tick(29)

    @tiles(nh)
    def _(i):
        r = rows_of(i)
        send(10, eb, fr, i).wait()
        gn = nacc[rows_of(pc.h * nh + i), :].astype(BF).astype(F32) + fr[r, :].astype(F32)
        n, inv = norm_rows(x[rows_of(pc.h * nh + i), :].astype(F32))
        gacc[0:1, :] += jnp.sum(gn * n, axis=0, keepdims=True)
        a = gn * gr[0:1, :]
        back = (a - jnp.mean(a, axis=1, keepdims=True) - n * jnp.mean(a * n, axis=1, keepdims=True)) * inv
        tg[r, :] = s["ghs"][r, :] + back

    s["vb"][...] = gacc[...]
    cv = twin_copy(pc, s["vb"], s["vr"], vs, vrs)
    cv.start()
    tick(30)
    cv.wait()
    one = gacc[0:1, :] + s["vr"][0:1, :]
    both = jnp.where(sub((8, 768)) == 0, jnp.broadcast_to(one, (8, 768)), gacc[...])
    if custom:
        wide = jnp.concatenate([both, jnp.zeros((120, 768), F32)], 0)
        gbuf[0] = jnp.transpose(wide).astype(BF).reshape(gbuf.shape[1:])
        for t in range(31, max(28 + len(ssteps), 31 + len(tails))):
            tick(t)
            if t - 31 < len(tails):
                tails[t - 31](0)

        @pl.loop(0, 12)
        def _(i):
            S.drain(jnp.where(i < 8, i, i + 4))
        Sg.drain(0)
    else:
        c = pltpu.make_async_copy(wg, out_s, vs)
        c.start()
        out_g[...] = both
        c.wait()


def layer(nb, custom, *args):
    V = pl.BlockSpec(memory_space=pltpu.VMEM)
    A = pl.BlockSpec(memory_space=pl.ANY)
    nz = nb // 4
    dma = pltpu.SemaphoreType.DMA
    tt, ws = args[4], args[5:]
    R = ws[1].shape[0]
    shapes = scratch_shapes(custom, nz, R)
    out_shape = [jax.ShapeDtypeStruct((L // 2, 768), BF), jax.ShapeDtypeStruct((L // 2, 768), F32)]
    if custom:
        out_shape += [jax.ShapeDtypeStruct(sh, F32) for sh in ((1, R, 128), (3, R, 384), (R, 384), (R, 1536), (R, 1536))]
        out_specs = [V] * 7
        in_specs = [V] * len(args)
    else:
        out_shape += [jax.ShapeDtypeStruct((8, 768), F32), jax.ShapeDtypeStruct(shapes["wg"][0], BF)]
        out_specs = [V, V, V, A]
        in_specs = [V] * 5 + [A, V]
    scratch = [pltpu.VMEM(*sd) for sd in shapes.values()] + [pltpu.VMEM((tt.shape[1], 128), jnp.int32), dma((12,)), dma((12,)), dma, dma]
    if custom:
        ns, n2 = 2 * (nz - 1) + 4, 4 + 2 * nz
        vb = lambda *sh: pltpu.VMEM(sh, BF)
        scratch += [vb(1, nz, 4, R, 128), pltpu.VMEM((R, 384), F32), vb(1, nz, 4, R, 128), dma((12, ns)), dma((12, ns)), dma((1, ns)), dma((1, ns)),
                    dma((12, n2)), dma((12, n2)), dma((1, n2)), dma((1, n2))] + [vb(12, nz, R, 384)] * 5 + [vb(1, nz, R, 128)] * 5
    return pl.pallas_call(
        functools.partial(layer_body, nb, custom, tuple(shapes)),
        out_shape=out_shape, in_specs=in_specs, out_specs=out_specs, scratch_shapes=scratch,
        compiler_params=pltpu.CompilerParams(collective_id=0, has_side_effects=True, vmem_limit_bytes=int(63.9 * (1 << 20))),
    )(*args)


def on_device(tokens, attn_gain, qkv_weight, out_weight, ffn_gain, up_weight, down_weight, cotangent, segment, cluster, top_keys):
    nb = lax.axis_size("batch")
    R = qkv_weight.shape[0]
    custom = R % 16 == 0 and nb % 4 == 0
    x, ct = tokens[0], cotangent[0]
    tt = top_keys[0].transpose(0, 2, 1)
    if custom:
        ws = (qkv_weight.transpose(1, 0, 2), out_weight.T, up_weight, down_weight.T, attn_gain[None], ffn_gain[None])
    else:
        w = pack(qkv_weight, out_weight, up_weight, down_weight)
        gw = jnp.pad(jnp.stack([attn_gain, ffn_gain], 1), ((0, 0), (0, 126)))
        ws = (lax.all_gather(w, "batch", axis=1, tiled=True), lax.all_gather(gw, "batch", axis=0, tiled=True))
    y, tg, gg, *S = layer(nb, custom, x, ct, segment, cluster[0][:, None, :], tt, *ws)
    if custom:
        y, tg, qg, og, ug, dg, g1, g2 = finish(y, tg, *S, gg)
        return y[None], tg[None], g1[0], qg.transpose(1, 0, 2), og.T, g2[0], ug, dg.T
    S = lax.psum_scatter(S[0].astype(F32), "batch", scatter_dimension=1, tiled=True)
    g = lax.psum_scatter(gg, "batch", scatter_dimension=1, tiled=True)
    cat = lambda a: a.transpose(1, 0, 2).reshape(R, -1)
    qg = S[0:3].reshape(3, R, 3, 128).transpose(1, 2, 0, 3).reshape(R, 3, 384)
    return y[None], tg[None], g[0], qg, S[3].T, g[1], cat(S[4:8]), cat(S[12:16]).T


def pack(q, o, u, d):
    R = q.shape[0]
    qp = q.reshape(R, 3, 3, 128).transpose(2, 0, 1, 3).reshape(3, R, 384)
    up = u.reshape(R, 4, 384).transpose(1, 0, 2)
    dn = d.T.reshape(R, 4, 384).transpose(1, 0, 2)
    return jnp.concatenate([qp, o.T[None], up, dn], 0)


def solution(mesh):
    in_specs = (P("batch", None, None), P("batch"), P("batch", None, "head"), P("head", "batch"), P("batch"), P("batch", "head"), P("head", "batch"), P("batch", None, None), P("batch", None), P("batch", "head", None), P("batch", "head", None, None))
    out_specs = (P("batch", "head", None), P("batch", "head", None), P("batch"), P("batch", None, "head"), P("head", "batch"), P("batch"), P("batch", "head"), P("head", "batch"))
    return jax.shard_map(on_device, mesh=mesh, in_specs=in_specs, out_specs=out_specs, check_vma=False)
```

time: 223 us -> 194 us (0.87)
  local copies, waits for them, and re-layouts: 14.1 us -> 0 us
  Pallas kernels: 207 us -> 193 us
    pallas_call x2, Pallas kernels: 207 us -> 193 us  [the longest x1 189 us: layer(): pl.pallas_call(functools.partial(layer_body, nb, custom, tuple(shapes)),...]
    reshape x6 -> x0, local copies, waits for them, and re-layouts: 3.39 us -> none  [the longest x2 1.47 us: on_device(): cat = lambda a: a.transpose(1, 0, 2).reshape(R, -1)]
    unnamed x9 -> x0, local copies, waits for them, and re-layouts: 3.13 us -> none
    transpose x4 -> x0, local copies, waits for them, and re-layouts: 2.81 us -> none  [the longest x1 1.52 us: on_device(): return (y[None], tg[None], g1, qg, S[3].T, g2, cat(S[4:8]), cat(S[8:12]).T)]
    slice x2 -> x0, local copies, waits for them, and re-layouts: 2.46 us -> none  [the longest x1 1.51 us: on_device(): g1, g2 = (gg[0, :, 0], gg[0, :, 1])]
where the time goes in v3:
time: 194 us
  Pallas kernels  193 us (99%)
    pallas_call x1, Pallas kernels, layer(): pl.pallas_call(functools.partial(layer_body, nb, custom, tuple(shapes)),...  189 us
    pallas_call x1, Pallas kernels, finish(): pl.pallas_call(finish_body, out_shape=[jax.ShapeDtypeStruct(a.shape, a.dt...  4.44 us

profile of v3, /device:TPU:0, one launch (start us, length us, event | category | flops | bytes accessed | tf_op | source)
XLA Modules:
  0.0 194.0 jit_solution(2538021613626360348)
XLA Ops:
  0.6 188.7 %shard_map.170 = (bf16[512,768]{1,0:T(8,128)(2,1)}, f32[512,768]{1,0:T(8,128)}, f32[1,48,128]{2,1,0:T(8,128)}, f32[3,48,384]{2,1,0:T(8,128)}, f32[48,384]{1,0:T(...) custom-call(bf16[1024,768]{1,0:T(8,128)(2,1)} %bitcast.18, bf16[1024,768]{1,0:T(8,128)(2,1)} %bitcast.19, ...), custom_call_target="tpu_custom_call" | custom-call | tf_op jit(solution)/shard_map/pallas_call | solution.py:808
  189.4 4.4 %shard_map.171 = (bf16[512,768]{1,0:T(8,128)(2,1)}, f32[512,768]{1,0:T(8,128)}, f32[3,48,384]{2,1,0:T(8,128)}, f32[48,384]{1,0:T(8,128)}, f32[48,1536]{1,0:T(8,1...) custom-call(bf16[512,768]{1,0:T(8,128)(2,1)} %get-tuple-element.23.refs_0_, ...), custom_call_target="tpu_custom_call" | custom-call | tf_op jit(solution)/shard_map/pallas_call | solution.py:459

commit v4 on v3

--- a/solution.py
+++ b/solution.py
@@ -132,6 +132,18 @@
         def last(p):
             self.zk(p,nz-1); self.x0(p)
         return [self.z0]+[functools.partial(lambda d,p:self.zk(p,d),d) for d in range(1,nz-1)]+[last]+[NOP]+[self.x1]+[NOP]+[self.x2]
+
+class PlaneFirst(Gather):
+    def cz(self,p,zz,k,dev):
+        s=self.g.at[p,zz]
+        return rc(s,s,self.ss.at[p,k],self.rs.at[p,k],dev)
+    def cb(self,p,r,k,dev):
+        s=self.g.at[p,self.pc.z,r]
+        return rc(s,s,self.ss.at[p,self.n+k],self.rs.at[p,self.n+k],dev)
+    def ch(self,p,r,lo,k,dev):
+        n=self.g.shape[3]; h=(n//32)*16
+        s=self.g.at[p,self.pc.z,r,pl.ds(0,h)] if lo else self.g.at[p,self.pc.z,r,pl.ds(h,n-h)]
+        return rc(s,s,self.ss.at[p,self.n+k],self.rs.at[p,self.n+k],dev)
 
 class Scatter:
     def __init__(self, pc, g, d, rx, ry, ru, rd, ss, rs, slot=lambda p: p):
@@ -499,17 +511,27 @@
         G, Gg = Gather(pc, wg, ss, rs), Gather(pc, gg, gss, grs)
         S = Scatter(pc, wg, *land, ss2, rs2, slot=lambda p: p - 4 if isinstance(p, int) and p >= 12 else p if isinstance(p, int) else jnp.where(p >= 12, p - 4, p))
         Sg = Scatter(pc, gbuf, *gland, gss2, grs2)
+        Gp = PlaneFirst(pc, wg, ss, rs)
         m = pc.nz - 1
-        line = [(d, functools.partial(lambda d, p: G.zk(p, d), d), 0, 12) for d in range(1, m)]
 
         def last(p):
             G.zk(p, m)
             G.x0(p)
-        gather = [(m + 3, G.x2, 3, 12), (m + 2, G.x2, 0, 3), (m + 2, G.x1, 3, 12), (m + 1, G.x1, 0, 3), (m, last, 0, 12)] + line[::-1] + [(0, G.z0, 0, 12)]
+
+        def turn(p):
+            Gp.x2(p)
+            Gp.z0(p)
+        line = lambda g, off: [(off + d, functools.partial(lambda d, p: g.zk(p, d), d)) for d in range(1, m)][::-1]
+        nine = lambda k: k + k // 3
+        three = lambda k: k + 3
+        rest = list(range(1, 9))
+        gather = [(m + 2, G.x2, [0], nine), (m + 1, G.x1, [0], nine), (m + 3, G.x2, rest, nine), (m + 2, G.x1, rest, nine)]
+        gather += [(e, fn, list(range(9)), nine) for e, fn in [(m, last)] + line(G, 0) + [(0, G.z0)]]
+        gather += [(e, fn, [0, 4, 8], three) for e, fn in [(m + 3, lambda p: Gp.zk(p, m))] + line(Gp, 3) + [(2, turn), (1, Gp.x1), (0, Gp.x0)]]
         gsteps = [Gg.z0] + [functools.partial(lambda d: Gg.zk(0, d), d) for d in range(1, m)] + [None, Gg.x1, Gg.x2]
         ssteps = S.steps(lambda p: place_sum(p, tot, out_s), tot)
         tails = Sg.tight(out_g)
-        starts = {14: 12, 15: 13, 16: 14, 17: 15, 19: 4, 20: 5, 21: 6, 22: 7, 23: 3, 24: 0, 26: 1, 28: 2}
+        starts = {13: 12, 14: 13, 15: 14, 16: 15, 18: 4, 19: 5, 20: 6, 21: 7, 22: 3, 24: 0, 26: 1, 28: 2}
 
         def tick(t, span=None):
             fixed = isinstance(t, int)
@@ -525,11 +547,13 @@
                 ok = functools.reduce(jnp.logical_or, [u == k for k in hits])
                 part = functools.reduce(lambda a, k: jnp.where(u == k, starts[k], a), hits, 0)
                 pl.when(ok)(lambda i=i, part=part: ssteps[i](part))
-            for off, fn, lo, hi in gather:
-                if not any(lo <= u - off < hi for u in ts):
+            for off, fn, at, to in gather:
+                hits = [u - off for u in ts if u - off in at]
+                if not hits:
                     continue
-                p = t - off
-                pick(None, True if fixed else (p >= lo) & (p < hi), lambda fn=fn, p=p: fn(p))
+                u = t - off
+                ok = True if fixed else functools.reduce(jnp.logical_or, [u == k for k in hits])
+                pick(None, ok, lambda fn=fn, p=to(u): fn(p))
             if fixed and t < len(gsteps):
                 if t == m:
                     Gg.zk(0, m)
@@ -622,20 +646,15 @@
             act[q, rows_of(i), :] = a.astype(BF)
             dg[q, rows_of(i), :] = d.astype(BF)
 
-    pl.loop(0, 2)(up)
+    def down_grad(q):
+        up(q)
+        put(12 + q, aT[...], act[q])
+
+    pl.loop(0, 2)(down_grad)
     tick(13)
-    pl.loop(2, 4)(up)
-
-    def down_grad(q):
-        put(12 + q, aT[...], act[q])
-
-    pl.loop(0, 2)(down_grad)
+    pl.loop(2, 4)(down_grad)
     tick(14)
-    pl.loop(2, 4)(down_grad)
-    tick(15)
     transpose_into(n2)
-    tick(16)
-    tick(17)
 
     def part(i):
         acc = dot(act[0, rows_of(i), :], flat(wg, 8), NT)
@@ -647,6 +666,8 @@
     def _(i):
         eb[rows_of(i), :] = part((1 - pc.h) * nh + i).astype(BF)
         send(4, eb, fr, i).start()
+
+    tick(15)
 
     @pl.loop(0, 4)
     def _(q):
@@ -661,11 +682,15 @@
         send(4, eb, fr, i).wait()
         y[rows_of(i), :] = (hid[rows_of(pc.h * nh + i), :] + (acc + fr[rows_of(i), :].astype(F32))).astype(BF)
 
-    tick(18)
+    tick(16)
     if custom:
-        @pl.loop(0, 12)
-        def _(p):
-            G.drain(p)
+        @pl.loop(0, 9)
+        def _(k):
+            G.drain(nine(k))
+
+        @pl.loop(0, 3)
+        def _(k):
+            Gp.drain(4 * k + 3)
         Gg.drain(0)
 
     @tiles(nt)
@@ -679,9 +704,11 @@
     def up_grad(q):
         put(4 + q, aT[...], dg[q])
 
+    tick(17)
     pl.loop(0, 2)(up_grad)
+    tick(18)
+    pl.loop(2, 4)(up_grad)
     tick(19)
-    pl.loop(2, 4)(up_grad)
     gacc[...] = jnp.zeros_like(gacc)
     gat = n2
 

time: 194 us -> 185 us (0.954)
  Pallas kernels: 193 us -> 184 us
    pallas_call x1, Pallas kernels: 189 us -> 179 us  [layer(): pl.pallas_call(functools.partial(layer_body, nb, custom, tuple(shapes)),...]
where the time goes in v4:
time: 185 us; the launch traced here: 184 us
  Pallas kernels  184 us (99%)
    pallas_call x1, Pallas kernels, layer(): pl.pallas_call(functools.partial(layer_body, nb, custom, tuple(shapes)),...  179 us
    pallas_call x1, Pallas kernels, finish(): pl.pallas_call(finish_body, out_shape=[jax.ShapeDtypeStruct(a.shape, a.dt...  4.44 us

profile of v4, /device:TPU:0, one launch (start us, length us, event | category | flops | bytes accessed | tf_op | source)
XLA Modules:
  0.0 184.4 jit_solution(17279786492175478773)
XLA Ops:
  0.6 179.2 %shard_map.170 = (bf16[512,768]{1,0:T(8,128)(2,1)}, f32[512,768]{1,0:T(8,128)}, f32[1,48,128]{2,1,0:T(8,128)}, f32[3,48,384]{2,1,0:T(8,128)}, f32[48,384]{1,0:T(...) custom-call(bf16[1024,768]{1,0:T(8,128)(2,1)} %bitcast.18, bf16[1024,768]{1,0:T(8,128)(2,1)} %bitcast.19, ...), custom_call_target="tpu_custom_call" | custom-call | tf_op jit(solution)/shard_map/pallas_call | solution.py:835
  179.8 4.4 %shard_map.171 = (bf16[512,768]{1,0:T(8,128)(2,1)}, f32[512,768]{1,0:T(8,128)}, f32[3,48,384]{2,1,0:T(8,128)}, f32[48,384]{1,0:T(8,128)}, f32[48,1536]{1,0:T(8,1...) custom-call(bf16[512,768]{1,0:T(8,128)(2,1)} %get-tuple-element.23.refs_0_, ...), custom_call_target="tpu_custom_call" | custom-call | tf_op jit(solution)/shard_map/pallas_call | solution.py:471

commit v5 on v4

--- a/solution.py
+++ b/solution.py
@@ -41,8 +41,8 @@
     return m,n
 
 
-TQ = 256
-TJ = 256
+TQ = 512
+TJ = 512
 MESH=pl.DeviceIdType.MESH
 
 
@@ -275,36 +275,48 @@
     return jnp.where(cl[hh] == sub((128, L)), 1.0, 0.0).astype(BF)
 
 
-def fwd_head(p, h, qkv, mb, cl, n_s, seg, qaug, kaug, att, ex, prob_o):
-    odd = h == 1
-    hh = 2 * p + h
+def pair_members(cl, p):
+    return jnp.concatenate([members(cl, 2 * p), members(cl, 2 * p + 1)], 0)
+
+
+def pair_own():
+    return (lane((256, 128)) >= 64) == (sub((256, 128)) >= 128)
+
+
+def fwd_clusters(p, qkv, cl, n_s, seg, prob_o):
     q = qkv[p, :, 0:128]
     k = qkv[p, :, 128:256]
     v = qkv[p, :, 256:384]
+    own = pair_own()
+    mt = pair_members(cl, p)
+    cnt = jnp.maximum(jnp.sum(mt.astype(F32), axis=1, keepdims=True), 1.0)
+    cen = jnp.where(own, dot(mt, q) / cnt, 0.0).astype(BF)
+    s = dot((cen.astype(F32) * 0.125).astype(BF), k, NT)
+    top = jnp.concatenate([jnp.transpose(n_s[2 * p + h]).astype(F32) for h in range(2)], 0) == 0.0
+    c = sub((256, 1))
+    cm = lax.rem(jnp.where(c < 128, c, c - 128), jnp.int32(10))
+    s = jnp.where(seg[...] == cm, s, -BIG)
+    e = jnp.exp(s - jnp.max(s, axis=1, keepdims=True))
+    prob = e / jnp.sum(e, axis=1, keepdims=True)
+    mass = jnp.sum(jnp.where(top, prob, 0.0), axis=1, keepdims=True)
+    signed = jnp.where(top, -prob, prob).astype(BF)
+    prob_o[2 * p] = signed[0:128]
+    prob_o[2 * p + 1] = signed[128:256]
+    rest = dot(jnp.where(top, 0.0, prob).astype(BF), v)
+    rh, rl = split2(jnp.where(own, rest, jnp.broadcast_to(mass, (256, 128))))
+    rr = jnp.concatenate([rh, rl], 1)
+    return rr[0:128], rr[128:256]
+
+
+def fwd_head(p, h, rr, qkv, mb, n_s, qaug, kaug, att, ex):
+    odd = h == 1
+    hh = 2 * p + h
+    k = qkv[p, :, 128:256]
     ln = lane((L, 128))
     mine = (ln >= 64) if odd else (ln < 64)
-    lc = lane((128, 128))
-    minec = (lc >= 64) if odd else (lc < 64)
     zero = jnp.zeros((), BF)
-    qm = jnp.where(mine, q, zero)
-    vaug = jnp.where(mine, v, jnp.ones((), BF))
-    mt = members(cl, hh)
-    top = jnp.transpose(n_s[hh]).astype(F32) == 0.0
-    cnt = jnp.maximum(jnp.sum(mt.astype(F32), axis=1, keepdims=True), 1.0)
-    cen = (dot(mt, qm) / cnt).astype(BF)
-    cs = (cen.astype(F32) * 0.125).astype(BF)
-    s = dot(cs, k, NT)
-    cm = lax.rem(sub((128, 1)), jnp.int32(10))
-    s = jnp.where(seg[...] == cm, s, -BIG)
-    mx = jnp.max(s, axis=1, keepdims=True)
-    e = jnp.exp(s - mx)
-    prob = e / jnp.sum(e, axis=1, keepdims=True)
-    mass = jnp.sum(jnp.where(top, prob, 0.0), axis=1, keepdims=True)
-    prob_o[hh] = jnp.where(top, -prob, prob).astype(BF)
-    rest = dot(jnp.where(top, 0.0, prob).astype(BF), v)
-    rh, rl = split2(jnp.where(minec, rest, jnp.broadcast_to(mass, (128, 128))))
-    rr = jnp.concatenate([rh, rl], 1)
-    qaug[:, :128] = (qm.astype(F32) * 0.125).astype(BF)
+    vaug = jnp.where(mine, qkv[p, :, 256:384], jnp.ones((), BF))
+    qaug[:, :128] = (jnp.where(mine, qkv[p, :, 0:128], zero).astype(F32) * 0.125).astype(BF)
     qaug[:, 128:] = mb[hh]
     kaug[:, :128] = k
     kaug[:, 128:] = n_s[hh]
@@ -356,78 +368,81 @@
     gg[0, pc.z, pc.r] = jnp.where(ln == 0, as_column(ga[...]), jnp.where(ln == 1, as_column(gf[...]), 0.0)).astype(BF)
 
 
-def bwd_head(p, h, cl, s, qaug, kaug, gaug, vaug, dq_o, dk_o, dv_o, dqt):
-    qkv, g, ex = s["qkv"], s["gatt"], s["ex"]
-    hh = 2 * p + h
+def bwd_clusters(p, cl, s, gaugs, dq_o, dk_o, dv_o):
+    qkv = s["qkv"]
     cols = pl.ds(pl.multiple_of(p * 128, 128), 128)
     qv = qkv[p, :, 0:128]
     kv = qkv[p, :, 128:256]
     vv = qkv[p, :, 256:384]
-    gv = g[:, cols]
+    gv = s["gatt"][:, cols]
+    ln = lane((L, 128))
+    lc = lane((256, 128))
+    row = sub((256, 128))
+    own = pair_own()
+    prod = gv.astype(F32) * s["ex"][:, cols].astype(F32)
+    dots = jnp.zeros((L, 128), F32)
+    for h in range(2):
+        mine = (ln >= 64) if h else (ln < 64)
+        o = 0 if h else 64
+        three = [a.astype(F32) for a in split3(jnp.sum(jnp.where(mine, prod, 0.0), axis=1, keepdims=True))]
+        ga = jnp.where(mine, gv.astype(F32), 0.0)
+        for i, a in enumerate(three):
+            ga = jnp.where(ln == o + i, a, ga)
+            dots = jnp.where(ln == 3 * h + i, a, dots)
+        gaugs[h][...] = ga.astype(BF)
+    mt = pair_members(cl, p)
+    cnt = jnp.maximum(jnp.sum(mt.astype(F32), axis=1, keepdims=True), 1.0)
+    cq = dot(mt, jnp.concatenate([qv, gv], 1))
+    cen = jnp.where(own, cq[:, 0:128] / cnt, 0.0).astype(BF)
+    cs = (cen.astype(F32) * 0.125).astype(BF)
+    grest = jnp.where(own, cq[:, 128:256], 0.0).astype(BF)
+    gm = dot(mt, dots.astype(BF))
+    lo = jnp.where(row >= 128, 3, 0)
+    gmass = jnp.sum(jnp.where((lc >= lo) & (lc < lo + 3), gm, 0.0), axis=1, keepdims=True)
+    signed = jnp.concatenate([s["prob"][2 * p], s["prob"][2 * p + 1]], 0).astype(F32)
+    top = signed < 0.0
+    prob = jnp.abs(signed)
+    gp = jnp.where(top, gmass, dot(grest, vv, NT))
+    gs = (prob * (gp - jnp.sum(prob * gp, axis=1, keepdims=True))).astype(BF)
+    rw = jnp.where(top, 0.0, prob).astype(BF)
+    gcen = jnp.where(own, dot(gs, kv) / cnt, 0.0)
+    gh, gl = split2(gcen)
+    dk_o[...] = dot(jnp.transpose(gs), cs)
+    dv_o[...] = dot(jnp.transpose(rw), grest)
+    zero = jnp.zeros((), BF)
+    two = jnp.concatenate([jnp.where(ln < 100, s["mb"][2 * p + h], zero) for h in range(2)], 1)
+    dd = dot(two, jnp.concatenate([gh, gl], 1))
+    dq_o[...] = dd[:, :128] + dd[:, 128:]
+
+
+def bwd_head(p, h, s, qaug, kaug, gaug, vaug, dk_o, dv_o, dqt):
+    qkv = s["qkv"]
+    hh = 2 * p + h
+    cols = pl.ds(pl.multiple_of(p * 128, 128), 128)
+    kv = qkv[p, :, 128:256]
     ln = lane((L, 128))
     zero = jnp.zeros((), BF)
-    lc = lane((128, 128))
-    kT = jnp.transpose(kv)
-    prod = gv.astype(F32) * ex[:, cols].astype(F32)
     mine = (ln >= 64) if h else (ln < 64)
-    minec = (lc >= 64) if h else (lc < 64)
     o = 0 if h else 64
-    r = jnp.sum(jnp.where(mine, prod, 0.0), axis=1, keepdims=True)
-    h3, m3, l3 = split3(r)
-    gm = jnp.where(mine, gv, zero)
-    ga = jnp.where(ln == o, h3.astype(F32), jnp.where(ln == o + 1, m3.astype(F32), jnp.where(ln == o + 2, l3.astype(F32), gm.astype(F32)))).astype(BF)
-    gaug[...] = ga
-    vaug[...] = jnp.where(mine, vv, jnp.where((ln >= o) & (ln < o + 3), jnp.full((), -1.0, BF), zero))
-    qm = jnp.where(mine, qv, zero)
-    qs = (qm.astype(F32) * 0.125).astype(BF)
+    gm = jnp.where(mine, s["gatt"][:, cols], zero)
+    vaug[...] = jnp.where(mine, qkv[p, :, 256:384], jnp.where((ln >= o) & (ln < o + 3), jnp.full((), -1.0, BF), zero))
+    qs = (jnp.where(mine, qkv[p, :, 0:128], zero).astype(F32) * 0.125).astype(BF)
     qaug[:, :128] = qs
     qaug[:, 128:] = s["mb"][hh]
     kaug[:, :128] = kv
     kaug[:, 128:] = s["ns"][hh]
-    mt = members(cl, hh)
-    signed = s["prob"][hh].astype(F32)
-    top = signed < 0.0
-    prob = jnp.abs(signed)
-    cnt = jnp.maximum(jnp.sum(mt.astype(F32), axis=1, keepdims=True), 1.0)
-    cen = (dot(mt, qm) / cnt).astype(BF)
-    cs = (cen.astype(F32) * 0.125).astype(BF)
-    gr = dot(mt, ga)
-    gmass = jnp.sum(jnp.where((lc >= o) & (lc < o + 3), gr, 0.0), axis=1, keepdims=True)
-    grest = jnp.where(minec, gr, 0.0).astype(BF)
-    gp = jnp.where(top, gmass, dot(grest, vv, NT))
-    gs = (prob * (gp - jnp.sum(prob * gp, axis=1, keepdims=True))).astype(BF)
-    rw = jnp.where(top, 0.0, prob).astype(BF)
-    gcen = dot(gs, jnp.where(mine, kv, zero)) / cnt
-    gh, gl = split2(gcen)
-    gg = jnp.concatenate([gh, gl], 1)
-    gsT = jnp.transpose(gs)
-    rwT = jnp.transpose(rw)
-    kTh = kT[64 * h:64 * h + 64]
+    kTh = jnp.transpose(kv)[64 * h:64 * h + 64]
     for t in range(L // TJ):
         sl = pl.ds(t * TJ, TJ)
-        st = dot(kaug[sl, :], qaug[...], NT)
-        pr = jnp.exp(st)
-        dp = dot(vaug[sl, :], gaug[...], NT)
-        ds = (pr * dp).astype(BF)
-        dv = dot(pr.astype(BF), gm) + dot(rwT[t * TJ:(t + 1) * TJ], grest)
-        dk = dot(ds, qs) + dot(gsT[t * TJ:(t + 1) * TJ], cs)
-        if h == 0:
-            dv_o[sl, :] = dv
-            dk_o[sl, :] = dk
-        else:
-            dv_o[sl, :] += dv
-            dk_o[sl, :] += dk
+        pr = jnp.exp(dot(kaug[sl, :], qaug[...], NT))
+        ds = (pr * dot(vaug[sl, :], gaug[...], NT)).astype(BF)
+        dv_o[sl, :] += dot(pr.astype(BF), gm)
+        dk_o[sl, :] += dot(ds, qs)
         dqp = dot(kTh[:, t * TJ:(t + 1) * TJ], ds)
         if t == 0:
             dqt[64 * h:64 * h + 64, :] = dqp
         else:
             dqt[64 * h:64 * h + 64, :] += dqp
-    dd = dot(jnp.where(ln < 100, s["mb"][hh], zero), gg)
-    dd = dd[:, :128] + dd[:, 128:]
-    if h == 0:
-        dq_o[...] = dd
-    else:
-        dq_o[...] += dd
 
 
 def place_sum(p, tot, outs):
@@ -485,8 +500,8 @@
         "gr": f(8, 768), "n1": b(L, 768), "qkv": b(3, L, 384), "att": b(L, 384), "ex": b(L, 384), "mb": b(6, L, 128),
         "ns": b(6, L, 128), "prob": b(6, 128, L), "hid": f(L, 768), "n2": b(L, 768), "act": b(4, L, 384), "dg": b(4, L, 384),
         "aT": b(768, L), "ghs": f(L // 2, 768), "eb": b(L, 768), "er": b(L, 768), "fr": b(L // 2, 768), "gatt": b(L, 384),
-        "dqkv": b(L, 384), "qaug": b(L, 256), "kaug": b(L, 256), "gaug": b(L, 128), "vaug": b(L, 128),
-        "dqs": f(L, 128), "dks": f(L, 128), "dvs": f(L, 128), "dqt": f(128, L), "gacc": f(8, 768), "vb": f(8, 768), "vr": f(8, 768),
+        "dqkv": b(L, 384), "qaug": b(L, 256), "kaug": b(L, 256), "gaug": b(L, 128), "gaug1": b(L, 128), "vaug": b(L, 128),
+        "dqs": f(L, 128), "dks": f(L, 128), "dvs": f(L, 128), "dqt": f(128, L), "gacc": f(8, 768),
         "wg": b(*wide),
     }
 
@@ -506,7 +521,7 @@
     half, nh, nt = L // 2, L // 2 // RT, L // RT
 
     if custom:
-        gg, tot, gbuf, ss, rs, gss, grs, ss2, rs2, gss2, grs2 = take(11)
+        gg, tot, gbuf, ss, rs, gss, grs, ss2, rs2, gss2, grs2, gown, gtwin = take(13)
         land, gland = take(5), take(5)
         G, Gg = Gather(pc, wg, ss, rs), Gather(pc, gg, gss, grs)
         S = Scatter(pc, wg, *land, ss2, rs2, slot=lambda p: p - 4 if isinstance(p, int) and p >= 12 else p if isinstance(p, int) else jnp.where(p >= 12, p - 4, p))
@@ -530,8 +545,8 @@
         gather += [(e, fn, [0, 4, 8], three) for e, fn in [(m + 3, lambda p: Gp.zk(p, m))] + line(Gp, 3) + [(2, turn), (1, Gp.x1), (0, Gp.x0)]]
         gsteps = [Gg.z0] + [functools.partial(lambda d: Gg.zk(0, d), d) for d in range(1, m)] + [None, Gg.x1, Gg.x2]
         ssteps = S.steps(lambda p: place_sum(p, tot, out_s), tot)
-        tails = Sg.tight(out_g)
-        starts = {13: 12, 14: 13, 15: 14, 16: 15, 18: 4, 19: 5, 20: 6, 21: 7, 22: 3, 24: 0, 26: 1, 28: 2}
+        tails = Sg.tight(gown)
+        starts = {13: 12, 14: 13, 15: 14, 16: 15, 17: 4, 18: 5, 19: 6, 20: 7, 21: 3, 22: 0, 23: 1, 25: 2}
 
         def tick(t, span=None):
             fixed = isinstance(t, int)
@@ -617,9 +632,10 @@
         @tiles(nt)
         def _(i):
             qkv[p, rows_of(i), :] = dot(n1[rows_of(i), :], flat(wg, p)).astype(BF)
+        rr = fwd_clusters(p, qkv, cl, s["ns"], seg, s["prob"])
         for h in range(2):
             tick(6 + 2 * p + h, (6 + h, 12, 2))
-            fwd_head(p, h, qkv, s["mb"], cl, s["ns"], seg, s["qaug"], s["kaug"], att, ex, s["prob"])
+            fwd_head(p, h, rr[h], qkv, s["mb"], s["ns"], s["qaug"], s["kaug"], att, ex)
 
     def send(k, src, dst, i):
         return twin_copy(pc, src.at[rows_of(i)], dst.at[rows_of(i)], es.at[k + i], ers.at[k + i])
@@ -704,11 +720,8 @@
     def up_grad(q):
         put(4 + q, aT[...], dg[q])
 
+    pl.loop(0, 4)(up_grad)
     tick(17)
-    pl.loop(0, 2)(up_grad)
-    tick(18)
-    pl.loop(2, 4)(up_grad)
-    tick(19)
     gacc[...] = jnp.zeros_like(gacc)
     gat = n2
 
@@ -718,7 +731,6 @@
         send(6, eb, er, i).wait()
         gn = eb[r, :].astype(F32) + er[r, :].astype(F32)
         n, inv = norm_rows(hid[r, :])
-        gacc[1:2, :] += jnp.sum(gn * n, axis=0, keepdims=True)
         a = gn * gr[1:2, :]
         back = (a - jnp.mean(a, axis=1, keepdims=True) - n * jnp.mean(a * n, axis=1, keepdims=True)) * inv
         gh = ct[r, :].astype(F32) + back
@@ -727,8 +739,9 @@
         @pl.when((i >= pc.h * nh) & (i < pc.h * nh + nh))
         def _():
             s["ghs"][rows_of(i - pc.h * nh), :] = gh
-
-    tick(20)
+            gacc[1:2, :] += jnp.sum(gn * n, axis=0, keepdims=True)
+
+    tick(18)
 
     @tiles(nt)
     def _(i):
@@ -736,17 +749,17 @@
 
     transpose_into(gat)
     put(3, aT[...], att[...])
-    tick(21)
+    tick(19)
     transpose_into(n1)
-    tick(22)
     nacc = hid
     dqkv = s["dqkv"]
 
     @pl.loop(0, 3)
     def _(p):
-        bwd_head(p, 0, cl, s, s["qaug"], s["kaug"], s["gaug"], s["vaug"], s["dqs"], s["dks"], s["dvs"], s["dqt"])
-        tick(23 + 2 * p, (23, 29, 2))
-        bwd_head(p, 1, cl, s, s["qaug"], s["kaug"], s["gaug"], s["vaug"], s["dqs"], s["dks"], s["dvs"], s["dqt"])
+        bwd_clusters(p, cl, s, (s["gaug"], s["gaug1"]), s["dqs"], s["dks"], s["dvs"])
+        bwd_head(p, 0, s, s["qaug"], s["kaug"], s["gaug"], s["vaug"], s["dks"], s["dvs"], s["dqt"])
+        tick(20 + 2 * p, (20, 26, 2))
+        bwd_head(p, 1, s, s["qaug"], s["kaug"], s["gaug1"], s["vaug"], s["dks"], s["dvs"], s["dqt"])
         dqkv[:, 0:128] = ((s["dqs"][...] + jnp.transpose(s["dqt"][...])) * 0.125).astype(BF)
         dqkv[:, 128:256] = s["dks"][...].astype(BF)
         dqkv[:, 256:384] = s["dvs"][...].astype(BF)
@@ -763,14 +776,29 @@
             def _():
                 nacc[rows_of(i), :] += v
         put(p, aT[...], dqkv[...])
-        tick(24 + 2 * p, (24, 30, 2))
+        tick(21 + 2 * p, (21, 27, 2))
 
     @tiles(nh)
     def _(i):
         eb[rows_of(i), :] = nacc[rows_of((1 - pc.h) * nh + i), :].astype(BF)
         send(10, eb, fr, i).start()
 
-    tick(29)
+    @tiles(nt)
+    def _(i):
+        n = norm_rows(x[rows_of(i), :].astype(F32))[0]
+        gacc[0:1, :] += jnp.sum(nacc[rows_of(i), :] * n, axis=0, keepdims=True)
+
+    if custom:
+        wide = jnp.concatenate([gacc[...], jnp.zeros((120, 768), F32)], 0)
+        gbuf[0] = jnp.transpose(wide).astype(BF).reshape(gbuf.shape[1:])
+
+    def late(t):
+        tick(t)
+        if custom and t - 26 < len(tails):
+            tails[t - 26](0)
+
+    late(26)
+    late(27)
 
     @tiles(nh)
     def _(i):
@@ -778,34 +806,27 @@
         send(10, eb, fr, i).wait()
         gn = nacc[rows_of(pc.h * nh + i), :].astype(BF).astype(F32) + fr[r, :].astype(F32)
         n, inv = norm_rows(x[rows_of(pc.h * nh + i), :].astype(F32))
-        gacc[0:1, :] += jnp.sum(gn * n, axis=0, keepdims=True)
         a = gn * gr[0:1, :]
         back = (a - jnp.mean(a, axis=1, keepdims=True) - n * jnp.mean(a * n, axis=1, keepdims=True)) * inv
         tg[r, :] = s["ghs"][r, :] + back
 
-    s["vb"][...] = gacc[...]
-    cv = twin_copy(pc, s["vb"], s["vr"], vs, vrs)
-    cv.start()
-    tick(30)
-    cv.wait()
-    one = gacc[0:1, :] + s["vr"][0:1, :]
-    both = jnp.where(sub((8, 768)) == 0, jnp.broadcast_to(one, (8, 768)), gacc[...])
-    if custom:
-        wide = jnp.concatenate([both, jnp.zeros((120, 768), F32)], 0)
-        gbuf[0] = jnp.transpose(wide).astype(BF).reshape(gbuf.shape[1:])
-        for t in range(31, max(28 + len(ssteps), 31 + len(tails))):
-            tick(t)
-            if t - 31 < len(tails):
-                tails[t - 31](0)
+    if custom:
+        for t in range(28, max(25 + len(ssteps), 26 + len(tails))):
+            late(t)
+            if t == 25 + len(tails):
+                cv = twin_copy(pc, gown, gtwin, vs, vrs)
+                cv.start()
 
         @pl.loop(0, 12)
         def _(i):
             S.drain(jnp.where(i < 8, i, i + 4))
         Sg.drain(0)
+        cv.wait()
+        out_g[0] = gown[0] + gtwin[0]
     else:
         c = pltpu.make_async_copy(wg, out_s, vs)
         c.start()
-        out_g[...] = both
+        out_g[...] = gacc[...]
         c.wait()
 
 
@@ -831,7 +852,7 @@
         ns, n2 = 2 * (nz - 1) + 4, 4 + 2 * nz
         vb = lambda *sh: pltpu.VMEM(sh, BF)
         scratch += [vb(1, nz, 4, R, 128), pltpu.VMEM((R, 384), F32), vb(1, nz, 4, R, 128), dma((12, ns)), dma((12, ns)), dma((1, ns)), dma((1, ns)),
-                    dma((12, n2)), dma((12, n2)), dma((1, n2)), dma((1, n2))] + [vb(12, nz, R, 384)] * 5 + [vb(1, nz, R, 128)] * 5
+                    dma((12, n2)), dma((12, n2)), dma((1, n2)), dma((1, n2)), pltpu.VMEM((1, R, 128), F32), pltpu.VMEM((1, R, 128), F32)] + [vb(12, nz, R, 384)] * 5 + [vb(1, nz, R, 128)] * 5
     return pl.pallas_call(
         functools.partial(layer_body, nb, custom, tuple(shapes)),
         out_shape=out_shape, in_specs=in_specs, out_specs=out_specs, scratch_shapes=scratch,
@@ -856,7 +877,7 @@
         y, tg, qg, og, ug, dg, g1, g2 = finish(y, tg, *S, gg)
         return y[None], tg[None], g1[0], qg.transpose(1, 0, 2), og.T, g2[0], ug, dg.T
     S = lax.psum_scatter(S[0].astype(F32), "batch", scatter_dimension=1, tiled=True)
-    g = lax.psum_scatter(gg, "batch", scatter_dimension=1, tiled=True)
+    g = lax.psum_scatter(lax.psum(gg, "head"), "batch", scatter_dimension=1, tiled=True)
     cat = lambda a: a.transpose(1, 0, 2).reshape(R, -1)
     qg = S[0:3].reshape(3, R, 3, 128).transpose(1, 2, 0, 3).reshape(R, 3, 384)
     return y[None], tg[None], g[0], qg, S[3].T, g[1], cat(S[4:8]), cat(S[12:16]).T

time: 185 us -> 173 us (0.935)
  Pallas kernels: 184 us -> 172 us
    pallas_call x1, Pallas kernels: 179 us -> 168 us  [layer(): pl.pallas_call(functools.partial(layer_body, nb, custom, tuple(shapes)),...]
where the time goes in v5:
time: 173 us
  Pallas kernels  172 us (99%)
    pallas_call x1, Pallas kernels, layer(): pl.pallas_call(functools.partial(layer_body, nb, custom, tuple(shapes)),...  168 us
    pallas_call x1, Pallas kernels, finish(): pl.pallas_call(finish_body, out_shape=[jax.ShapeDtypeStruct(a.shape, a.dt...  4.44 us

profile of v5, /device:TPU:0, one launch (start us, length us, event | category | flops | bytes accessed | tf_op | source)
XLA Modules:
  0.0 173.0 jit_solution(13312961489951114338)
XLA Ops:
  0.6 167.7 %shard_map.170 = (bf16[512,768]{1,0:T(8,128)(2,1)}, f32[512,768]{1,0:T(8,128)}, f32[1,48,128]{2,1,0:T(8,128)}, f32[3,48,384]{2,1,0:T(8,128)}, f32[48,384]{1,0:T(...) custom-call(bf16[1024,768]{1,0:T(8,128)(2,1)} %bitcast.18, bf16[1024,768]{1,0:T(8,128)(2,1)} %bitcast.19, ...), custom_call_target="tpu_custom_call" | custom-call | tf_op jit(solution)/shard_map/pallas_call | solution.py:856
  168.4 4.4 %shard_map.171 = (bf16[512,768]{1,0:T(8,128)(2,1)}, f32[512,768]{1,0:T(8,128)}, f32[3,48,384]{2,1,0:T(8,128)}, f32[48,384]{1,0:T(8,128)}, f32[48,1536]{1,0:T(8,1...) custom-call(bf16[512,768]{1,0:T(8,128)(2,1)} %get-tuple-element.23.refs_0_, ...), custom_call_target="tpu_custom_call" | custom-call | tf_op jit(solution)/shard_map/pallas_call | solution.py:486

commit v6 on v5

--- a/solution.py
+++ b/solution.py
@@ -226,7 +226,7 @@
 
 
 EPS = 1e-5
-RT = 256
+RT = 512
 
 
 def pick(static, cond, body):
@@ -455,7 +455,7 @@
     def wide(ref, q):
         ref[:, pl.ds(pl.multiple_of(q * 384, 128), 384)] = tot[...]
 
-    pick(None, p < 3, lambda: pair(p))
+    pick(None, (8 <= p < 12) if isinstance(p, int) else (p >= 8) & (p < 12), lambda: pair(p - 8))
     pick(None, p == 3, lambda: og.__setitem__(..., tot[...]))
     pick(None, (3 < p < 8) if isinstance(p, int) else (p > 3) & (p < 8), lambda: wide(ug, p - 4))
     pick(None, p >= 12, lambda: wide(dg, p - 12))
@@ -499,8 +499,8 @@
     return {
         "gr": f(8, 768), "n1": b(L, 768), "qkv": b(3, L, 384), "att": b(L, 384), "ex": b(L, 384), "mb": b(6, L, 128),
         "ns": b(6, L, 128), "prob": b(6, 128, L), "hid": f(L, 768), "n2": b(L, 768), "act": b(4, L, 384), "dg": b(4, L, 384),
-        "aT": b(768, L), "ghs": f(L // 2, 768), "eb": b(L, 768), "er": b(L, 768), "fr": b(L // 2, 768), "gatt": b(L, 384),
-        "dqkv": b(L, 384), "qaug": b(L, 256), "kaug": b(L, 256), "gaug": b(L, 128), "gaug1": b(L, 128), "vaug": b(L, 128),
+        "aT": b(768, L), "eb": b(L, 768), "er": b(L, 768), "fr": b(L // 2, 768), "gatt": b(L, 384),
+        "qaug": b(L, 256), "kaug": b(L, 256), "gaug": b(L, 128), "gaug1": b(L, 128), "vaug": b(L, 128),
         "dqs": f(L, 128), "dks": f(L, 128), "dvs": f(L, 128), "dqt": f(128, L), "gacc": f(8, 768),
         "wg": b(*wide),
     }
@@ -524,7 +524,7 @@
         gg, tot, gbuf, ss, rs, gss, grs, ss2, rs2, gss2, grs2, gown, gtwin = take(13)
         land, gland = take(5), take(5)
         G, Gg = Gather(pc, wg, ss, rs), Gather(pc, gg, gss, grs)
-        S = Scatter(pc, wg, *land, ss2, rs2, slot=lambda p: p - 4 if isinstance(p, int) and p >= 12 else p if isinstance(p, int) else jnp.where(p >= 12, p - 4, p))
+        S = Scatter(pc, wg, *land, ss2, rs2, slot=lambda p: (p - 4 if p >= 12 else p - 8 if p >= 8 else p) if isinstance(p, int) else jnp.where(p >= 12, p - 4, jnp.where(p >= 8, p - 8, p)))
         Sg = Scatter(pc, gbuf, *gland, gss2, grs2)
         Gp = PlaneFirst(pc, wg, ss, rs)
         m = pc.nz - 1
@@ -546,7 +546,7 @@
         gsteps = [Gg.z0] + [functools.partial(lambda d: Gg.zk(0, d), d) for d in range(1, m)] + [None, Gg.x1, Gg.x2]
         ssteps = S.steps(lambda p: place_sum(p, tot, out_s), tot)
         tails = Sg.tight(gown)
-        starts = {13: 12, 14: 13, 15: 14, 16: 15, 17: 4, 18: 5, 19: 6, 20: 7, 21: 3, 22: 0, 23: 1, 25: 2}
+        starts = {13: 12, 14: 13, 15: 14, 16: 15, 17: 4, 18: 5, 19: 6, 20: 7, 21: 3, 22: 8, 23: 9, 25: 10}
 
         def tick(t, span=None):
             fixed = isinstance(t, int)
@@ -668,7 +668,14 @@
 
     pl.loop(0, 2)(down_grad)
     tick(13)
+    def gate(q):
+        @tiles(nt)
+        def _(i):
+            ga = dot(ct[rows_of(i), :], flat(wg, 8 + q))
+            dg[q, rows_of(i), :] = (ga * dg[q, rows_of(i), :].astype(F32)).astype(BF)
+
     pl.loop(2, 4)(down_grad)
+    pl.loop(0, 2)(gate)
     tick(14)
     transpose_into(n2)
 
@@ -685,12 +692,7 @@
 
     tick(15)
 
-    @pl.loop(0, 4)
-    def _(q):
-        @tiles(nt)
-        def _(i):
-            ga = dot(ct[rows_of(i), :], flat(wg, 8 + q))
-            dg[q, rows_of(i), :] = (ga * dg[q, rows_of(i), :].astype(F32)).astype(BF)
+    pl.loop(2, 4)(gate)
 
     @tiles(nh)
     def _(i):
@@ -738,7 +740,7 @@
 
         @pl.when((i >= pc.h * nh) & (i < pc.h * nh + nh))
         def _():
-            s["ghs"][rows_of(i - pc.h * nh), :] = gh
+            tg[rows_of(i - pc.h * nh), :] = gh
             gacc[1:2, :] += jnp.sum(gn * n, axis=0, keepdims=True)
 
     tick(18)
@@ -752,7 +754,7 @@
     tick(19)
     transpose_into(n1)
     nacc = hid
-    dqkv = s["dqkv"]
+    dqkv = att
 
     @pl.loop(0, 3)
     def _(p):
@@ -764,6 +766,9 @@
         dqkv[:, 128:256] = s["dks"][...].astype(BF)
         dqkv[:, 256:384] = s["dvs"][...].astype(BF)
 
+        put(8 + p, aT[...], dqkv[...])
+        tick(21 + 2 * p, (21, 27, 2))
+
         @tiles(nt)
         def _(i):
             v = dot(dqkv[rows_of(i), :], flat(wg, p), NT)
@@ -775,8 +780,6 @@
             @pl.when(p > 0)
             def _():
                 nacc[rows_of(i), :] += v
-        put(p, aT[...], dqkv[...])
-        tick(21 + 2 * p, (21, 27, 2))
 
     @tiles(nh)
     def _(i):
@@ -808,7 +811,7 @@
         n, inv = norm_rows(x[rows_of(pc.h * nh + i), :].astype(F32))
         a = gn * gr[0:1, :]
         back = (a - jnp.mean(a, axis=1, keepdims=True) - n * jnp.mean(a * n, axis=1, keepdims=True)) * inv
-        tg[r, :] = s["ghs"][r, :] + back
+        tg[r, :] += back
 
     if custom:
         for t in range(28, max(25 + len(ssteps), 26 + len(tails))):
@@ -819,7 +822,7 @@
 
         @pl.loop(0, 12)
         def _(i):
-            S.drain(jnp.where(i < 8, i, i + 4))
+            S.drain(jnp.where(i < 3, i + 8, jnp.where(i < 8, i, i + 4)))
         Sg.drain(0)
         cv.wait()
         out_g[0] = gown[0] + gtwin[0]
@@ -879,7 +882,7 @@
     S = lax.psum_scatter(S[0].astype(F32), "batch", scatter_dimension=1, tiled=True)
     g = lax.psum_scatter(lax.psum(gg, "head"), "batch", scatter_dimension=1, tiled=True)
     cat = lambda a: a.transpose(1, 0, 2).reshape(R, -1)
-    qg = S[0:3].reshape(3, R, 3, 128).transpose(1, 2, 0, 3).reshape(R, 3, 384)
+    qg = S[8:11].reshape(3, R, 3, 128).transpose(1, 2, 0, 3).reshape(R, 3, 384)
     return y[None], tg[None], g[0], qg, S[3].T, g[1], cat(S[4:8]), cat(S[12:16]).T
 
 

time: 173 us -> 167 us (0.965)
  Pallas kernels: 172 us -> 166 us
    pallas_call x1, Pallas kernels: 168 us -> 161 us  [layer(): pl.pallas_call(functools.partial(layer_body, nb, custom, tuple(shapes)),...]
where the time goes in v6:
time: 167 us
  Pallas kernels  166 us (99%)
    pallas_call x1, Pallas kernels, layer(): pl.pallas_call(functools.partial(layer_body, nb, custom, tuple(shapes)),...  161 us
    pallas_call x1, Pallas kernels, finish(): pl.pallas_call(finish_body, out_shape=[jax.ShapeDtypeStruct(a.shape, a.dt...  4.44 us

profile of v6, /device:TPU:0, one launch (start us, length us, event | category | flops | bytes accessed | tf_op | source)
XLA Modules:
  0.0 166.6 jit_solution(5331718185559716902)
XLA Ops:
  0.6 161.3 %shard_map.170 = (bf16[512,768]{1,0:T(8,128)(2,1)}, f32[512,768]{1,0:T(8,128)}, f32[1,48,128]{2,1,0:T(8,128)}, f32[3,48,384]{2,1,0:T(8,128)}, f32[48,384]{1,0:T(...) custom-call(bf16[1024,768]{1,0:T(8,128)(2,1)} %bitcast.18, bf16[1024,768]{1,0:T(8,128)(2,1)} %bitcast.19, ...), custom_call_target="tpu_custom_call" | custom-call | tf_op jit(solution)/shard_map/pallas_call | solution.py:859
  162.0 4.4 %shard_map.171 = (bf16[512,768]{1,0:T(8,128)(2,1)}, f32[512,768]{1,0:T(8,128)}, f32[3,48,384]{2,1,0:T(8,128)}, f32[48,384]{1,0:T(8,128)}, f32[48,1536]{1,0:T(8,1...) custom-call(bf16[512,768]{1,0:T(8,128)(2,1)} %get-tuple-element.23.refs_0_, ...), custom_call_target="tpu_custom_call" | custom-call | tf_op jit(solution)/shard_map/pallas_call | solution.py:486

commit v7 on v6

--- a/solution.py
+++ b/solution.py
@@ -463,8 +463,9 @@
 
 def finish_body(*refs):
     ins, gg, outs, (g1, g2), bufs, (si, so) = refs[:6], refs[6], refs[7:13], refs[13:15], refs[15:21], refs[21:]
-    ci = [pltpu.make_async_copy(a, b, si.at[i]) for i, (a, b) in enumerate(zip(ins, bufs))]
-    co = [pltpu.make_async_copy(a, b, so.at[i]) for i, (a, b) in enumerate(zip(bufs, outs))]
+    cuts = [(i, j * (a.shape[0] // n), a.shape[0] // n) for i, (a, n) in enumerate(zip(ins, (2, 4, 3, 1, 1, 1))) for j in range(n)]
+    ci = [pltpu.make_async_copy(ins[i].at[pl.ds(o, n)], bufs[i].at[pl.ds(o, n)], si.at[k]) for k, (i, o, n) in enumerate(cuts)]
+    co = [pltpu.make_async_copy(bufs[i].at[pl.ds(o, n)], outs[i].at[pl.ds(o, n)], so.at[k]) for k, (i, o, n) in enumerate(cuts)]
     for c in ci:
         c.start()
     R = gg.shape[1]
@@ -487,7 +488,7 @@
         finish_body,
         out_shape=[jax.ShapeDtypeStruct(a.shape, a.dtype) for a in arrays[:6]] + [jax.ShapeDtypeStruct((1, R), F32)] * 2,
         in_specs=[A] * 6 + [V], out_specs=[A] * 6 + [V] * 2,
-        scratch_shapes=[pltpu.VMEM(a.shape, a.dtype) for a in arrays[:6]] + [dma((6,)), dma((6,))],
+        scratch_shapes=[pltpu.VMEM(a.shape, a.dtype) for a in arrays[:6]] + [dma((12,)), dma((12,))],
         compiler_params=pltpu.CompilerParams(vmem_limit_bytes=60 << 20),
     )(*arrays)
 
@@ -542,6 +543,7 @@
         rest = list(range(1, 9))
         gather = [(m + 2, G.x2, [0], nine), (m + 1, G.x1, [0], nine), (m + 3, G.x2, rest, nine), (m + 2, G.x1, rest, nine)]
         gather += [(e, fn, list(range(9)), nine) for e, fn in [(m, last)] + line(G, 0) + [(0, G.z0)]]
+        gather += [(9, G.drain, list(range(9)), nine), (8, Gp.drain, [0, 4, 8], three)]
         gather += [(e, fn, [0, 4, 8], three) for e, fn in [(m + 3, lambda p: Gp.zk(p, m))] + line(Gp, 3) + [(2, turn), (1, Gp.x1), (0, Gp.x0)]]
         gsteps = [Gg.z0] + [functools.partial(lambda d: Gg.zk(0, d), d) for d in range(1, m)] + [None, Gg.x1, Gg.x2]
         ssteps = S.steps(lambda p: place_sum(p, tot, out_s), tot)
@@ -633,9 +635,10 @@
         def _(i):
             qkv[p, rows_of(i), :] = dot(n1[rows_of(i), :], flat(wg, p)).astype(BF)
         rr = fwd_clusters(p, qkv, cl, s["ns"], seg, s["prob"])
-        for h in range(2):
-            tick(6 + 2 * p + h, (6 + h, 12, 2))
-            fwd_head(p, h, rr[h], qkv, s["mb"], s["ns"], s["qaug"], s["kaug"], att, ex)
+        fwd_head(p, 0, rr[0], qkv, s["mb"], s["ns"], s["qaug"], s["kaug"], att, ex)
+        pl.when(p == 0)(lambda: tick(6))
+        fwd_head(p, 1, rr[1], qkv, s["mb"], s["ns"], s["qaug"], s["kaug"], att, ex)
+        tick(7 + p, (7, 10))
 
     def send(k, src, dst, i):
         return twin_copy(pc, src.at[rows_of(i)], dst.at[rows_of(i)], es.at[k + i], ers.at[k + i])
@@ -645,7 +648,7 @@
         eb[rows_of(i), :] = dot(att[rows_of(i), :], flat(wg, 3), NT).astype(BF)
         send(0, eb, er, i).start()
 
-    tick(12)
+    tick(10)
 
     @tiles(nt)
     def _(i):
@@ -666,8 +669,9 @@
         up(q)
         put(12 + q, aT[...], act[q])
 
+    tick(11)
     pl.loop(0, 2)(down_grad)
-    tick(13)
+    tick(12)
     def gate(q):
         @tiles(nt)
         def _(i):
@@ -675,6 +679,7 @@
             dg[q, rows_of(i), :] = (ga * dg[q, rows_of(i), :].astype(F32)).astype(BF)
 
     pl.loop(2, 4)(down_grad)
+    tick(13)
     pl.loop(0, 2)(gate)
     tick(14)
     transpose_into(n2)
@@ -701,16 +706,6 @@
         y[rows_of(i), :] = (hid[rows_of(pc.h * nh + i), :] + (acc + fr[rows_of(i), :].astype(F32))).astype(BF)
 
     tick(16)
-    if custom:
-        @pl.loop(0, 9)
-        def _(k):
-            G.drain(nine(k))
-
-        @pl.loop(0, 3)
-        def _(k):
-            Gp.drain(4 * k + 3)
-        Gg.drain(0)
-
     @tiles(nt)
     def _(i):
         acc = dot(dg[0, rows_of(i), :], flat(wg, 4), NT)
@@ -814,16 +809,21 @@
         tg[r, :] += back
 
     if custom:
+        @pl.loop(0, 9)
+        def _(i):
+            S.drain(jnp.where(i < 5, i + 3, i + 7))
+
         for t in range(28, max(25 + len(ssteps), 26 + len(tails))):
             late(t)
             if t == 25 + len(tails):
                 cv = twin_copy(pc, gown, gtwin, vs, vrs)
                 cv.start()
 
-        @pl.loop(0, 12)
-        def _(i):
-            S.drain(jnp.where(i < 3, i + 8, jnp.where(i < 8, i, i + 4)))
+        @pl.loop(8, 11)
+        def _(p):
+            S.drain(p)
         Sg.drain(0)
+        Gg.drain(0)
         cv.wait()
         out_g[0] = gown[0] + gtwin[0]
     else:

time: 167 us -> 163 us (0.976)
  Pallas kernels: 166 us -> 162 us
    pallas_call x1, Pallas kernels: 161 us -> 158 us  [layer(): pl.pallas_call(functools.partial(layer_body, nb, custom, tuple(shapes)),...]
where the time goes in v7:
time: 163 us
  Pallas kernels  162 us (99%)
    pallas_call x1, Pallas kernels, layer(): pl.pallas_call(functools.partial(layer_body, nb, custom, tuple(shapes)),...  158 us
    pallas_call x1, Pallas kernels, finish(): pl.pallas_call(finish_body, out_shape=[jax.ShapeDtypeStruct(a.shape, a.dt...  4.14 us

profile of v7, /device:TPU:0, one launch (start us, length us, event | category | flops | bytes accessed | tf_op | source)
XLA Modules:
  0.0 162.9 jit_solution(3076716260778483595)
XLA Ops:
  0.6 157.9 %shard_map.170 = (bf16[512,768]{1,0:T(8,128)(2,1)}, f32[512,768]{1,0:T(8,128)}, f32[1,48,128]{2,1,0:T(8,128)}, f32[3,48,384]{2,1,0:T(8,128)}, f32[48,384]{1,0:T(...) custom-call(bf16[1024,768]{1,0:T(8,128)(2,1)} %bitcast.18, bf16[1024,768]{1,0:T(8,128)(2,1)} %bitcast.19, ...), custom_call_target="tpu_custom_call" | custom-call | tf_op jit(solution)/shard_map/pallas_call | solution.py:859
  158.6 4.1 %shard_map.171 = (bf16[512,768]{1,0:T(8,128)(2,1)}, f32[512,768]{1,0:T(8,128)}, f32[3,48,384]{2,1,0:T(8,128)}, f32[48,384]{1,0:T(8,128)}, f32[48,1536]{1,0:T(8,1...) custom-call(bf16[512,768]{1,0:T(8,128)(2,1)} %get-tuple-element.23.refs_0_, ...), custom_call_target="tpu_custom_call" | custom-call | tf_op jit(solution)/shard_map/pallas_call | solution.py:487

commit v8 on v7

--- a/solution.py
+++ b/solution.py
@@ -58,7 +58,7 @@
         self.rd=3-self.r
         self.X=(self.z*4+self.rx,self.h); self.Y=(self.z*4+self.ry,self.h)
         self.up=(self.b+4,self.h); self.dn=(self.b-4,self.h); self.twin=(self.b,1-self.h)
-    def barrier(self):
+    def greet(self):
         bar=pltpu.get_barrier_semaphore()
         for d in (self.X,self.Y,self.twin):
             pl.semaphore_signal(bar,inc=1,device_id=d,device_id_type=MESH)
@@ -66,6 +66,8 @@
         def _(): pl.semaphore_signal(bar,inc=1,device_id=self.up,device_id_type=MESH)
         @pl.when(self.z>0)
         def _(): pl.semaphore_signal(bar,inc=1,device_id=self.dn,device_id_type=MESH)
+    def meet(self):
+        bar=pltpu.get_barrier_semaphore()
         lines=jnp.where(self.z<self.nz-1,1,0)+jnp.where(self.z>0,1,0)
         pl.semaphore_wait(bar,3+lines)
 
@@ -584,10 +586,11 @@
     else:
         tick = lambda t, span=None: None
 
+    pc.greet()
     tpad[...] = jnp.full_like(tpad, -1)
-    pc.barrier()
     if custom:
         fill_own(pc, wg, gg, *own)
+    pc.meet()
     tick(0)
 
     @tiles(nt)

time: 163 us -> 163 us (level)
  no operation moved by 1% of the time
where the time goes in v8:
time: 163 us
  Pallas kernels  162 us (99%)
    pallas_call x1, Pallas kernels, layer(): pl.pallas_call(functools.partial(layer_body, nb, custom, tuple(shapes)),...  158 us
    pallas_call x1, Pallas kernels, finish(): pl.pallas_call(finish_body, out_shape=[jax.ShapeDtypeStruct(a.shape, a.dt...  4.14 us

profile of v8, /device:TPU:0, one launch (start us, length us, event | category | flops | bytes accessed | tf_op | source)
XLA Modules:
  0.0 162.7 jit_solution(16886326721490200607)
XLA Ops:
  0.6 157.7 %shard_map.170 = (bf16[512,768]{1,0:T(8,128)(2,1)}, f32[512,768]{1,0:T(8,128)}, f32[1,48,128]{2,1,0:T(8,128)}, f32[3,48,384]{2,1,0:T(8,128)}, f32[48,384]{1,0:T(...) custom-call(bf16[1024,768]{1,0:T(8,128)(2,1)} %bitcast.18, bf16[1024,768]{1,0:T(8,128)(2,1)} %bitcast.19, ...), custom_call_target="tpu_custom_call" | custom-call | tf_op jit(solution)/shard_map/pallas_call | solution.py:862
  158.4 4.1 %shard_map.171 = (bf16[512,768]{1,0:T(8,128)(2,1)}, f32[512,768]{1,0:T(8,128)}, f32[3,48,384]{2,1,0:T(8,128)}, f32[48,384]{1,0:T(8,128)}, f32[48,1536]{1,0:T(8,1...) custom-call(bf16[512,768]{1,0:T(8,128)(2,1)} %get-tuple-element.23.refs_0_, ...), custom_call_target="tpu_custom_call" | custom-call | tf_op jit(solution)/shard_map/pallas_call | solution.py:489
